TPU v7x, 512 devices: a whole 4x4x16 slice. The times are simulated.
512 devices in a mesh: row: 16 (over y, x), col: 32 (over z, core).
Axes of the slice: x: 4, y: 4, z: 16, core: 2. Of those that a mesh axis runs over, the one named last changes fastest.
Arguments:
- matrix: float32 [8192, 8192], P('row', 'col'), may hold values from -6 to 6
- row_struct: int32 [2, 32], P(None, 'row'), may hold values from 0 to 1
- col_struct: int32 [2, 32], P(None, 'col'), may hold values from 0 to 1
- panel_index: int32 [2], replicated, may hold values from 0 to 30, as said below
- lower_inv: float32 [2, 512, 512], replicated, as said below
- upper_inv: float32 [2, 512, 512], replicated, as said below
Outputs:
- factored: float32 [8192, 8192], P('row', 'col')
Inputs may be any that keep to these rules, and one draw needn't show every extreme that they name: `panel_index`: even block indices; the two steps' panels are disjoint; one of them is the last block pair. `lower_inv`: unit lower triangular. `upper_inv`: upper triangular with positive diagonal.
All inputs are finite; a program needn't handle non-finite values.
Results may differ from a plain program's by a relative error of at most 0.0001.
Values sent between devices are 32-bit elements; how exact they have to be, the bound alone decides.
No kernel may reach another device: no remote copies, remote signals or barrier semaphores. Data moves between devices by JAX's collectives and lax.ppermute only.
A program may use at most 64 MiB of HBM per device.

v0:
```python
import jax
import jax.numpy as jnp
from jax import lax
from jax.sharding import PartitionSpec as P

PREC = lax.Precision.HIGH


def dot(a, b):
    return jnp.dot(a, b, precision=PREC, preferred_element_type=jnp.float32)


def local(matrix, row_struct, col_struct, panel_index, lower_inv, upper_inv):
    n_row = lax.axis_size("row")
    n_col = lax.axis_size("col")
    n_z = n_col // 2
    my_row = lax.axis_index("row")
    my_col = lax.axis_index("col")
    my_z, core = my_col // 2, my_col % 2
    width = upper_inv.shape[1]
    size = width // 2
    def send_z(value, hops):
        pairs = [(2 * (a % n_z) + c, 2 * (b % n_z) + c) for a, b in hops for c in range(2)]
        return lax.ppermute(value, "col", pairs)

    def from_class(value, place, spacing, hop):
        return send_z(value, [(z, z + hop) for z in range(place % spacing, n_z, spacing)])

    def exchange(value):
        return lax.all_to_all(value, "row", 0, 0, tiled=True)

    def first_stage(place):
        def run(block, own):
            far = [from_class(block, place, 8, 8)]
            far += [from_class(block, place, 4, hop) for hop in (4, -4)]
            return far[0], far[1], far[2], exchange(own)

        return run

    def second_stage(place):
        def run(middle, chunk):
            up = from_class(middle, place, 4, 1)
            down = from_class(middle, place, 4, -1)
            top = from_class(middle[:size], place, 4, 2)
            bottom = from_class(middle[size:], place, 4, -2)
            return up, down, top, bottom, exchange(jnp.tile(chunk, (n_row, 1)))

        return run

    first_stages = [first_stage(place) for place in range(8)]
    second_stages = [second_stage(place) for place in range(4)]

    def fetch(block, first):
        plane = first // 2
        dist = (my_z - plane) % n_z
        root, slot = first % n_row, first // n_row
        own = lax.dynamic_slice_in_dim(block, slot * size, size, 0)
        across, ahead, behind, scattered = lax.switch(plane % 8, first_stages, block, own)
        middle = jnp.where(
            dist == 8,
            across,
            jnp.where(dist == 4, ahead, jnp.where(dist == n_z - 4, behind, block)),
        )
        piece = size // n_row
        chunk = lax.dynamic_slice_in_dim(scattered, root * piece, 2 * piece, 0)
        up, down, top, bottom, gathered = lax.switch(plane % 4, second_stages, middle, chunk)
        near = dist % 4
        columns = jnp.where(
            near == 0,
            middle,
            jnp.where(
                near == 1, up, jnp.where(near == 3, down, jnp.concatenate([top, bottom], axis=0))
            ),
        )
        rows = gathered.reshape(n_row, 2, piece, size).transpose(1, 0, 2, 3).reshape(width, size)
        return columns, rows

    block = matrix
    for step in range(panel_index.shape[0]):
        first = panel_index[step]
        plane = first // 2
        mine, rows = fetch(block, first)
        other = lax.ppermute(mine, "col", [(i, i ^ 1) for i in range(n_col)])
        upper = dot(lower_inv[step], rows)
        u_mine = lax.dynamic_slice_in_dim(upper_inv[step], core * size, size, 0)
        u_other = lax.dynamic_slice_in_dim(upper_inv[step], (1 - core) * size, size, 0)
        lower = dot(mine, u_mine) + dot(other, u_other)
        row_hit = jnp.repeat(row_struct[step] > 0, size)[:, None]
        col_hit = col_struct[step, 0] > 0
        schur = dot(
            jnp.where(row_hit, lower, jnp.float32(0.0)),
            jnp.where(col_hit, upper, jnp.float32(0.0)),
        )
        block = block - schur
        lower_mine = lax.dynamic_slice_in_dim(lower, core * size, size, 1)
        block = jnp.where((my_z == plane) & row_hit, lower_mine, block)
        for member in range(2):
            root, slot = (first + member) % n_row, (first + member) // n_row
            take = jnp.repeat(jnp.arange(2) == slot, size)[:, None] & (my_row == root) & col_hit
            part = upper[member * size : (member + 1) * size]
            block = jnp.where(take, jnp.concatenate([part, part], axis=0), block)
    return block


def solution(mesh):
    return jax.shard_map(
        local,
        mesh=mesh,
        in_specs=(P("row", "col"), P(None, "row"), P(None, "col"), P(), P(), P()),
        out_specs=P("row", "col"),
        check_vma=False,
    )
```

profile of v0, /device:TPU:99, one launch (start us, length us, event | category | flops | bytes accessed | tf_op | source)
XLA Modules:
  0.0 170.3 jit_solution(2736686139880297385)
XLA Ops:
  4.9 28.4 %conditional.4 = (f32[512,256]{1,0:T(8,128)}, f32[512,256]{1,0:T(8,128)}, f32[512,256]{1,0:T(8,128)}, f32[256,256]{1,0:T(8,128)S(1)}) conditional(s32[]{:T(128)} %clamp.15, (f32[512,256]{1,0:T(8,128)}, f32[256,256]{1,0:T(8,128)S(1)}) %tuple.111, (f32[512,256]{1,0:T(8,128)}, f32[256,256]{1,0:T(8,128)S(1)}) %tuple.111, ...), branch_computations={%region_0.1_spmd, %region_1.2_spmd, %region_2.3_spmd, %region_3.4_... | conditional | bytes 6815896 | solution.py:58
  5.0 9.8 %collective-permute-start.23 = (f32[512,256]{1,0:T(8,128)}, f32[512,256]{1,0:T(8,128)}, u32[]{:S(2)}, u32[]{:S(2)}) collective-permute-start(f32[512,256]{1,0:T(8,128)} %get-tuple-element.125), channel_id=1, source_target_pairs={{6,30},{7,31},{14,6},{15,7},{22,14},{23,15},{30,22},{31,23},{38,62... | collective-permute-start | bytes 1572872 | tf_op jit(solution)/shard_map/cond/branch_7_fun/ppermute | solution.py:24
  14.7 1.9 %collective-permute-start.22 = (f32[512,256]{1,0:T(8,128)}, f32[512,256]{1,0:T(8,128)}, u32[]{:S(2)}, u32[]{:S(2)}) collective-permute-start(f32[512,256]{1,0:T(8,128)} %get-tuple-element.125), channel_id=1, source_target_pairs={{6,14},{7,15},{14,22},{15,23},{22,30},{23,31},{30,6},{31,7},{38,46... | collective-permute-start | bytes 1572872 | tf_op jit(solution)/shard_map/cond/branch_7_fun/ppermute | solution.py:24
  18.2 13.6 %all_to_all.191 = f32[16,16,256]{2,1,0:T(8,128)S(1)} all-to-all(f32[16,16,256]{2,1,0:T(8,128)S(1)} %bitcast.83), channel_id=1, replica_groups=mesh['row'=16,'col'=32] {'row'}, dimensions={0} | all-to-all | bytes 524288 | tf_op jit(solution)/shard_map/cond/branch_7_fun/all_to_all | solution.py:30
  34.7 22.8 %conditional.5 = (f32[512,256]{1,0:T(8,128)}, f32[512,256]{1,0:T(8,128)}, f32[256,256]{1,0:T(8,128)}, f32[256,256]{1,0:T(8,128)}, f32[16,32,256]{2,1,0:T(8,128)}) conditional(s32[]{:T(128)} %clamp.14, (f32[512,256]{1,0:T(8,128)S(1)}, f32[32,256]{1,0:T(8,128)S(1)}) %tuple.112, (f32[512,256]{1,0:T(8,128)S(1)}, ...), branch_computations={%region_8.9_spmd, %region_9.10_spmd, %region_10.11_spmd, %region_1... | conditional | bytes 9470184 | solution.py:66
  34.7 2.1 %collective-permute-start.61 = (f32[512,256]{1,0:T(8,128)S(1)}, f32[512,256]{1,0:T(8,128)}, u32[]{:S(2)}, u32[]{:S(2)}) collective-permute-start(f32[512,256]{1,0:T(8,128)S(1)} %get-tuple-element.133), channel_id=1, source_target_pairs={{6,4},{7,5},{14,12},{15,13},{22,20},{23,21},{30,28},{31,29},{38,36... | collective-permute-start | bytes 1572872 | tf_op jit(solution)/shard_map/cond/branch_3_fun/ppermute | solution.py:24
  36.8 2.1 %collective-permute-start.60 = (f32[512,256]{1,0:T(8,128)S(1)}, f32[512,256]{1,0:T(8,128)}, u32[]{:S(2)}, u32[]{:S(2)}) collective-permute-start(f32[512,256]{1,0:T(8,128)S(1)} %get-tuple-element.133), channel_id=1, source_target_pairs={{6,8},{7,9},{14,16},{15,17},{22,24},{23,25},{30,0},{31,1},{38,40},... | collective-permute-start | bytes 1572872 | tf_op jit(solution)/shard_map/cond/branch_3_fun/ppermute | solution.py:24
  39.8 6.9 %all-to-all-start.19 = ((f32[16,32,256]{2,1,0:T(8,128)}), f32[16,32,256]{2,1,0:T(8,128)}, u32[]{:S(2)}, u32[]{:S(2)}) async-start(f32[16,32,256]{2,1,0:T(8,128)} %tile.21), calls=%async_computation.19 | async-start | bytes 1048576 | tf_op jit(solution)/shard_map/cond/branch_3_fun/all_to_all | solution.py:30
  46.7 2.0 %collective-permute-start.63 = (f32[256,256]{1,0:T(8,128)S(1)}, f32[256,256]{1,0:T(8,128)}, u32[]{:S(2)}, u32[]{:S(2)}) collective-permute-start(f32[256,256]{1,0:T(8,128)S(1)} %get-tuple-element.400), channel_id=1, source_target_pairs={{6,2},{7,3},{14,10},{15,11},{22,18},{23,19},{30,26},{31,27},{38,34... | collective-permute-start | bytes 786440 | tf_op jit(solution)/shard_map/cond/branch_3_fun/ppermute | solution.py:24
  48.7 2.0 %collective-permute-start.62 = (f32[256,256]{1,0:T(8,128)S(1)}, f32[256,256]{1,0:T(8,128)}, u32[]{:S(2)}, u32[]{:S(2)}) collective-permute-start(f32[256,256]{1,0:T(8,128)S(1)} %get-tuple-element.401), channel_id=1, source_target_pairs={{6,10},{7,11},{14,18},{15,19},{22,26},{23,27},{30,2},{31,3},{38,42... | collective-permute-start | bytes 786440 | tf_op jit(solution)/shard_map/cond/branch_3_fun/ppermute | solution.py:24
  50.7 6.7 %collective-permute-done.63 = f32[256,256]{1,0:T(8,128)} collective-permute-done((f32[256,256]{1,0:T(8,128)S(1)}, f32[256,256]{1,0:T(8,128)}, u32[]{:S(2)}, u32[]{:S(2)}) %collective-permute-start.63) | collective-permute-done | bytes 262176 | tf_op jit(solution)/shard_map/cond/branch_3_fun/ppermute | solution.py:24
  57.5 2.0 %fusion.7 = f32[512,256]{1,0:T(8,128)} fusion(f32[512,256]{1,0:T(8,128)S(1)} %select_select_fusion.1, f32[512,256]{1,0:T(8,128)} %get-tuple-element.182, f32[512,256]{1,0:T(8,128)} %get-tuple-element.183, f32[256,256]{1,0:T(8,128)} %get-tuple-element.185, f32[256,256]{1,0:T(8,128)} %get-tuple-element.184, pred[]{:T(512)S(6)} %eq.110, pred[]{:T(512)S(6)} %eq.109, ...), kind=kLoop, calls=%fused_computation.28 | loop fusion | flops 524288 | bytes 2621443 | tf_op jit(solution)/shard_map/jit(_where)/select_n | solution.py:68
  59.5 2.7 %collective-permute-start.80 = (f32[512,256]{1,0:T(8,128)}, f32[512,256]{1,0:T(8,128)}, u32[]{:S(2)}, u32[]{:S(2)}) collective-permute-start(f32[512,256]{1,0:T(8,128)} %fusion.7), channel_id=1, source_target_pairs={{0,1},{1,0},{2,3},{3,2},{4,5},{5,4},{6,7},{7,6},{8,9},{9,8},{10,11... | collective-permute-start | bytes 1572872 | tf_op jit(solution)/shard_map/ppermute | solution.py:83
  67.9 1.9 %copy.77 = f32[2,16,16,256]{3,2,1,0:T(8,128)} copy(f32[2,16,16,256]{3,2,0,1:T(8,128)} %bitcast.37) | data formatting | bytes 1048576 | tf_op jit(solution)/shard_map/transpose | solution.py:75
  69.7 1.7 %fusion.52 = (f32[1,512,512]{2,1,0:T(8,128)S(1)}, f32[1,512,512]{2,1,0:T(8,128)S(1)}) fusion(f32[2,512,512]{2,1,0:T(8,128)} %param.35), kind=kLoop, calls=%fused_computation.80 | loop fusion | bytes 4194304 | tf_op jit(solution)/shard_map/slice | solution.py:85
  71.5 2.5 %convolution_bitcast_fusion.1 = f32[512,256]{0,1:T(8,128)S(1)} fusion(f32[512,256]{1,0:T(8,128)} %bitcast.84, f32[2,512,512]{2,1,0:T(8,128)} %param.34), kind=kOutput, calls=%fused_computation.17 | convolution fusion | flops 402653184 | bytes 2097152 | tf_op jit(solution)/shard_map/dot_general | solution.py:10
  77.2 1.7 %convolution_add_fusion.1 = f32[512,512]{0,1:T(8,128)S(1)} fusion(f32[512,512]{0,1:T(8,128)S(1)} %fusion.14, f32[512,256]{1,0:T(8,128)} %collective-permute-done.80, f32[1,512,512]{2,1,0:T(8,128)S(1)} %get-tuple-element.411, s32[]{:T(128)S(6)} %select_n.254), kind=kOutput, calls=%fused_computation.13 | convolution fusion | flops 402915328 | bytes 3145732 | tf_op jit(solution)/shard_map/dot_general | solution.py:10
  79.7 19.0 %conditional.6 = (f32[256,256]{1,0:T(8,128)}, f32[512,256]{0,1:T(8,128)S(1)}, f32[512,256]{0,1:T(8,128)S(1)}, f32[512,256]{0,1:T(8,128)S(1)}) conditional(s32[]{:T(128)} %clamp.13, (f32[512,256]{0,1:T(8,128)S(1)}, f32[512,256]{0,1:T(8,128)S(1)}, s32[]{:T(128)}, s32[]{:T(128)}, s32[]{:T(128)}, /*index=5*/s32[]{:T(128)}, ...), branch_computations={%region_12.13_spmd, %region_13.14_spmd, %region_14.15_spmd, %regio... | conditional | flops 3 | bytes 12320990 | solution.py:58
  84.8 6.6 %all-to-all-start.13 = ((f32[16,16,256]{2,1,0:T(8,128)}), f32[16,16,256]{2,1,0:T(8,128)}, u32[]{:S(2)}, u32[]{:S(2)}) async-start(f32[16,16,256]{2,1,0:T(8,128)} %bitcast.26), calls=%async_computation.13 | async-start | bytes 524288 | tf_op jit(solution)/shard_map/cond/branch_5_fun/all_to_all | solution.py:30
  94.1 4.5 %all-to-all-done.13 = f32[16,16,256]{2,1,0:T(8,128)} async-done(((f32[16,16,256]{2,1,0:T(8,128)}), f32[16,16,256]{2,1,0:T(8,128)}, u32[]{:S(2)}, u32[]{:S(2)}) %all-to-all-start.13) | async-done | bytes 262176 | tf_op jit(solution)/shard_map/cond/branch_5_fun/all_to_all | solution.py:30
  99.7 59.7 %conditional.7 = (f32[16,32,256]{2,1,0:T(8,128)}, f32[512,256]{0,1:T(8,128)S(1)}, f32[512,256]{0,1:T(8,128)S(1)}, f32[256,256]{0,1:T(8,128)}, f32[256,256]{0,1:T(8,128)S(1)}) conditional(s32[]{:T(128)} %clamp.12, (f32[512,256]{0,1:T(8,128)S(1)}, f32[256,256]{1,0:T(8,128)}, s32[]{:T(128)}, s32[]{:T(128)}, s32[]{:T(128)}, ...), branch_computations={%region_20.21_spmd, %region_21.22_spmd, %region_22.23_spmd, %regio... | conditional | flops 3 | bytes 13730062 | solution.py:66
  104.5 5.4 %all-to-all-start.21 = ((f32[16,32,256]{2,1,0:T(8,128)}), f32[16,32,256]{2,1,0:T(8,128)}, u32[]{:S(2)}, u32[]{:S(2)}) async-start(f32[16,32,256]{2,1,0:T(8,128)} %tile.23), calls=%async_computation.21 | async-start | bytes 1048576 | tf_op jit(solution)/shard_map/cond/branch_1_fun/all_to_all | solution.py:30
  113.2 42.6 %collective-permute-done.71 = f32[256,256]{1,0:T(8,128)S(1)} collective-permute-done((f32[256,256]{1,0:T(8,128)S(1)}, f32[256,256]{1,0:T(8,128)S(1)}, u32[]{:S(2)}, u32[]{:S(2)}) %collective-permute-start.71) | collective-permute-done | bytes 262176 | tf_op jit(solution)/shard_map/cond/branch_1_fun/ppermute | solution.py:24
  162.4 3.8 %collective-permute-start.81 = (f32[512,256]{0,1:T(8,128)S(1)}, f32[512,256]{0,1:T(8,128)S(1)}, u32[]{:S(2)}, u32[]{:S(2)}) collective-permute-start(f32[512,256]{0,1:T(8,128)S(1)} %fusion.9), channel_id=1, source_target_pairs={{0,1},{1,0},{2,3},{3,2},{4,5},{5,4},{6,7},{7,6},{8,9},{9,8},{10,11... | collective-permute-start | bytes 1572872 | tf_op jit(solution)/shard_map/ppermute | solution.py:83
  (89 shorter events, 39.3 us)
Async XLA Ops:
  5.0 26.8 %collective-permute-start.23 = (f32[512,256]{1,0:T(8,128)}, f32[512,256]{1,0:T(8,128)}, u32[]{:S(2)}, u32[]{:S(2)}) collective-permute-start(f32[512,256]{1,0:T(8,128)} %get-tuple-element.125), channel_id=1, source_target_pairs={{6,30},{7,31},{14,6},{15,7},{22,14},{23,15},{30,22},{31,23},{38,62... | collective-permute-start | bytes 1572872 | tf_op jit(solution)/shard_map/cond/branch_7_fun/ppermute | solution.py:24
  14.7 18.6 %collective-permute-start.22 = (f32[512,256]{1,0:T(8,128)}, f32[512,256]{1,0:T(8,128)}, u32[]{:S(2)}, u32[]{:S(2)}) collective-permute-start(f32[512,256]{1,0:T(8,128)} %get-tuple-element.125), channel_id=1, source_target_pairs={{6,14},{7,15},{14,22},{15,23},{22,30},{23,31},{30,6},{31,7},{38,46... | collective-permute-start | bytes 1572872 | tf_op jit(solution)/shard_map/cond/branch_7_fun/ppermute | solution.py:24
  16.7 16.7 %collective-permute-start.21 = (f32[512,256]{1,0:T(8,128)}, f32[512,256]{1,0:T(8,128)}, u32[]{:S(2)}, u32[]{:S(2)}) collective-permute-start(f32[512,256]{1,0:T(8,128)} %get-tuple-element.125), channel_id=1, source_target_pairs={{14,30},{15,31},{30,14},{31,15},{46,62},{47,63},{62,46},{63,47},{7... | collective-permute-start | bytes 1572872 | tf_op jit(solution)/shard_map/cond/branch_7_fun/ppermute | solution.py:24
  34.7 22.7 %collective-permute-start.61 = (f32[512,256]{1,0:T(8,128)S(1)}, f32[512,256]{1,0:T(8,128)}, u32[]{:S(2)}, u32[]{:S(2)}) collective-permute-start(f32[512,256]{1,0:T(8,128)S(1)} %get-tuple-element.133), channel_id=1, source_target_pairs={{6,4},{7,5},{14,12},{15,13},{22,20},{23,21},{30,28},{31,29},{38,36... | collective-permute-start | bytes 1572872 | tf_op jit(solution)/shard_map/cond/branch_3_fun/ppermute | solution.py:24
  36.8 20.6 %collective-permute-start.60 = (f32[512,256]{1,0:T(8,128)S(1)}, f32[512,256]{1,0:T(8,128)}, u32[]{:S(2)}, u32[]{:S(2)}) collective-permute-start(f32[512,256]{1,0:T(8,128)S(1)} %get-tuple-element.133), channel_id=1, source_target_pairs={{6,8},{7,9},{14,16},{15,17},{22,24},{23,25},{30,0},{31,1},{38,40},... | collective-permute-start | bytes 1572872 | tf_op jit(solution)/shard_map/cond/branch_3_fun/ppermute | solution.py:24
  39.8 17.7 %all-to-all-start.19 = ((f32[16,32,256]{2,1,0:T(8,128)}), f32[16,32,256]{2,1,0:T(8,128)}, u32[]{:S(2)}, u32[]{:S(2)}) async-start(f32[16,32,256]{2,1,0:T(8,128)} %tile.21), calls=%async_computation.19 | async-start | bytes 1048576 | tf_op jit(solution)/shard_map/cond/branch_3_fun/all_to_all | solution.py:30
  46.7 10.7 %collective-permute-start.63 = (f32[256,256]{1,0:T(8,128)S(1)}, f32[256,256]{1,0:T(8,128)}, u32[]{:S(2)}, u32[]{:S(2)}) collective-permute-start(f32[256,256]{1,0:T(8,128)S(1)} %get-tuple-element.400), channel_id=1, source_target_pairs={{6,2},{7,3},{14,10},{15,11},{22,18},{23,19},{30,26},{31,27},{38,34... | collective-permute-start | bytes 786440 | tf_op jit(solution)/shard_map/cond/branch_3_fun/ppermute | solution.py:24
  48.7 8.7 %collective-permute-start.62 = (f32[256,256]{1,0:T(8,128)S(1)}, f32[256,256]{1,0:T(8,128)}, u32[]{:S(2)}, u32[]{:S(2)}) collective-permute-start(f32[256,256]{1,0:T(8,128)S(1)} %get-tuple-element.401), channel_id=1, source_target_pairs={{6,10},{7,11},{14,18},{15,19},{22,26},{23,27},{30,2},{31,3},{38,42... | collective-permute-start | bytes 786440 | tf_op jit(solution)/shard_map/cond/branch_3_fun/ppermute | solution.py:24
  57.5 8.2 %copy-start.6 = (s32[2,2]{1,0:T(2,128)S(1)}, s32[2,2]{1,0:T(2,128)}, u32[]{:S(2)}) copy-start(s32[2,2]{1,0:T(2,128)} %param.31) | copy-start | bytes 52
  57.5 8.4 %copy-start.5 = (s32[2,1]{0,1:T(1,128)S(1)}, s32[2,1]{0,1:T(1,128)}, u32[]{:S(2)}) copy-start(s32[2,1]{0,1:T(1,128)} %param.32) | copy-start | bytes 28
  59.5 17.7 %collective-permute-start.80 = (f32[512,256]{1,0:T(8,128)}, f32[512,256]{1,0:T(8,128)}, u32[]{:S(2)}, u32[]{:S(2)}) collective-permute-start(f32[512,256]{1,0:T(8,128)} %fusion.7), channel_id=1, source_target_pairs={{0,1},{1,0},{2,3},{3,2},{4,5},{5,4},{6,7},{7,6},{8,9},{9,8},{10,11... | collective-permute-start | bytes 1572872 | tf_op jit(solution)/shard_map/ppermute | solution.py:83
  71.4 2.7 %copy-start = (f32[512,256]{1,0:T(8,128)S(1)}, f32[512,256]{1,0:T(8,128)}, u32[]{:S(2)}) copy-start(f32[512,256]{1,0:T(8,128)} %param.30) | copy-start | bytes 1572868
  77.2 1.8 %copy-start.1 = (f32[512,256]{0,1:T(8,128)S(1)}, f32[512,256]{0,1:T(8,128)}, u32[]{:S(2)}) copy-start(f32[512,256]{0,1:T(8,128)} %copy.80) | copy-start | bytes 1572868
  80.1 11.3 %collective-permute-start.40 = (f32[512,256]{1,0:T(8,128)S(1)}, f32[512,256]{1,0:T(8,128)S(1)}, u32[]{:S(2)}, u32[]{:S(2)}) collective-permute-start(f32[512,256]{1,0:T(8,128)S(1)} %copy.92), channel_id=1, source_target_pairs={{2,10},{3,11},{10,18},{11,19},{18,26},{19,27},{26,2},{27,3},{34,42... | collective-permute-start | bytes 1572872 | tf_op jit(solution)/shard_map/cond/branch_5_fun/ppermute | solution.py:24
  80.8 10.8 %collective-permute-start.39 = (f32[512,256]{1,0:T(8,128)S(1)}, f32[512,256]{1,0:T(8,128)}, u32[]{:S(2)}, u32[]{:S(2)}) collective-permute-start(f32[512,256]{1,0:T(8,128)S(1)} %copy.92), channel_id=1, source_target_pairs={{10,26},{11,27},{26,10},{27,11},{42,58},{43,59},{58,42},{59,43},{7... | collective-permute-start | bytes 1572872 | tf_op jit(solution)/shard_map/cond/branch_5_fun/ppermute | solution.py:24
  82.3 10.5 %collective-permute-start.41 = (f32[512,256]{1,0:T(8,128)S(1)}, f32[512,256]{1,0:T(8,128)}, u32[]{:S(2)}, u32[]{:S(2)}) collective-permute-start(f32[512,256]{1,0:T(8,128)S(1)} %copy.92), channel_id=1, source_target_pairs={{2,26},{3,27},{10,2},{11,3},{18,10},{19,11},{26,18},{27,19},{34,58... | collective-permute-start | bytes 1572872 | tf_op jit(solution)/shard_map/cond/branch_5_fun/ppermute | solution.py:24
  84.8 13.9 %all-to-all-start.13 = ((f32[16,16,256]{2,1,0:T(8,128)}), f32[16,16,256]{2,1,0:T(8,128)}, u32[]{:S(2)}, u32[]{:S(2)}) async-start(f32[16,16,256]{2,1,0:T(8,128)} %bitcast.26), calls=%async_computation.13 | async-start | bytes 524288 | tf_op jit(solution)/shard_map/cond/branch_5_fun/all_to_all | solution.py:30
  99.9 56.9 %collective-permute-start.69 = (f32[512,256]{1,0:T(8,128)S(1)}, f32[512,256]{1,0:T(8,128)}, u32[]{:S(2)}, u32[]{:S(2)}) collective-permute-start(f32[512,256]{1,0:T(8,128)S(1)} %copy.102), channel_id=1, source_target_pairs={{2,0},{3,1},{10,8},{11,9},{18,16},{19,17},{26,24},{27,25},{34,32},... | collective-permute-start | bytes 1572872 | tf_op jit(solution)/shard_map/cond/branch_1_fun/ppermute | solution.py:24
  101.4 56.7 %collective-permute-start.68 = (f32[512,256]{1,0:T(8,128)S(1)}, f32[512,256]{1,0:T(8,128)}, u32[]{:S(2)}, u32[]{:S(2)}) collective-permute-start(f32[512,256]{1,0:T(8,128)S(1)} %copy.102), channel_id=1, source_target_pairs={{2,4},{3,5},{10,12},{11,13},{18,20},{19,21},{26,28},{27,29},{34,36... | collective-permute-start | bytes 1572872 | tf_op jit(solution)/shard_map/cond/branch_1_fun/ppermute | solution.py:24
  104.5 54.9 %all-to-all-start.21 = ((f32[16,32,256]{2,1,0:T(8,128)}), f32[16,32,256]{2,1,0:T(8,128)}, u32[]{:S(2)}, u32[]{:S(2)}) async-start(f32[16,32,256]{2,1,0:T(8,128)} %tile.23), calls=%async_computation.21 | async-start | bytes 1048576 | tf_op jit(solution)/shard_map/cond/branch_1_fun/all_to_all | solution.py:30
  110.6 45.2 %collective-permute-start.71 = (f32[256,256]{1,0:T(8,128)S(1)}, f32[256,256]{1,0:T(8,128)S(1)}, u32[]{:S(2)}, u32[]{:S(2)}) collective-permute-start(f32[256,256]{1,0:T(8,128)S(1)} %get-tuple-element.404), channel_id=1, source_target_pairs={{2,30},{3,31},{10,6},{11,7},{18,14},{19,15},{26,22},{27,23},{34,62... | collective-permute-start | bytes 786440 | tf_op jit(solution)/shard_map/cond/branch_1_fun/ppermute | solution.py:24
  111.9 44.1 %collective-permute-start.70 = (f32[256,256]{1,0:T(8,128)}, f32[256,256]{1,0:T(8,128)S(1)}, u32[]{:S(2)}, u32[]{:S(2)}) collective-permute-start(f32[256,256]{1,0:T(8,128)} %get-tuple-element.405), channel_id=1, source_target_pairs={{2,6},{3,7},{10,14},{11,15},{18,22},{19,23},{26,30},{27,31},{34,38... | collective-permute-start | bytes 786440 | tf_op jit(solution)/shard_map/cond/branch_1_fun/ppermute | solution.py:24
  159.4 6.9 %copy-start.2 = (f32[2,512,512]{2,1,0:T(8,128)S(1)}, f32[2,512,512]{2,1,0:T(8,128)}, u32[]{:S(2)}) copy-start(f32[2,512,512]{2,1,0:T(8,128)} %param.34) | copy-start | bytes 6291460
  162.4 5.6 %collective-permute-start.81 = (f32[512,256]{0,1:T(8,128)S(1)}, f32[512,256]{0,1:T(8,128)S(1)}, u32[]{:S(2)}, u32[]{:S(2)}) collective-permute-start(f32[512,256]{0,1:T(8,128)S(1)} %fusion.9), channel_id=1, source_target_pairs={{0,1},{1,0},{2,3},{3,2},{4,5},{5,4},{6,7},{7,6},{8,9},{9,8},{10,11... | collective-permute-start | bytes 1572872 | tf_op jit(solution)/shard_map/ppermute | solution.py:83
  (2 other events, 1.6 us)
where the time goes:
time: 172 us; the launch traced here: 170 us
  starting transfers between devices  56 us (33%)
  waiting for transfers between devices  55.5 us (32%)
  local copies, waits for them, and re-layouts  22.5 us (13%)
  blocking collectives  13.6 us (8%)
  matrix products  9.56 us (6%)
  between operations  7.89 us (5%)
  other arithmetic  4.76 us (3%)
    ppermute x14, waiting for transfers between devices, send_z(): return lax.ppermute(value, 'col', pairs)  51 us
    ppermute x14, starting transfers between devices, send_z(): return lax.ppermute(value, 'col', pairs)  30.5 us
    all_to_all x3, starting transfers between devices, exchange(): return lax.all_to_all(value, 'row', 0, 0, tiled=True)  19 us
    all_to_all x1, blocking collectives, exchange(): return lax.all_to_all(value, 'row', 0, 0, tiled=True)  13.6 us
    dot_general x8, matrix products, dot(): return jnp.dot(a, b, precision=PREC, preferred_element_type=jnp.float32)  9.56 us
    ppermute x2, starting transfers between devices, local(): other = lax.ppermute(mine, 'col', [(i, i ^ 1) for i in range(n_col)])  6.51 us
    all_to_all x3, waiting for transfers between devices, exchange(): return lax.all_to_all(value, 'row', 0, 0, tiled=True)  4.54 us
    cond x4, local copies, waits for them, and re-layouts, fetch(): lax.switch(plane % 4, second_stages, middle, chunk)  3.44 us
  transfers between devices with their start and end apart: 19, of which 4 were waited for; matrix products, arithmetic and copies ran while one was open for 13% of the time, Pallas kernels for 0%

commit v1 on v0

v1 whole, which is shorter than its diff:
```python
import functools

import jax
import jax.numpy as jnp
from jax import lax
from jax.experimental import pallas as pl
from jax.experimental.pallas import tpu as pltpu
from jax.sharding import PartitionSpec as P

VMEM_BYTES = 40 * 1024 * 1024


def split(value):
    high = value.astype(jnp.bfloat16)
    low = (value - high.astype(jnp.float32)).astype(jnp.bfloat16)
    return high, low


def dot(a, b):
    (a_high, a_low), (b_high, b_low) = a, b
    mul = functools.partial(jnp.dot, preferred_element_type=jnp.float32)
    return mul(a_high, b_high) + (mul(a_high, b_low) + mul(a_low, b_high))


def early_kernel(n_row, gathered_ref, mine_ref, lower_ref, upper_ref, rows_out, cols_out, rows):
    size = rows.shape[1]
    piece = size // n_row
    for r in range(n_row):
        at = 2 * piece * r
        rows[piece * r : piece * (r + 1)] = gathered_ref[at : at + piece]
        rows[size + piece * r : size + piece * (r + 1)] = gathered_ref[
            at + piece : at + 2 * piece
        ]
    half = pl.ds(pl.multiple_of(lax.axis_index("col") % 2 * size, size), size)
    rows_out[...] = dot(split(lower_ref[0]), split(rows[...]))
    cols_out[...] = dot(split(mine_ref[...]), split(upper_ref[0, half]))


def late_kernel(
    n_row,
    step,
    row_struct,
    col_struct,
    panel,
    other_ref,
    part_ref,
    rows_ref,
    upper_ref,
    block_ref,
    out_ref,
    cols,
):
    size = rows_ref.shape[1]
    my_row, my_col = lax.axis_index("row"), lax.axis_index("col")
    core = my_col % 2
    first = panel[step]
    half = pl.ds(pl.multiple_of((1 - core) * size, size), size)
    cols[...] = part_ref[...] + dot(split(other_ref[...]), split(upper_ref[0, half]))
    col_hit = col_struct[step, 0] > 0
    rows = rows_ref[...]
    kept = split(jnp.where(col_hit, rows, jnp.float32(0.0)))
    owner = my_col // 2 == first // 2
    for slot in range(2):
        at = slice(slot * size, (slot + 1) * size)
        row_hit = row_struct[step, slot] > 0
        whole = cols[at]
        masked = jnp.where(row_hit, whole, jnp.float32(0.0))
        new = block_ref[at] - dot(split(masked), kept)
        own = jnp.where(core == 0, whole[:, :size], whole[:, size:])
        new = jnp.where(owner & row_hit, own, new)
        for member in range(2):
            here = (my_row == (first + member) % n_row) & (slot == first // n_row) & col_hit
            new = jnp.where(here, rows[member * size : (member + 1) * size], new)
        out_ref[at] = new


def local(matrix, row_struct, col_struct, panel_index, lower_inv, upper_inv):
    n_row = lax.axis_size("row")
    n_col = lax.axis_size("col")
    n_z = n_col // 2
    my_col = lax.axis_index("col")
    my_z = my_col // 2
    width = upper_inv.shape[1]
    size = width // 2
    piece = size // n_row

    def send_z(value, hops):
        pairs = [(2 * (a % n_z) + c, 2 * (b % n_z) + c) for a, b in hops for c in range(2)]
        return lax.ppermute(value, "col", pairs)

    def from_class(value, place, spacing, hop):
        return send_z(value, [(z, z + hop) for z in range(place % spacing, n_z, spacing)])

    def exchange(value):
        return lax.all_to_all(value, "row", 0, 0, tiled=True)

    def first_stage(place):
        def run(block, first):
            dist = (my_z - first // 2) % n_z
            across = from_class(block, place, 8, 8)
            ahead = from_class(block, place, 4, 4)
            behind = from_class(block, place, 4, -4)
            own = lax.dynamic_slice_in_dim(block, first // n_row * size, size, 0)
            scattered = exchange(own)
            chunk = lax.dynamic_slice_in_dim(scattered, first % n_row * piece, 2 * piece, 0)
            middle = jnp.where(
                dist == 8,
                across,
                jnp.where(dist == 4, ahead, jnp.where(dist == n_z - 4, behind, block)),
            )
            return middle, chunk

        return run

    def second_stage(place):
        def run(middle, chunk, first):
            near = (my_z - first // 2) % 4
            up = from_class(middle, place, 4, 1)
            down = from_class(middle, place, 4, -1)
            halves = lax.optimization_barrier((middle[:size], middle[size:], chunk))
            top = from_class(halves[0], place, 4, 2)
            bottom = from_class(halves[1], place, 4, -2)
            gathered = exchange(jnp.tile(halves[2], (n_row, 1)))
            both = jnp.concatenate([top, bottom], axis=0)
            columns = jnp.where(
                near == 0, middle, jnp.where(near == 1, up, jnp.where(near == 3, down, both))
            )
            return columns, gathered

        return run

    first_stages = [first_stage(place) for place in range(8)]
    second_stages = [second_stage(place) for place in range(4)]
    whole = pl.BlockSpec(memory_space=pltpu.VMEM)
    scalars = pl.BlockSpec(memory_space=pltpu.SMEM)
    params = pltpu.CompilerParams(vmem_limit_bytes=VMEM_BYTES)
    f32 = jnp.float32

    block = matrix
    for step in range(panel_index.shape[0]):
        first = panel_index[step]
        plane = first // 2
        matrix_of = pl.BlockSpec((1, width, width), lambda i, step=step: (step, 0, 0))
        middle, chunk = lax.switch(plane % 8, first_stages, block, first)
        mine, gathered = lax.switch(plane % 4, second_stages, middle, chunk, first)
        other = lax.ppermute(mine, "col", [(i, i ^ 1) for i in range(n_col)])
        rows, part = pl.pallas_call(
            functools.partial(early_kernel, n_row),
            grid=(1,),
            out_shape=(
                jax.ShapeDtypeStruct((width, size), f32),
                jax.ShapeDtypeStruct((2 * size, width), f32),
            ),
            in_specs=[whole, whole, matrix_of, matrix_of],
            out_specs=(whole, whole),
            scratch_shapes=[pltpu.VMEM((width, size), f32)],
            compiler_params=params,
            cost_estimate=pl.CostEstimate(
                flops=6 * width * width * width, bytes_accessed=12 * width * width, transcendentals=0
            ),
            name="early",
        )(gathered, mine, lower_inv, upper_inv)
        block = pl.pallas_call(
            functools.partial(late_kernel, n_row, step),
            grid=(1,),
            out_shape=jax.ShapeDtypeStruct(matrix.shape, f32),
            in_specs=[scalars, scalars, scalars, whole, whole, whole, matrix_of, whole],
            out_specs=whole,
            scratch_shapes=[pltpu.VMEM((2 * size, width), f32)],
            compiler_params=params,
            cost_estimate=pl.CostEstimate(
                flops=6 * width * width * width, bytes_accessed=12 * width * width, transcendentals=0
            ),
            name="late",
        )(row_struct, col_struct, panel_index, other, part, rows, upper_inv, block)
    return block


def solution(mesh):
    return jax.shard_map(
        local,
        mesh=mesh,
        in_specs=(P("row", "col"), P(None, "row"), P(None, "col"), P(), P(), P()),
        out_specs=P("row", "col"),
        check_vma=False,
    )
```

time: 172 us -> 152 us (0.88)
  the two profiles are of different devices: /device:TPU:99 before, /device:TPU:33 now
where the time goes in v1:
time: 152 us; the launch traced here: 150 us
  waiting for transfers between devices  60.4 us (40%)
  starting transfers between devices  46.7 us (31%)
  local copies, waits for them, and re-layouts  12.6 us (8%)
  loops' own time  11.6 us (8%)
  Pallas kernels  8.67 us (6%)
  between operations  5.77 us (4%)
  other arithmetic  4.46 us (3%)
    ppermute x14, waiting for transfers between devices, send_z(): return lax.ppermute(value, 'col', pairs)  44.5 us
    all_to_all x4, starting transfers between devices, exchange(): return lax.all_to_all(value, 'row', 0, 0, tiled=True)  22 us
    ppermute x14, starting transfers between devices, send_z(): return lax.ppermute(value, 'col', pairs)  16.1 us
    all_to_all x4, waiting for transfers between devices, exchange(): return lax.all_to_all(value, 'row', 0, 0, tiled=True)  15.9 us
    ppermute x2, starting transfers between devices, local(): other = lax.ppermute(mine, 'col', [(i, i ^ 1) for i in range(n_col)])  8.65 us
    another operation x2, loops' own time, local(): middle, chunk = lax.switch(plane % 8, first_stages, block, first)  5.88 us
    another operation x2, loops' own time, local(): mine, gathered = lax.switch(plane % 4, second_stages, middle, chunk, first)  5.75 us
    pallas_call x2, Pallas kernels, local(): pl.pallas_call(functools.partial(early_kernel, n_row), grid=(1,), out_sha...  4.42 us
  transfers between devices with their start and end apart: 20, of which 6 were waited for; matrix products, arithmetic and copies ran while one was open for 6% of the time, Pallas kernels for 3%

profile of v1, /device:TPU:33, one launch (start us, length us, event | category | flops | bytes accessed | tf_op | source)
XLA Modules:
  0.0 150.3 jit_solution(17912043658220859796)
XLA Ops:
  4.2 22.1 %conditional.4 = (f32[512,256]{1,0:T(8,128)S(1)}, f32[32,256]{1,0:T(8,128)S(1)}) conditional(s32[]{:T(128)} %clamp.15, (s32[]{:T(128)}, s32[]{:T(128)}, f32[512,256]{1,0:T(8,128)}) %tuple.109, (s32[]{:T(128)}, s32[]{:T(128)}, f32[512,256]{1,0:T(8,128)}) %tuple.109, (s32[]{:T(128)}, s32[]{:T(128)}, ...), branch_computations={%region_0.1_spmd, %region_1.2_spmd, %region_2.3_spmd, %region_3.4_... | conditional | flops 393268 | bytes 10289861 | solution.py:144
  9.1 1.7 %constant_dynamic-slice_fusion.7 = f32[256,256]{1,0:T(8,128)} fusion(f32[512,256]{1,0:T(8,128)} %get-tuple-element.176, s32[]{:T(128)S(6)} %select_n.621), kind=kLoop, calls=%fused_computation.11 | loop fusion | bytes 524292 | tf_op jit(solution)/shard_map/cond/branch_3_fun/dynamic_slice | solution.py:103
  10.8 6.8 %all-to-all-start.3 = ((f32[16,16,256]{2,1,0:T(8,128)}), f32[16,16,256]{2,1,0:T(8,128)S(1)}, u32[]{:S(2)}, u32[]{:S(2)}) async-start(f32[16,16,256]{2,1,0:T(8,128)} %bitcast.6), calls=%async_computation.3 | async-start | bytes 524288 | tf_op jit(solution)/shard_map/cond/branch_3_fun/all_to_all | solution.py:95
  17.6 7.5 %all-to-all-done.3 = f32[16,16,256]{2,1,0:T(8,128)S(1)} async-done(((f32[16,16,256]{2,1,0:T(8,128)}), f32[16,16,256]{2,1,0:T(8,128)S(1)}, u32[]{:S(2)}, u32[]{:S(2)}) %all-to-all-start.3) | async-done | bytes 262176 | tf_op jit(solution)/shard_map/cond/branch_3_fun/all_to_all | solution.py:95
  26.4 45.3 %conditional.5 = (f32[512,256]{1,0:T(8,128)S(1)}, f32[512,256]{1,0:T(8,128)}) conditional(s32[]{:T(128)} %clamp.14, (s32[]{:T(128)}, s32[]{:T(128)}, f32[512,256]{1,0:T(8,128)S(1)}, f32[32,256]{1,0:T(8,128)S(1)}) %tuple.110, (s32[]{:T(128)}, s32[]{:T(128)}, f32[512,256]{1,0:T(8,128)S(1)}, ...), branch_computations={%region_8.9_spmd, %region_9.10_spmd, %region_10.11_spmd, %region_1... | conditional | flops 524318 | bytes 14189081 | solution.py:145
  32.9 4.2 %all-to-all-start.19 = ((f32[16,32,256]{2,1,0:T(8,128)}), f32[16,32,256]{2,1,0:T(8,128)}, u32[]{:S(2)}, u32[]{:S(2)}) async-start(f32[16,32,256]{2,1,0:T(8,128)} %tile.21), calls=%async_computation.19 | async-start | bytes 1048576 | tf_op jit(solution)/shard_map/cond/branch_3_fun/all_to_all | solution.py:95
  39.9 19.4 %collective-permute-done.62 = f32[256,256]{1,0:T(8,128)} collective-permute-done((f32[256,256]{1,0:T(8,128)}, f32[256,256]{1,0:T(8,128)}, u32[]{:S(2)}, u32[]{:S(2)}) %collective-permute-start.62) | collective-permute-done | bytes 262176 | tf_op jit(solution)/shard_map/cond/branch_3_fun/ppermute | solution.py:89
  59.4 10.3 %collective-permute-done.63 = f32[256,256]{1,0:T(8,128)} collective-permute-done((f32[256,256]{1,0:T(8,128)S(1)}, f32[256,256]{1,0:T(8,128)}, u32[]{:S(2)}, u32[]{:S(2)}) %collective-permute-start.63) | collective-permute-done | bytes 262176 | tf_op jit(solution)/shard_map/cond/branch_3_fun/ppermute | solution.py:89
  72.5 4.7 %collective-permute-start.80 = (f32[512,256]{1,0:T(8,128)}, f32[512,256]{1,0:T(8,128)S(1)}, u32[]{:S(2)}, u32[]{:S(2)}) collective-permute-start(f32[512,256]{1,0:T(8,128)} %copy-done.6), channel_id=1, source_target_pairs={{0,1},{1,0},{2,3},{3,2},{4,5},{5,4},{6,7},{7,6},{8,9},{9,8},{10,11... | collective-permute-start | bytes 1572872 | tf_op jit(solution)/shard_map/ppermute | solution.py:146
  80.1 1.6 %copy-done.1 = f32[2,512,512]{2,1,0:T(8,128)S(1)} copy-done((f32[2,512,512]{2,1,0:T(8,128)S(1)}, f32[2,512,512]{2,1,0:T(8,128)}, u32[]{:S(2)}) %copy-start.1) | copy-done | bytes 2097176
  81.7 2.2 %early.2 = (f32[512,256]{1,0:T(8,128)S(1)}, f32[512,512]{1,0:T(8,128)S(1)}) custom-call(f32[512,256]{1,0:T(8,128)} %get-tuple-element.284.gathered_ref, f32[512,256]{1,0:T(8,128)} %copy-done.6, f32[2,512,512]{2,1,0:T(8,128)S(1)} %copy-done.1, f32[2,512,512]{2,1,0:T(8,128)S(1)} %copy-done), custom_call_target="tpu_custom_call" | custom-call | flops 805306368 | bytes 3145728 | tf_op jit(solution)/shard_map/early/pallas_call | solution.py:147
  84.0 1.7 %late.2.block_ref = f32[512,256]{1,0:T(8,128)S(1)} custom-call(s32[2,2]{1,0:T(2,128)S(1)} %copy-done.4, s32[2,1]{1,0:T(2,128)S(1)} %copy.8.col_struct, s32[2]{0:T(128)S(1)} %copy-done.3, f32[512,256]{1,0:T(8,128)S(1)} %collective-permute-done.80.other_ref, f32[512,512]{1,0:T(8,128)S(1)} %get-tuple-element.285.part_ref, ...), custom_call_target="tpu_custom_call" | custom-call | flops 805306368 | bytes 3145728 | tf_op jit(solution)/shard_map/late/pallas_call | solution.py:163
  85.7 23.4 %conditional.6 = (f32[512,256]{1,0:T(8,128)S(1)}, f32[32,256]{1,0:T(8,128)S(1)}) conditional(s32[]{:T(128)} %clamp.13, (s32[]{:T(128)}, s32[]{:T(128)}, f32[512,256]{1,0:T(8,128)S(1)}) %tuple.111, (s32[]{:T(128)}, s32[]{:T(128)}, f32[512,256]{1,0:T(8,128)S(1)}) %tuple.111, (s32[]{:T(128)}, s32[]{:T(128)}, ...), branch_computations={%region_12.13_spmd, %region_13.14_spmd, %region_14.15_spmd, %regio... | conditional | flops 393268 | bytes 12387041 | solution.py:144
  92.9 6.8 %all-to-all-start.15 = ((f32[16,16,256]{2,1,0:T(8,128)}), f32[16,16,256]{2,1,0:T(8,128)S(1)}, u32[]{:S(2)}, u32[]{:S(2)}) async-start(f32[16,16,256]{2,1,0:T(8,128)} %bitcast.34), calls=%async_computation.15 | async-start | bytes 524288 | tf_op jit(solution)/shard_map/cond/branch_7_fun/all_to_all | solution.py:95
  99.7 8.5 %all-to-all-done.15 = f32[16,16,256]{2,1,0:T(8,128)S(1)} async-done(((f32[16,16,256]{2,1,0:T(8,128)}), f32[16,16,256]{2,1,0:T(8,128)S(1)}, u32[]{:S(2)}, u32[]{:S(2)}) %all-to-all-start.15) | async-done | bytes 262176 | tf_op jit(solution)/shard_map/cond/branch_7_fun/all_to_all | solution.py:95
  109.1 30.9 %conditional.7 = (f32[512,256]{1,0:T(8,128)}, f32[512,256]{1,0:T(8,128)}) conditional(s32[]{:T(128)} %clamp.12, (s32[]{:T(128)}, s32[]{:T(128)}, f32[512,256]{1,0:T(8,128)S(1)}, f32[32,256]{1,0:T(8,128)S(1)}) %tuple.112, (s32[]{:T(128)}, s32[]{:T(128)}, f32[512,256]{1,0:T(8,128)S(1)}, ...), branch_computations={%region_20.21_spmd, %region_21.22_spmd, %region_22.23_spmd, %regio... | conditional | flops 524318 | bytes 12091901 | solution.py:145
  116.3 4.2 %all-to-all-start.23 = ((f32[16,32,256]{2,1,0:T(8,128)}), f32[16,32,256]{2,1,0:T(8,128)}, u32[]{:S(2)}, u32[]{:S(2)}) async-start(f32[16,32,256]{2,1,0:T(8,128)} %tile.30), calls=%async_computation.23 | async-start | bytes 1048576 | tf_op jit(solution)/shard_map/cond/branch_3_fun/all_to_all | solution.py:95
  123.3 11.0 %collective-permute-done.78 = f32[256,256]{1,0:T(8,128)} collective-permute-done((f32[256,256]{1,0:T(8,128)}, f32[256,256]{1,0:T(8,128)}, u32[]{:S(2)}, u32[]{:S(2)}) %collective-permute-start.78) | collective-permute-done | bytes 262176 | tf_op jit(solution)/shard_map/cond/branch_3_fun/ppermute | solution.py:89
  134.3 3.7 %collective-permute-done.79 = f32[256,256]{1,0:T(8,128)} collective-permute-done((f32[256,256]{1,0:T(8,128)S(1)}, f32[256,256]{1,0:T(8,128)}, u32[]{:S(2)}, u32[]{:S(2)}) %collective-permute-start.79) | collective-permute-done | bytes 262176 | tf_op jit(solution)/shard_map/cond/branch_3_fun/ppermute | solution.py:89
  138.0 2.0 %fusion.15 = f32[512,256]{1,0:T(8,128)} fusion(f32[512,256]{1,0:T(8,128)S(1)} %get-tuple-element.264, f32[512,256]{1,0:T(8,128)} %collective-permute-done.76, f32[512,256]{1,0:T(8,128)} %collective-permute-done.77, f32[256,256]{1,0:T(8,128)} %collective-permute-done.79, f32[256,256]{1,0:T(8,128)} %collective-permute-done.78, pred[]{:T(512)S(6)} %eq.260, ...), kind=kLoop, calls=%fused_computation.71 | loop fusion | flops 524288 | bytes 2621443 | tf_op jit(solution)/shard_map/cond/branch_3_fun/jit(_where)/select_n | solution.py:125
  140.0 4.0 %collective-permute-start.81 = (f32[512,256]{1,0:T(8,128)}, f32[512,256]{1,0:T(8,128)S(1)}, u32[]{:S(2)}, u32[]{:S(2)}) collective-permute-start(f32[512,256]{1,0:T(8,128)} %get-tuple-element.289.mine_ref), channel_id=1, source_target_pairs={{0,1},{1,0},{2,3},{3,2},{4,5},{5,4},{6,7},{7,6},{8,9},{9,8},{10,11... | collective-permute-start | bytes 1572872 | tf_op jit(solution)/shard_map/ppermute | solution.py:146
  144.0 1.6 %copy-done.2 = f32[2,512,512]{2,1,0:T(8,128)S(1)} copy-done((f32[2,512,512]{2,1,0:T(8,128)S(1)}, f32[2,512,512]{2,1,0:T(8,128)}, u32[]{:S(2)}) %copy-start.2) | copy-done | bytes 2097176
  145.6 2.2 %early.3 = (f32[512,256]{1,0:T(8,128)S(1)}, f32[512,512]{1,0:T(8,128)S(1)}) custom-call(f32[512,256]{1,0:T(8,128)} %get-tuple-element.290.gathered_ref, f32[512,256]{1,0:T(8,128)} %get-tuple-element.289.mine_ref, f32[2,512,512]{2,1,0:T(8,128)S(1)} %copy-done.2, f32[2,512,512]{2,1,0:T(8,128)S(1)} %copy-done), custom_call_target="tpu_custom_call" | custom-call | flops 805306368 | bytes 3145728 | tf_op jit(solution)/shard_map/early/pallas_call | solution.py:147
  147.8 2.5 %late.3 = f32[512,256]{1,0:T(8,128)} custom-call(s32[2,2]{1,0:T(2,128)S(1)} %copy-done.4, s32[2,1]{1,0:T(2,128)S(1)} %copy.8.col_struct, s32[2]{0:T(128)S(1)} %copy-done.3, f32[512,256]{1,0:T(8,128)S(1)} %collective-permute-done.81.other_ref, f32[512,512]{1,0:T(8,128)S(1)} %get-tuple-element.291.part_ref, f32[512,256]{1,0:T(8,128)S(1)} %get-tuple-element.292.rows_ref, ...), custom_call_target="tpu_custom_call" | custom-call | flops 805306368 | bytes 3145728 | tf_op jit(solution)/shard_map/late/pallas_call | solution.py:163
  (58 shorter events, 26.4 us)
Async XLA Ops:
  4.3 20.9 %collective-permute-start.10 = (f32[512,256]{1,0:T(8,128)}, f32[512,256]{1,0:T(8,128)S(1)}, u32[]{:S(2)}, u32[]{:S(2)}) collective-permute-start(f32[512,256]{1,0:T(8,128)} %get-tuple-element.176), channel_id=1, source_target_pairs={{6,14},{7,15},{14,22},{15,23},{22,30},{23,31},{30,6},{31,7},{38,46... | collective-permute-start | bytes 1572872 | tf_op jit(solution)/shard_map/cond/branch_3_fun/ppermute | solution.py:89
  5.0 20.2 %collective-permute-start.11 = (f32[512,256]{1,0:T(8,128)}, f32[512,256]{1,0:T(8,128)S(1)}, u32[]{:S(2)}, u32[]{:S(2)}) collective-permute-start(f32[512,256]{1,0:T(8,128)} %get-tuple-element.176), channel_id=1, source_target_pairs={{6,30},{7,31},{14,6},{15,7},{22,14},{23,15},{30,22},{31,23},{38,62... | collective-permute-start | bytes 1572872 | tf_op jit(solution)/shard_map/cond/branch_3_fun/ppermute | solution.py:89
  5.7 19.5 %collective-permute-start.9 = (f32[512,256]{1,0:T(8,128)}, f32[512,256]{1,0:T(8,128)S(1)}, u32[]{:S(2)}, u32[]{:S(2)}) collective-permute-start(f32[512,256]{1,0:T(8,128)} %get-tuple-element.176), channel_id=1, source_target_pairs={{6,22},{7,23},{22,6},{23,7},{38,54},{39,55},{54,38},{55,39},{70,86... | collective-permute-start | bytes 1572872 | tf_op jit(solution)/shard_map/cond/branch_3_fun/ppermute | solution.py:89
  10.8 14.3 %all-to-all-start.3 = ((f32[16,16,256]{2,1,0:T(8,128)}), f32[16,16,256]{2,1,0:T(8,128)S(1)}, u32[]{:S(2)}, u32[]{:S(2)}) async-start(f32[16,16,256]{2,1,0:T(8,128)} %bitcast.6), calls=%async_computation.3 | async-start | bytes 524288 | tf_op jit(solution)/shard_map/cond/branch_3_fun/all_to_all | solution.py:95
  26.3 53.6 %copy-start.19 = (s32[2,1]{0,1:T(1,128)S(1)}, s32[2,1]{0,1:T(1,128)}, u32[]{:S(2)}) copy-start(s32[2,1]{0,1:T(1,128)} %param.32) | copy-start | bytes 28
  26.4 53.7 %copy-start = (f32[2,512,512]{2,1,0:T(8,128)S(1)}, f32[2,512,512]{2,1,0:T(8,128)}, u32[]{:S(2)}) copy-start(f32[2,512,512]{2,1,0:T(8,128)} %upper_ref.7) | copy-start | bytes 6291460
  26.4 43.3 %collective-permute-start.60 = (f32[512,256]{1,0:T(8,128)S(1)}, f32[512,256]{1,0:T(8,128)S(1)}, u32[]{:S(2)}, u32[]{:S(2)}) collective-permute-start(f32[512,256]{1,0:T(8,128)S(1)} %get-tuple-element.212), channel_id=1, source_target_pairs={{6,8},{7,9},{14,16},{15,17},{22,24},{23,25},{30,0},{31,1},{38,40},... | collective-permute-start | bytes 1572872 | tf_op jit(solution)/shard_map/cond/branch_3_fun/ppermute | solution.py:89
  27.2 43.3 %collective-permute-start.61 = (f32[512,256]{1,0:T(8,128)S(1)}, f32[512,256]{1,0:T(8,128)}, u32[]{:S(2)}, u32[]{:S(2)}) collective-permute-start(f32[512,256]{1,0:T(8,128)S(1)} %get-tuple-element.212), channel_id=1, source_target_pairs={{6,4},{7,5},{14,12},{15,13},{22,20},{23,21},{30,28},{31,29},{38,36... | collective-permute-start | bytes 1572872 | tf_op jit(solution)/shard_map/cond/branch_3_fun/ppermute | solution.py:89
  29.4 29.9 %collective-permute-start.62 = (f32[256,256]{1,0:T(8,128)}, f32[256,256]{1,0:T(8,128)}, u32[]{:S(2)}, u32[]{:S(2)}) collective-permute-start(f32[256,256]{1,0:T(8,128)} %get-tuple-element.214), channel_id=1, source_target_pairs={{6,10},{7,11},{14,18},{15,19},{22,26},{23,27},{30,2},{31,3},{38,42... | collective-permute-start | bytes 786440 | tf_op jit(solution)/shard_map/cond/branch_3_fun/ppermute | solution.py:89
  30.7 39.0 %collective-permute-start.63 = (f32[256,256]{1,0:T(8,128)S(1)}, f32[256,256]{1,0:T(8,128)}, u32[]{:S(2)}, u32[]{:S(2)}) collective-permute-start(f32[256,256]{1,0:T(8,128)S(1)} %get-tuple-element.215), channel_id=1, source_target_pairs={{6,2},{7,3},{14,10},{15,11},{22,18},{23,19},{30,26},{31,27},{38,34... | collective-permute-start | bytes 786440 | tf_op jit(solution)/shard_map/cond/branch_3_fun/ppermute | solution.py:89
  32.9 38.8 %all-to-all-start.19 = ((f32[16,32,256]{2,1,0:T(8,128)}), f32[16,32,256]{2,1,0:T(8,128)}, u32[]{:S(2)}, u32[]{:S(2)}) async-start(f32[16,32,256]{2,1,0:T(8,128)} %tile.21), calls=%async_computation.19 | async-start | bytes 1048576 | tf_op jit(solution)/shard_map/cond/branch_3_fun/all_to_all | solution.py:95
  72.5 11.5 %collective-permute-start.80 = (f32[512,256]{1,0:T(8,128)}, f32[512,256]{1,0:T(8,128)S(1)}, u32[]{:S(2)}, u32[]{:S(2)}) collective-permute-start(f32[512,256]{1,0:T(8,128)} %copy-done.6), channel_id=1, source_target_pairs={{0,1},{1,0},{2,3},{3,2},{4,5},{5,4},{6,7},{7,6},{8,9},{9,8},{10,11... | collective-permute-start | bytes 1572872 | tf_op jit(solution)/shard_map/ppermute | solution.py:146
  81.7 2.3 %copy-start.4 = (s32[2,2]{1,0:T(2,128)S(1)}, s32[2,2]{1,0:T(2,128)}, u32[]{:S(2)}) copy-start(s32[2,2]{1,0:T(2,128)} %row_struct.3) | copy-start | bytes 52
  81.7 2.3 %copy-start.5 = (f32[512,256]{1,0:T(8,128)S(1)}, f32[512,256]{1,0:T(8,128)}, u32[]{:S(2)}) copy-start(f32[512,256]{1,0:T(8,128)} %block_ref.1) | copy-start | bytes 1572868
  85.7 22.5 %collective-permute-start.45 = (f32[512,256]{1,0:T(8,128)S(1)}, f32[512,256]{1,0:T(8,128)S(1)}, u32[]{:S(2)}, u32[]{:S(2)}) collective-permute-start(f32[512,256]{1,0:T(8,128)S(1)} %get-tuple-element.240), channel_id=1, source_target_pairs={{14,30},{15,31},{30,14},{31,15},{46,62},{47,63},{62,46},{63,47},{7... | collective-permute-start | bytes 1572872 | tf_op jit(solution)/shard_map/cond/branch_7_fun/ppermute | solution.py:89
  86.4 21.8 %collective-permute-start.46 = (f32[512,256]{1,0:T(8,128)S(1)}, f32[512,256]{1,0:T(8,128)}, u32[]{:S(2)}, u32[]{:S(2)}) collective-permute-start(f32[512,256]{1,0:T(8,128)S(1)} %get-tuple-element.240), channel_id=1, source_target_pairs={{6,14},{7,15},{14,22},{15,23},{22,30},{23,31},{30,6},{31,7},{38,46... | collective-permute-start | bytes 1572872 | tf_op jit(solution)/shard_map/cond/branch_7_fun/ppermute | solution.py:89
  87.9 21.1 %collective-permute-start.47 = (f32[512,256]{1,0:T(8,128)S(1)}, f32[512,256]{1,0:T(8,128)}, u32[]{:S(2)}, u32[]{:S(2)}) collective-permute-start(f32[512,256]{1,0:T(8,128)S(1)} %get-tuple-element.240), channel_id=1, source_target_pairs={{6,30},{7,31},{14,6},{15,7},{22,14},{23,15},{30,22},{31,23},{38,62... | collective-permute-start | bytes 1572872 | tf_op jit(solution)/shard_map/cond/branch_7_fun/ppermute | solution.py:89
  92.9 15.3 %all-to-all-start.15 = ((f32[16,16,256]{2,1,0:T(8,128)}), f32[16,16,256]{2,1,0:T(8,128)S(1)}, u32[]{:S(2)}, u32[]{:S(2)}) async-start(f32[16,16,256]{2,1,0:T(8,128)} %bitcast.34), calls=%async_computation.15 | async-start | bytes 524288 | tf_op jit(solution)/shard_map/cond/branch_7_fun/all_to_all | solution.py:95
  109.2 28.9 %collective-permute-start.76 = (f32[512,256]{1,0:T(8,128)S(1)}, f32[512,256]{1,0:T(8,128)}, u32[]{:S(2)}, u32[]{:S(2)}) collective-permute-start(f32[512,256]{1,0:T(8,128)S(1)} %get-tuple-element.264), channel_id=1, source_target_pairs={{6,8},{7,9},{14,16},{15,17},{22,24},{23,25},{30,0},{31,1},{38,40},... | collective-permute-start | bytes 1572872 | tf_op jit(solution)/shard_map/cond/branch_3_fun/ppermute | solution.py:89
  110.6 27.4 %collective-permute-start.77 = (f32[512,256]{1,0:T(8,128)S(1)}, f32[512,256]{1,0:T(8,128)}, u32[]{:S(2)}, u32[]{:S(2)}) collective-permute-start(f32[512,256]{1,0:T(8,128)S(1)} %get-tuple-element.264), channel_id=1, source_target_pairs={{6,4},{7,5},{14,12},{15,13},{22,20},{23,21},{30,28},{31,29},{38,36... | collective-permute-start | bytes 1572872 | tf_op jit(solution)/shard_map/cond/branch_3_fun/ppermute | solution.py:89
  112.8 21.5 %collective-permute-start.78 = (f32[256,256]{1,0:T(8,128)}, f32[256,256]{1,0:T(8,128)}, u32[]{:S(2)}, u32[]{:S(2)}) collective-permute-start(f32[256,256]{1,0:T(8,128)} %get-tuple-element.266), channel_id=1, source_target_pairs={{6,10},{7,11},{14,18},{15,19},{22,26},{23,27},{30,2},{31,3},{38,42... | collective-permute-start | bytes 786440 | tf_op jit(solution)/shard_map/cond/branch_3_fun/ppermute | solution.py:89
  114.1 23.9 %collective-permute-start.79 = (f32[256,256]{1,0:T(8,128)S(1)}, f32[256,256]{1,0:T(8,128)}, u32[]{:S(2)}, u32[]{:S(2)}) collective-permute-start(f32[256,256]{1,0:T(8,128)S(1)} %get-tuple-element.267), channel_id=1, source_target_pairs={{6,2},{7,3},{14,10},{15,11},{22,18},{23,19},{30,26},{31,27},{38,34... | collective-permute-start | bytes 786440 | tf_op jit(solution)/shard_map/cond/branch_3_fun/ppermute | solution.py:89
  116.3 23.7 %all-to-all-start.23 = ((f32[16,32,256]{2,1,0:T(8,128)}), f32[16,32,256]{2,1,0:T(8,128)}, u32[]{:S(2)}, u32[]{:S(2)}) async-start(f32[16,32,256]{2,1,0:T(8,128)} %tile.30), calls=%async_computation.23 | async-start | bytes 1048576 | tf_op jit(solution)/shard_map/cond/branch_3_fun/all_to_all | solution.py:95
  140.0 7.8 %collective-permute-start.81 = (f32[512,256]{1,0:T(8,128)}, f32[512,256]{1,0:T(8,128)S(1)}, u32[]{:S(2)}, u32[]{:S(2)}) collective-permute-start(f32[512,256]{1,0:T(8,128)} %get-tuple-element.289.mine_ref), channel_id=1, source_target_pairs={{0,1},{1,0},{2,3},{3,2},{4,5},{5,4},{6,7},{7,6},{8,9},{9,8},{10,11... | collective-permute-start | bytes 1572872 | tf_op jit(solution)/shard_map/ppermute | solution.py:146
  (6 other events, 7.8 us)

commit v2 on v1

v2 whole, which is shorter than its diff:
```python
import functools

import jax
import jax.numpy as jnp
from jax import lax
from jax.experimental import pallas as pl
from jax.experimental.pallas import tpu as pltpu
from jax.sharding import PartitionSpec as P

VMEM_BYTES = 40 * 1024 * 1024


def split(value):
    high = value.astype(jnp.bfloat16)
    low = (value - high.astype(jnp.float32)).astype(jnp.bfloat16)
    return high, low


def dot(a, b):
    (a_high, a_low), (b_high, b_low) = a, b
    mul = functools.partial(jnp.dot, preferred_element_type=jnp.float32)
    return mul(a_high, b_high) + (mul(a_high, b_low) + mul(a_low, b_high))


def early_kernel(
    n_row,
    step,
    gathered_ref,
    mine_ref,
    lower_ref,
    upper_ref,
    rows_out,
    cols_out,
    upper_out,
    rows,
    lower,
    upper,
    sems,
):
    size = rows.shape[1]
    piece = size // n_row
    core = lax.axis_index("col") & 1
    near = pl.ds(pl.multiple_of(core * size, size), size)
    far = pl.ds(pl.multiple_of((1 - core) * size, size), size)
    copies = [
        pltpu.make_async_copy(upper_ref.at[step, near], upper, sems.at[0]),
        pltpu.make_async_copy(lower_ref.at[step], lower, sems.at[1]),
        pltpu.make_async_copy(upper_ref.at[step, far], upper_out, sems.at[2]),
    ]
    for copy in copies:
        copy.start()
    for r in range(n_row):
        at = 2 * piece * r
        rows[piece * r : piece * (r + 1)] = gathered_ref[at : at + piece]
        rows[size + piece * r : size + piece * (r + 1)] = gathered_ref[
            at + piece : at + 2 * piece
        ]
    copies[0].wait()
    cols_out[...] = dot(split(mine_ref[...]), split(upper[...]))
    copies[1].wait()
    rows_out[...] = dot(split(lower[...]), split(rows[...]))
    copies[2].wait()


def late_kernel(
    n_row, step, flags, other_ref, part_ref, rows_ref, upper_ref, block_ref, out_ref, cols
):
    size = rows_ref.shape[1]
    my_row, my_col = lax.axis_index("row"), lax.axis_index("col")
    core = my_col & 1
    first = flags[6 + step]
    cols[...] = part_ref[...] + dot(split(other_ref[...]), split(upper_ref[...]))
    col_hit = flags[4 + step] > 0
    rows = rows_ref[...]
    kept = split(jnp.where(col_hit, rows, jnp.float32(0.0)))
    owner = (my_col >> 1) == (first >> 1)
    for slot in range(2):
        at = slice(slot * size, (slot + 1) * size)
        row_hit = flags[2 * step + slot] > 0
        whole = cols[at]
        masked = jnp.where(row_hit, whole, jnp.float32(0.0))
        new = block_ref[at] - dot(split(masked), kept)
        own = jnp.where(core == 0, whole[:, :size], whole[:, size:])
        new = jnp.where(owner & row_hit, own, new)
        for member in range(2):
            here = (
                (my_row == lax.rem(first + member, n_row))
                & (slot == lax.div(first, n_row))
                & col_hit
            )
            new = jnp.where(here, rows[member * size : (member + 1) * size], new)
        out_ref[at] = new


def local(matrix, row_struct, col_struct, panel_index, lower_inv, upper_inv):
    n_row = lax.axis_size("row")
    n_col = lax.axis_size("col")
    n_z = n_col // 2
    my_z = lax.axis_index("col") >> 1
    width = upper_inv.shape[1]
    size = width // 2
    piece = size // n_row

    def send_z(value, hops):
        pairs = [(2 * (a % n_z) + c, 2 * (b % n_z) + c) for a, b in hops for c in range(2)]
        return lax.ppermute(value, "col", pairs)

    def from_class(value, place, spacing, hop):
        return send_z(value, [(z, z + hop) for z in range(place % spacing, n_z, spacing)])

    def exchange(value):
        return lax.all_to_all(value, "row", 0, 0, tiled=True)

    def fetch(place):
        def run(block, chunk_at, own_at, dist, near):
            across = from_class(block, place, 8, 8)
            ahead = from_class(block, place, 4, 4)
            behind = from_class(block, place, 4, -4)
            own = lax.dynamic_slice_in_dim(block, own_at, size, 0)
            chunk = lax.dynamic_slice_in_dim(exchange(own), chunk_at, 2 * piece, 0)
            tiled, anchor = lax.optimization_barrier((jnp.tile(chunk, (n_row, 1)), block))
            gathered = exchange(tiled)
            middle = jnp.where(
                dist == 8,
                across,
                jnp.where(dist == 4, ahead, jnp.where(dist == n_z - 4, behind, anchor)),
            )
            up = from_class(middle, place, 4, 1)
            down = from_class(middle, place, 4, -1)
            top = from_class(middle[:size], place, 4, 2)
            bottom = from_class(middle[size:], place, 4, -2)
            both = jnp.concatenate([top, bottom], axis=0)
            columns = jnp.where(
                near == 0, middle, jnp.where(near == 1, up, jnp.where(near == 3, down, both))
            )
            return columns, gathered

        return run

    fetches = [fetch(place) for place in range(8)]
    whole = pl.BlockSpec(memory_space=pltpu.VMEM)
    scalars = pl.BlockSpec(memory_space=pltpu.SMEM)
    outside = pl.BlockSpec(memory_space=pltpu.HBM)
    params = pltpu.CompilerParams(vmem_limit_bytes=VMEM_BYTES)
    cost = pl.CostEstimate(
        flops=6 * width * width * width, bytes_accessed=12 * width * width, transcendentals=0
    )
    f32 = jnp.float32
    flags = jnp.concatenate([row_struct.reshape(-1), col_struct.reshape(-1), panel_index])

    places = []
    for step in range(panel_index.shape[0]):
        first = panel_index[step]
        plane = first >> 1
        dist = (my_z - plane) & (n_z - 1)
        places += [
            plane & 7,
            (first & (n_row - 1)) * piece,
            (first >> (n_row.bit_length() - 1)) * size,
            dist,
            dist & 3,
        ]
    flags, places = lax.optimization_barrier((flags, places))

    block = matrix
    for step in range(panel_index.shape[0]):
        which, *at = places[5 * step : 5 * step + 5]
        mine, gathered = lax.switch(which, fetches, block, *at)
        other = lax.ppermute(mine, "col", [(i, i ^ 1) for i in range(n_col)])
        rows, part, upper = pl.pallas_call(
            functools.partial(early_kernel, n_row, step),
            out_shape=(
                jax.ShapeDtypeStruct((width, size), f32),
                jax.ShapeDtypeStruct((2 * size, width), f32),
                jax.ShapeDtypeStruct((size, width), f32),
            ),
            in_specs=[whole, whole, outside, outside],
            out_specs=(whole, whole, whole),
            scratch_shapes=[
                pltpu.VMEM((width, size), f32),
                pltpu.VMEM((width, width), f32),
                pltpu.VMEM((size, width), f32),
                pltpu.SemaphoreType.DMA((3,)),
            ],
            compiler_params=params,
            cost_estimate=cost,
            name="early",
        )(gathered, mine, lower_inv, upper_inv)
        block = pl.pallas_call(
            functools.partial(late_kernel, n_row, step),
            out_shape=jax.ShapeDtypeStruct(matrix.shape, f32),
            in_specs=[scalars, whole, whole, whole, whole, whole],
            out_specs=whole,
            scratch_shapes=[pltpu.VMEM((2 * size, width), f32)],
            compiler_params=params,
            cost_estimate=cost,
            name="late",
        )(flags, other, part, rows, upper, block)
    return block


def solution(mesh):
    return jax.shard_map(
        local,
        mesh=mesh,
        in_specs=(P("row", "col"), P(None, "row"), P(None, "col"), P(), P(), P()),
        out_specs=P("row", "col"),
        check_vma=False,
    )
```

time: 152 us -> 150 us (0.987)
  loops' own time: 11.6 us -> 0.42 us
  waiting for transfers between devices: 60.4 us -> 67.2 us
  Pallas kernels: 8.67 us -> 10.9 us
  between operations: 5.77 us -> 3.7 us
    another operation x4 -> x2, loops' own time: 11.6 us -> 0.42 us  [local(): mine, gathered = lax.switch(which, fetches, block, *at)]
    ppermute x14, waiting for transfers between devices: 44.5 us -> 51.1 us  [send_z(): return lax.ppermute(value, 'col', pairs)]
    all_to_all x4, starting transfers between devices: 22 us -> 18.8 us  [exchange(): return lax.all_to_all(value, 'row', 0, 0, tiled=True)]
    ppermute x2, starting transfers between devices: 8.65 us -> 11.1 us  [local(): other = lax.ppermute(mine, 'col', [(i, i ^ 1) for i in range(n_col)])]
    pallas_call x4, Pallas kernels: 8.67 us -> 10.9 us  [the longest x2 6.71 us: local(): pl.pallas_call(functools.partial(early_kernel, n_row, step), out_shape=(j...]
    ppermute x14, starting transfers between devices: 16.1 us -> 17.6 us  [send_z(): return lax.ppermute(value, 'col', pairs)]
    unnamed x17 -> x10, local copies, waits for them, and re-layouts: 4.08 us -> 3.97 us
  transfers between devices with their start and end apart: 20 -> 20, of which waited for: 6 -> 4; matrix products, arithmetic and copies ran while one was open for 6% -> 6% of each run, Pallas kernels for 3% -> 4%
where the time goes in v2:
time: 150 us; the launch traced here: 149 us
  waiting for transfers between devices  67.2 us (45%)
  starting transfers between devices  47.4 us (32%)
  local copies, waits for them, and re-layouts  14 us (9%)
  Pallas kernels  10.9 us (7%)
  other arithmetic  5.5 us (4%)
  between operations  3.7 us (2%)
    ppermute x14, waiting for transfers between devices, send_z(): return lax.ppermute(value, 'col', pairs)  51.1 us
    all_to_all x4, starting transfers between devices, exchange(): return lax.all_to_all(value, 'row', 0, 0, tiled=True)  18.8 us
    ppermute x14, starting transfers between devices, send_z(): return lax.ppermute(value, 'col', pairs)  17.6 us
    all_to_all x4, waiting for transfers between devices, exchange(): return lax.all_to_all(value, 'row', 0, 0, tiled=True)  16 us
    ppermute x2, starting transfers between devices, local(): other = lax.ppermute(mine, 'col', [(i, i ^ 1) for i in range(n_col)])  11.1 us
    pallas_call x2, Pallas kernels, local(): pl.pallas_call(functools.partial(early_kernel, n_row, step), out_shape=(j...  6.71 us
    pallas_call x2, Pallas kernels, local(): pl.pallas_call(functools.partial(late_kernel, n_row, step), out_shape=jax...  4.21 us
    unnamed x10, local copies, waits for them, and re-layouts  3.97 us
  transfers between devices with their start and end apart: 20, of which 4 were waited for; matrix products, arithmetic and copies ran while one was open for 6% of the time, Pallas kernels for 4%

profile of v2, /device:TPU:33, one launch (start us, length us, event | category | flops | bytes accessed | tf_op | source)
XLA Modules:
  0.0 149.2 jit_solution(11492102736544012613)
XLA Ops:
  6.4 56.7 %conditional.2 = (f32[512,256]{1,0:T(8,128)S(1)}, f32[512,256]{1,0:T(8,128)}) conditional(s32[]{:T(128)} %clamp.7, (s32[]{:T(128)}, s32[]{:T(128)}, f32[512,256]{1,0:T(8,128)}, s32[]{:T(128)}, s32[]{:T(128)}) %tuple.87, (s32[]{:T(128)}, s32[]{:T(128)}, f32[512,256]{1,0:T(8,128)}, s32[]{:T(128)}, s32[]{:T(128)}) %tuple.87, ...), branch_computations={%region_0.1_spmd, %region_1.2_spmd, %region_2.3_spmd, %region_3.4_... | conditional | flops 917516 | bytes 26575396 | solution.py:168
  7.9 1.5 collective-permute-start.2
  9.4 1.7 %constant_dynamic-slice_fusion.1 = f32[256,256]{1,0:T(8,128)} fusion(f32[512,256]{1,0:T(8,128)} %get-tuple-element.170, s32[]{:T(128)S(6)} %select_n.454), kind=kLoop, calls=%fused_computation.5 | loop fusion | bytes 524292 | tf_op jit(solution)/shard_map/cond/branch_0_fun/dynamic_slice | solution.py:119
  11.1 6.8 %all-to-all-start = ((f32[16,16,256]{2,1,0:T(8,128)}), f32[16,16,256]{2,1,0:T(8,128)S(1)}, u32[]{:S(2)}, u32[]{:S(2)}) async-start(f32[16,16,256]{2,1,0:T(8,128)} %bitcast), calls=%async_computation | async-start | bytes 524288 | tf_op jit(solution)/shard_map/cond/branch_0_fun/all_to_all | solution.py:112
  17.9 7.5 %all-to-all-done = f32[16,16,256]{2,1,0:T(8,128)S(1)} async-done(((f32[16,16,256]{2,1,0:T(8,128)}), f32[16,16,256]{2,1,0:T(8,128)S(1)}, u32[]{:S(2)}, u32[]{:S(2)}) %all-to-all-start) | async-done | bytes 262176 | tf_op jit(solution)/shard_map/cond/branch_0_fun/all_to_all | solution.py:112
  29.6 1.5 collective-permute-start.4
  34.5 4.2 %all-to-all-start.1 = ((f32[16,32,256]{2,1,0:T(8,128)}), f32[16,32,256]{2,1,0:T(8,128)}, u32[]{:S(2)}, u32[]{:S(2)}) async-start(f32[16,32,256]{2,1,0:T(8,128)} %bitcast.3), calls=%async_computation.1 | async-start | bytes 1048576 | tf_op jit(solution)/shard_map/cond/branch_0_fun/all_to_all | solution.py:112
  38.8 22.0 %collective-permute-done.3 = f32[512,256]{1,0:T(8,128)S(1)} collective-permute-done((f32[512,256]{1,0:T(8,128)S(1)}, f32[512,256]{1,0:T(8,128)S(1)}, u32[]{:S(2)}, u32[]{:S(2)}) %collective-permute-start.3) | collective-permute-done | bytes 524320 | tf_op jit(solution)/shard_map/cond/branch_0_fun/ppermute | solution.py:106
  63.9 8.2 %collective-permute-start.112 = (f32[512,256]{1,0:T(8,128)}, f32[512,256]{1,0:T(8,128)S(1)}, u32[]{:S(2)}, u32[]{:S(2)}) collective-permute-start(f32[512,256]{1,0:T(8,128)} %copy-done.4), channel_id=1, source_target_pairs={{0,1},{1,0},{2,3},{3,2},{4,5},{5,4},{6,7},{7,6},{8,9},{9,8},{10,11... | collective-permute-start | bytes 1572872 | tf_op jit(solution)/shard_map/ppermute | solution.py:169
  72.1 1.6 %copy-done.1 = f32[2,512,512]{2,1,0:T(8,128)S(1)} copy-done((f32[2,512,512]{2,1,0:T(8,128)S(1)}, f32[2,512,512]{2,1,0:T(8,128)}, u32[]{:S(2)}) %copy-start.1) | copy-done | bytes 2097176
  73.7 3.4 %early.2 = (f32[512,256]{1,0:T(8,128)S(1)}, f32[512,512]{1,0:T(8,128)S(1)}, f32[256,512]{1,0:T(8,128)S(1)}) custom-call(f32[512,256]{1,0:T(8,128)} %get-tuple-element.308.gathered_ref, f32[512,256]{1,0:T(8,128)} %copy-done.4, f32[2,512,512]{2,1,0:T(8,128)S(1)} %copy-done, f32[2,512,512]{2,1,0:T(8,128)S(1)} %copy-done.1), custom_call_target="tpu_custom_call" | custom-call | flops 805306368 | bytes 3145728 | tf_op jit(solution)/shard_map/early/pallas_call | solution.py:170
  77.1 1.7 %late.2.block_ref = f32[512,256]{1,0:T(8,128)S(1)} custom-call(s32[8]{0:T(128)S(1)} %pad_add_fusion.flags, f32[512,256]{1,0:T(8,128)S(1)} %collective-permute-done.112.other_ref, f32[512,512]{1,0:T(8,128)S(1)} %get-tuple-element.309.part_ref, f32[512,256]{1,0:T(8,128)S(1)} %get-tuple-element.310.rows_ref, f32[256,512]{1,0:T(8,128)S(1)} %get-tuple-element.311.upper_ref, ...), custom_call_target="tpu_custom_call" | custom-call | flops 805306368 | bytes 3145728 | tf_op jit(solution)/shard_map/late/pallas_call | solution.py:189
  78.8 60.0 %conditional.3 = (f32[512,256]{1,0:T(8,128)}, f32[512,256]{1,0:T(8,128)}) conditional(s32[]{:T(128)} %clamp.6, (s32[]{:T(128)}, s32[]{:T(128)}, f32[512,256]{1,0:T(8,128)S(1)}, s32[]{:T(128)}, s32[]{:T(128)}) %tuple.88, (s32[]{:T(128)}, s32[]{:T(128)}, f32[512,256]{1,0:T(8,128)S(1)}, s32[]{:T(128)}, ...), branch_computations={%region_8.9_spmd, %region_9.10_spmd, %region_10.11_spmd, %region_1... | conditional | flops 917516 | bytes 24478216 | solution.py:168
  79.6 1.5 collective-permute-start.106
  83.3 3.5 %all-to-all-start.30 = ((f32[16,16,256]{2,1,0:T(8,128)}), f32[16,16,256]{2,1,0:T(8,128)S(1)}, u32[]{:S(2)}, u32[]{:S(2)}) async-start(f32[16,16,256]{2,1,0:T(8,128)} %bitcast.75), calls=%async_computation.30 | async-start | bytes 524288 | tf_op jit(solution)/shard_map/cond/branch_7_fun/all_to_all | solution.py:112
  86.8 8.5 %all-to-all-done.30 = f32[16,16,256]{2,1,0:T(8,128)S(1)} async-done(((f32[16,16,256]{2,1,0:T(8,128)}), f32[16,16,256]{2,1,0:T(8,128)S(1)}, u32[]{:S(2)}, u32[]{:S(2)}) %all-to-all-start.30) | async-done | bytes 262176 | tf_op jit(solution)/shard_map/cond/branch_7_fun/all_to_all | solution.py:112
  97.1 1.5 collective-permute-start.108
  103.4 4.2 %all-to-all-start.31 = ((f32[16,32,256]{2,1,0:T(8,128)}), f32[16,32,256]{2,1,0:T(8,128)}, u32[]{:S(2)}, u32[]{:S(2)}) async-start(f32[16,32,256]{2,1,0:T(8,128)} %tile.122), calls=%async_computation.31 | async-start | bytes 1048576 | tf_op jit(solution)/shard_map/cond/branch_7_fun/all_to_all | solution.py:112
  107.7 29.1 %collective-permute-done.110 = f32[256,256]{1,0:T(8,128)} collective-permute-done((f32[256,256]{1,0:T(8,128)}, f32[256,256]{1,0:T(8,128)}, u32[]{:S(2)}, u32[]{:S(2)}) %collective-permute-start.110) | collective-permute-done | bytes 262176 | tf_op jit(solution)/shard_map/cond/branch_7_fun/ppermute | solution.py:106
  136.8 2.0 %fusion.31 = f32[512,256]{1,0:T(8,128)} fusion(f32[512,256]{1,0:T(8,128)S(1)} %select_select_fusion.15, f32[512,256]{1,0:T(8,128)} %collective-permute-done.108, f32[512,256]{1,0:T(8,128)} %collective-permute-done.109, f32[256,256]{1,0:T(8,128)} %collective-permute-done.111, f32[256,256]{1,0:T(8,128)} %collective-permute-done.110, pred[]{:T(512)S(6)} %eq.287, ...), kind=kLoop, calls=%fused_computation.92 | loop fusion | flops 524288 | bytes 2621443 | tf_op jit(solution)/shard_map/cond/branch_7_fun/jit(_where)/select_n | solution.py:133
  138.8 2.9 %collective-permute-start.113 = (f32[512,256]{1,0:T(8,128)}, f32[512,256]{1,0:T(8,128)S(1)}, u32[]{:S(2)}, u32[]{:S(2)}) collective-permute-start(f32[512,256]{1,0:T(8,128)} %get-tuple-element.314.mine_ref), channel_id=1, source_target_pairs={{0,1},{1,0},{2,3},{3,2},{4,5},{5,4},{6,7},{7,6},{8,9},{9,8},{10,11... | collective-permute-start | bytes 1572872 | tf_op jit(solution)/shard_map/ppermute | solution.py:169
  141.7 1.6 %copy-done.2 = f32[2,512,512]{2,1,0:T(8,128)S(1)} copy-done((f32[2,512,512]{2,1,0:T(8,128)S(1)}, f32[2,512,512]{2,1,0:T(8,128)}, u32[]{:S(2)}) %copy-start.2) | copy-done | bytes 2097176
  143.3 3.3 %early.3 = (f32[512,256]{1,0:T(8,128)S(1)}, f32[512,512]{1,0:T(8,128)S(1)}, f32[256,512]{1,0:T(8,128)S(1)}) custom-call(f32[512,256]{1,0:T(8,128)} %get-tuple-element.315.gathered_ref, f32[512,256]{1,0:T(8,128)} %get-tuple-element.314.mine_ref, f32[2,512,512]{2,1,0:T(8,128)S(1)} %copy-done, f32[2,512,512]{2,1,0:T(8,128)S(1)} %copy-done.2), custom_call_target="tpu_custom_call" | custom-call | flops 805306368 | bytes 3145728 | tf_op jit(solution)/shard_map/early/pallas_call | solution.py:170
  146.7 2.5 %late.3 = f32[512,256]{1,0:T(8,128)} custom-call(s32[8]{0:T(128)S(1)} %pad_add_fusion.flags, f32[512,256]{1,0:T(8,128)S(1)} %collective-permute-done.113.other_ref, f32[512,512]{1,0:T(8,128)S(1)} %get-tuple-element.316.part_ref, f32[512,256]{1,0:T(8,128)S(1)} %get-tuple-element.317.rows_ref, f32[256,512]{1,0:T(8,128)S(1)} %get-tuple-element.318.upper_ref, ...), custom_call_target="tpu_custom_call" | custom-call | flops 805306368 | bytes 3145728 | tf_op jit(solution)/shard_map/late/pallas_call | solution.py:189
  (53 shorter events, 24.4 us)
Async XLA Ops:
  6.4 65.7 %copy-start = (f32[2,512,512]{2,1,0:T(8,128)S(1)}, f32[2,512,512]{2,1,0:T(8,128)}, u32[]{:S(2)}) copy-start(f32[2,512,512]{2,1,0:T(8,128)} %lower_ref.3) | copy-start | bytes 6291460
  6.4 19.8 %collective-permute-start = (f32[512,256]{1,0:T(8,128)}, f32[512,256]{1,0:T(8,128)S(1)}, u32[]{:S(2)}, u32[]{:S(2)}) collective-permute-start(f32[512,256]{1,0:T(8,128)} %get-tuple-element.170), channel_id=1, source_target_pairs={{0,16},{1,17},{16,0},{17,1},{32,48},{33,49},{48,32},{49,33},{64,80... | collective-permute-start | bytes 1572872 | tf_op jit(solution)/shard_map/cond/branch_0_fun/ppermute | solution.py:106
  7.2 19.0 %collective-permute-start.1 = (f32[512,256]{1,0:T(8,128)}, f32[512,256]{1,0:T(8,128)S(1)}, u32[]{:S(2)}, u32[]{:S(2)}) collective-permute-start(f32[512,256]{1,0:T(8,128)} %get-tuple-element.170), channel_id=1, source_target_pairs={{0,8},{1,9},{8,16},{9,17},{16,24},{17,25},{24,0},{25,1},{32,40},{3... | collective-permute-start | bytes 1572872 | tf_op jit(solution)/shard_map/cond/branch_0_fun/ppermute | solution.py:106
  7.9 19.1 %collective-permute-start.2 = (f32[512,256]{1,0:T(8,128)}, f32[512,256]{1,0:T(8,128)}, u32[]{:S(2)}, u32[]{:S(2)}) collective-permute-start(f32[512,256]{1,0:T(8,128)} %get-tuple-element.170), channel_id=1, source_target_pairs={{0,24},{1,25},{8,0},{9,1},{16,8},{17,9},{24,16},{25,17},{32,56},{3... | collective-permute-start | bytes 1572872 | tf_op jit(solution)/shard_map/cond/branch_0_fun/ppermute | solution.py:106
  11.1 14.3 %all-to-all-start = ((f32[16,16,256]{2,1,0:T(8,128)}), f32[16,16,256]{2,1,0:T(8,128)S(1)}, u32[]{:S(2)}, u32[]{:S(2)}) async-start(f32[16,16,256]{2,1,0:T(8,128)} %bitcast), calls=%async_computation | async-start | bytes 524288 | tf_op jit(solution)/shard_map/cond/branch_0_fun/all_to_all | solution.py:112
  28.3 32.5 %collective-permute-start.3 = (f32[512,256]{1,0:T(8,128)S(1)}, f32[512,256]{1,0:T(8,128)S(1)}, u32[]{:S(2)}, u32[]{:S(2)}) collective-permute-start(f32[512,256]{1,0:T(8,128)S(1)} %select_select_fusion), channel_id=1, source_target_pairs={{0,2},{1,3},{8,10},{9,11},{16,18},{17,19},{24,26},{25,27},{32,34},... | collective-permute-start | bytes 1572872 | tf_op jit(solution)/shard_map/cond/branch_0_fun/ppermute | solution.py:106
  29.6 32.0 %collective-permute-start.4 = (f32[512,256]{1,0:T(8,128)S(1)}, f32[512,256]{1,0:T(8,128)}, u32[]{:S(2)}, u32[]{:S(2)}) collective-permute-start(f32[512,256]{1,0:T(8,128)S(1)} %select_select_fusion), channel_id=1, source_target_pairs={{0,30},{1,31},{8,6},{9,7},{16,14},{17,15},{24,22},{25,23},{32,62},... | collective-permute-start | bytes 1572872 | tf_op jit(solution)/shard_map/cond/branch_0_fun/ppermute | solution.py:106
  31.8 7.0 %collective-permute-start.5 = (f32[256,256]{1,0:T(8,128)}, f32[256,256]{1,0:T(8,128)}, u32[]{:S(2)}, u32[]{:S(2)}) collective-permute-start(f32[256,256]{1,0:T(8,128)} %get-tuple-element.319), channel_id=1, source_target_pairs={{0,4},{1,5},{8,12},{9,13},{16,20},{17,21},{24,28},{25,29},{32,36},... | collective-permute-start | bytes 786440 | tf_op jit(solution)/shard_map/cond/branch_0_fun/ppermute | solution.py:106
  33.2 5.6 %collective-permute-start.6 = (f32[256,256]{1,0:T(8,128)S(1)}, f32[256,256]{1,0:T(8,128)}, u32[]{:S(2)}, u32[]{:S(2)}) collective-permute-start(f32[256,256]{1,0:T(8,128)S(1)} %get-tuple-element.320), channel_id=1, source_target_pairs={{0,28},{1,29},{8,4},{9,5},{16,12},{17,13},{24,20},{25,21},{32,60},... | collective-permute-start | bytes 786440 | tf_op jit(solution)/shard_map/cond/branch_0_fun/ppermute | solution.py:106
  34.5 28.4 %all-to-all-start.1 = ((f32[16,32,256]{2,1,0:T(8,128)}), f32[16,32,256]{2,1,0:T(8,128)}, u32[]{:S(2)}, u32[]{:S(2)}) async-start(f32[16,32,256]{2,1,0:T(8,128)} %bitcast.3), calls=%async_computation.1 | async-start | bytes 1048576 | tf_op jit(solution)/shard_map/cond/branch_0_fun/all_to_all | solution.py:112
  63.9 13.2 %collective-permute-start.112 = (f32[512,256]{1,0:T(8,128)}, f32[512,256]{1,0:T(8,128)S(1)}, u32[]{:S(2)}, u32[]{:S(2)}) collective-permute-start(f32[512,256]{1,0:T(8,128)} %copy-done.4), channel_id=1, source_target_pairs={{0,1},{1,0},{2,3},{3,2},{4,5},{5,4},{6,7},{7,6},{8,9},{9,8},{10,11... | collective-permute-start | bytes 1572872 | tf_op jit(solution)/shard_map/ppermute | solution.py:169
  72.1 1.6 %copy-start.1 = (f32[2,512,512]{2,1,0:T(8,128)S(1)}, f32[2,512,512]{2,1,0:T(8,128)}, u32[]{:S(2)}) copy-start(f32[2,512,512]{2,1,0:T(8,128)} %upper_ref.3) | copy-start | bytes 6291460
  73.7 3.4 %copy-start.3 = (f32[512,256]{1,0:T(8,128)S(1)}, f32[512,256]{1,0:T(8,128)}, u32[]{:S(2)}) copy-start(f32[512,256]{1,0:T(8,128)} %block_ref.1) | copy-start | bytes 1572868
  78.9 17.3 %collective-permute-start.105 = (f32[512,256]{1,0:T(8,128)S(1)}, f32[512,256]{1,0:T(8,128)S(1)}, u32[]{:S(2)}, u32[]{:S(2)}) collective-permute-start(f32[512,256]{1,0:T(8,128)S(1)} %get-tuple-element.275), channel_id=1, source_target_pairs={{14,30},{15,31},{30,14},{31,15},{46,62},{47,63},{62,46},{63,47},{7... | collective-permute-start | bytes 1572872 | tf_op jit(solution)/shard_map/cond/branch_7_fun/ppermute | solution.py:106
  79.6 16.6 %collective-permute-start.106 = (f32[512,256]{1,0:T(8,128)S(1)}, f32[512,256]{1,0:T(8,128)}, u32[]{:S(2)}, u32[]{:S(2)}) collective-permute-start(f32[512,256]{1,0:T(8,128)S(1)} %get-tuple-element.275), channel_id=1, source_target_pairs={{6,14},{7,15},{14,22},{15,23},{22,30},{23,31},{30,6},{31,7},{38,46... | collective-permute-start | bytes 1572872 | tf_op jit(solution)/shard_map/cond/branch_7_fun/ppermute | solution.py:106
  81.1 15.9 %collective-permute-start.107 = (f32[512,256]{1,0:T(8,128)S(1)}, f32[512,256]{1,0:T(8,128)}, u32[]{:S(2)}, u32[]{:S(2)}) collective-permute-start(f32[512,256]{1,0:T(8,128)S(1)} %get-tuple-element.275), channel_id=1, source_target_pairs={{6,30},{7,31},{14,6},{15,7},{22,14},{23,15},{30,22},{31,23},{38,62... | collective-permute-start | bytes 1572872 | tf_op jit(solution)/shard_map/cond/branch_7_fun/ppermute | solution.py:106
  83.3 12.0 %all-to-all-start.30 = ((f32[16,16,256]{2,1,0:T(8,128)}), f32[16,16,256]{2,1,0:T(8,128)S(1)}, u32[]{:S(2)}, u32[]{:S(2)}) async-start(f32[16,16,256]{2,1,0:T(8,128)} %bitcast.75), calls=%async_computation.30 | async-start | bytes 524288 | tf_op jit(solution)/shard_map/cond/branch_7_fun/all_to_all | solution.py:112
  97.1 39.7 %collective-permute-start.108 = (f32[512,256]{1,0:T(8,128)S(1)}, f32[512,256]{1,0:T(8,128)}, u32[]{:S(2)}, u32[]{:S(2)}) collective-permute-start(f32[512,256]{1,0:T(8,128)S(1)} %select_select_fusion.15), channel_id=1, source_target_pairs={{6,8},{7,9},{14,16},{15,17},{22,24},{23,25},{30,0},{31,1},{38,40},... | collective-permute-start | bytes 1572872 | tf_op jit(solution)/shard_map/cond/branch_7_fun/ppermute | solution.py:106
  98.6 38.2 %collective-permute-start.109 = (f32[512,256]{1,0:T(8,128)S(1)}, f32[512,256]{1,0:T(8,128)}, u32[]{:S(2)}, u32[]{:S(2)}) collective-permute-start(f32[512,256]{1,0:T(8,128)S(1)} %select_select_fusion.15), channel_id=1, source_target_pairs={{6,4},{7,5},{14,12},{15,13},{22,20},{23,21},{30,28},{31,29},{38,36... | collective-permute-start | bytes 1572872 | tf_op jit(solution)/shard_map/cond/branch_7_fun/ppermute | solution.py:106
  100.8 36.0 %collective-permute-start.110 = (f32[256,256]{1,0:T(8,128)}, f32[256,256]{1,0:T(8,128)}, u32[]{:S(2)}, u32[]{:S(2)}) collective-permute-start(f32[256,256]{1,0:T(8,128)} %get-tuple-element.349), channel_id=1, source_target_pairs={{6,10},{7,11},{14,18},{15,19},{22,26},{23,27},{30,2},{31,3},{38,42... | collective-permute-start | bytes 786440 | tf_op jit(solution)/shard_map/cond/branch_7_fun/ppermute | solution.py:106
  102.1 34.7 %collective-permute-start.111 = (f32[256,256]{1,0:T(8,128)S(1)}, f32[256,256]{1,0:T(8,128)}, u32[]{:S(2)}, u32[]{:S(2)}) collective-permute-start(f32[256,256]{1,0:T(8,128)S(1)} %get-tuple-element.350), channel_id=1, source_target_pairs={{6,2},{7,3},{14,10},{15,11},{22,18},{23,19},{30,26},{31,27},{38,34... | collective-permute-start | bytes 786440 | tf_op jit(solution)/shard_map/cond/branch_7_fun/ppermute | solution.py:106
  103.4 35.4 %all-to-all-start.31 = ((f32[16,32,256]{2,1,0:T(8,128)}), f32[16,32,256]{2,1,0:T(8,128)}, u32[]{:S(2)}, u32[]{:S(2)}) async-start(f32[16,32,256]{2,1,0:T(8,128)} %tile.122), calls=%async_computation.31 | async-start | bytes 1048576 | tf_op jit(solution)/shard_map/cond/branch_7_fun/all_to_all | solution.py:112
  138.8 7.8 %collective-permute-start.113 = (f32[512,256]{1,0:T(8,128)}, f32[512,256]{1,0:T(8,128)S(1)}, u32[]{:S(2)}, u32[]{:S(2)}) collective-permute-start(f32[512,256]{1,0:T(8,128)} %get-tuple-element.314.mine_ref), channel_id=1, source_target_pairs={{0,1},{1,0},{2,3},{3,2},{4,5},{5,4},{6,7},{7,6},{8,9},{9,8},{10,11... | collective-permute-start | bytes 1572872 | tf_op jit(solution)/shard_map/ppermute | solution.py:169
  141.7 1.6 %copy-start.2 = (f32[2,512,512]{2,1,0:T(8,128)S(1)}, f32[2,512,512]{2,1,0:T(8,128)}, u32[]{:S(2)}) copy-start(f32[2,512,512]{2,1,0:T(8,128)} %upper_ref.3) | copy-start | bytes 6291460
  (4 other events, 3.2 us)

commit v3 on v2

v3 whole, which is shorter than its diff:
```python
import functools

import jax
import jax.numpy as jnp
from jax import lax
from jax.experimental import pallas as pl
from jax.experimental.pallas import tpu as pltpu
from jax.sharding import PartitionSpec as P

VMEM_BYTES = 40 * 1024 * 1024


def split(value):
    high = value.astype(jnp.bfloat16)
    low = (value - high.astype(jnp.float32)).astype(jnp.bfloat16)
    return high, low


def dot(a, b):
    (a_high, a_low), (b_high, b_low) = a, b
    mul = functools.partial(jnp.dot, preferred_element_type=jnp.float32)
    return mul(a_high, b_high) + (mul(a_high, b_low) + mul(a_low, b_high))


def early_kernel(n_row, gathered_ref, mine_ref, lower_ref, upper_ref, rows_out, cols_out, rows):
    size = rows.shape[1]
    piece = size // n_row
    for r in range(n_row):
        at = 2 * piece * r
        rows[piece * r : piece * (r + 1)] = gathered_ref[at : at + piece]
        rows[size + piece * r : size + piece * (r + 1)] = gathered_ref[
            at + piece : at + 2 * piece
        ]
    half = pl.ds(pl.multiple_of((lax.axis_index("col") & 1) * size, size), size)
    rows_out[...] = dot(split(lower_ref[...]), split(rows[...]))
    cols_out[...] = dot(split(mine_ref[...]), split(upper_ref[half]))


def late_kernel(
    n_row, step, flags, other_ref, part_ref, rows_ref, upper_ref, block_ref, out_ref, cols
):
    size = rows_ref.shape[1]
    my_row, my_col = lax.axis_index("row"), lax.axis_index("col")
    core = my_col & 1
    first = flags[6 + step]
    half = pl.ds(pl.multiple_of((1 - core) * size, size), size)
    cols[...] = part_ref[...] + dot(split(other_ref[...]), split(upper_ref[half]))
    col_hit = flags[4 + step] > 0
    rows = rows_ref[...]
    kept = split(jnp.where(col_hit, rows, jnp.float32(0.0)))
    owner = (my_col >> 1) == (first >> 1)
    for slot in range(2):
        at = slice(slot * size, (slot + 1) * size)
        row_hit = flags[2 * step + slot] > 0
        whole = cols[at]
        masked = jnp.where(row_hit, whole, jnp.float32(0.0))
        new = block_ref[at] - dot(split(masked), kept)
        own = jnp.where(core == 0, whole[:, :size], whole[:, size:])
        new = jnp.where(owner & row_hit, own, new)
        for member in range(2):
            here = (
                (my_row == lax.rem(first + member, n_row))
                & (slot == lax.div(first, n_row))
                & col_hit
            )
            new = jnp.where(here, rows[member * size : (member + 1) * size], new)
        out_ref[at] = new


def local(matrix, row_struct, col_struct, panel_index, lower_inv, upper_inv):
    n_row = lax.axis_size("row")
    n_col = lax.axis_size("col")
    n_z = n_col // 2
    my_z = lax.axis_index("col") >> 1
    width = upper_inv.shape[1]
    size = width // 2
    piece = size // n_row

    def send_z(value, hops):
        pairs = [(2 * (a % n_z) + c, 2 * (b % n_z) + c) for a, b in hops for c in range(2)]
        return lax.ppermute(value, "col", pairs)

    def from_class(value, place, spacing, hop):
        return send_z(value, [(z, z + hop) for z in range(place % spacing, n_z, spacing)])

    def exchange(value):
        return lax.all_to_all(value, "row", 0, 0, tiled=True)

    def to_leaders(place):
        hops = [hop if hop >= -7 else 8 for hop in (3 - place, 7 - place, -1 - place, -5 - place)]

        def run(block, chunk_at, own, dist, plane):
            quarter = None
            for n, hop in enumerate(hops):
                at = (((plane >> 2) + (0, 1, 3, 2)[n]) & 3) * part_rows
                part = lax.dynamic_slice_in_dim(block, at, part_rows, 0)
                got = part if hop == 0 else from_class(part, place, 4, hop)
                quarter = got if n == 0 else jnp.where(dist == hop % n_z, got, quarter)
            chunk = lax.dynamic_slice_in_dim(exchange(own), chunk_at, 2 * piece, 0)
            return quarter, chunk

        return run

    def fetch(block, inverses, which, chunk_at, own_at, dist, plane):
        own = lax.dynamic_slice_in_dim(block, own_at, size, 0)
        quarter, chunk = lax.switch(which, leads, block, chunk_at, own, dist, plane)
        around = [quarter] + [from_class(quarter, 3, 4, hop) for hop in (-4, 8, 4)]
        middle = jnp.zeros((4,) + quarter.shape, quarter.dtype)
        for n in range(4):
            middle = lax.dynamic_update_index_in_dim(
                middle, around[n], ((my_z >> 2) + n) & 3, 0
            )
        middle = middle.reshape(block.shape)
        up = from_class(middle, 3, 4, 1)
        down = from_class(middle, 3, 4, -1)
        top = from_class(middle[:size], 3, 4, 2)
        bottom = from_class(middle[size:], 3, 4, -2)
        gathered = exchange(jnp.tile(chunk, (n_row, 1)))
        near = my_z & 3
        up, inverses = lax.optimization_barrier((up, inverses))
        both = jnp.concatenate([top, bottom], axis=0)
        columns = jnp.where(
            near == 3, middle, jnp.where(near == 0, up, jnp.where(near == 2, down, both))
        )
        return columns, gathered, inverses

    part_rows = matrix.shape[0] // 4
    leads = [to_leaders(place) for place in range(4)]
    whole = pl.BlockSpec(memory_space=pltpu.VMEM)
    scalars = pl.BlockSpec(memory_space=pltpu.SMEM)
    params = pltpu.CompilerParams(vmem_limit_bytes=VMEM_BYTES)
    cost = pl.CostEstimate(
        flops=6 * width * width * width, bytes_accessed=12 * width * width, transcendentals=0
    )
    f32 = jnp.float32
    flags = jnp.concatenate([row_struct.reshape(-1), col_struct.reshape(-1), panel_index])

    places = []
    for step in range(panel_index.shape[0]):
        first = panel_index[step]
        plane = first >> 1
        dist = (my_z - plane) & (n_z - 1)
        places += [
            plane & 3,
            (first & (n_row - 1)) * piece,
            (first >> (n_row.bit_length() - 1)) * size,
            dist,
            plane,
        ]
    flags, places = lax.optimization_barrier((flags, places))

    block = matrix
    for step in range(panel_index.shape[0]):
        inverses = lower_inv[step], upper_inv[step]
        mine, gathered, (lower, upper) = fetch(block, inverses, *places[5 * step : 5 * step + 5])
        other = lax.ppermute(mine, "col", [(i, i ^ 1) for i in range(n_col)])
        rows, part = pl.pallas_call(
            functools.partial(early_kernel, n_row),
            out_shape=(
                jax.ShapeDtypeStruct((width, size), f32),
                jax.ShapeDtypeStruct((2 * size, width), f32),
            ),
            in_specs=[whole] * 4,
            out_specs=(whole, whole),
            scratch_shapes=[pltpu.VMEM((width, size), f32)],
            compiler_params=params,
            cost_estimate=cost,
            name="early",
        )(gathered, mine, lower, upper)
        block = pl.pallas_call(
            functools.partial(late_kernel, n_row, step),
            out_shape=jax.ShapeDtypeStruct(matrix.shape, f32),
            in_specs=[scalars] + [whole] * 5,
            out_specs=whole,
            scratch_shapes=[pltpu.VMEM((2 * size, width), f32)],
            compiler_params=params,
            cost_estimate=cost,
            name="late",
        )(flags, other, part, rows, upper, block)
    return block


def solution(mesh):
    return jax.shard_map(
        local,
        mesh=mesh,
        in_specs=(P("row", "col"), P(None, "row"), P(None, "col"), P(), P(), P()),
        out_specs=P("row", "col"),
        check_vma=False,
    )
```

time: 150 us -> 178 us (1.19)
  waiting for transfers between devices: 67.2 us -> 87.6 us
  starting transfers between devices: 47.4 us -> 52.3 us
  local copies, waits for them, and re-layouts: 14 us -> 17.1 us
    ppermute x14 -> x21, waiting for transfers between devices: 51.1 us -> 75.2 us  [send_z(): return lax.ppermute(value, 'col', pairs)]
    all_to_all x4, waiting for transfers between devices: 16 us -> 11.9 us  [exchange(): return lax.all_to_all(value, 'row', 0, 0, tiled=True)]
    squeeze x0 -> x1, local copies, waits for them, and re-layouts: none -> 3.8 us  [local(): inverses = (lower_inv[step], upper_inv[step])]
    pallas_call x2, Pallas kernels: 6.71 us -> 3.32 us  [local(): pl.pallas_call(functools.partial(early_kernel, n_row), out_shape=(jax.Sha...]
    dynamic_slice x2 -> x4, local copies, waits for them, and re-layouts: 2.4 us -> 5.54 us  [the longest x2 3.35 us: fetch(): own = lax.dynamic_slice_in_dim(block, own_at, size, 0)]
    unnamed x10 -> x8, local copies, waits for them, and re-layouts: 3.97 us -> 1.23 us
    all_to_all x4, starting transfers between devices: 18.8 us -> 21.2 us  [exchange(): return lax.all_to_all(value, 'row', 0, 0, tiled=True)]
    ppermute x2, starting transfers between devices: 11.1 us -> 13 us  [local(): other = lax.ppermute(mine, 'col', [(i, i ^ 1) for i in range(n_col)])]
  transfers between devices with their start and end apart: 20 -> 27, of which waited for: 4 -> 7; matrix products, arithmetic and copies ran while one was open for 6% -> 8% of each run, Pallas kernels for 4% -> 2%
where the time goes in v3:
time: 178 us; the launch traced here: 176 us
  waiting for transfers between devices  87.6 us (49%)
  starting transfers between devices  52.3 us (29%)
  local copies, waits for them, and re-layouts  17.1 us (10%)
  Pallas kernels  9.36 us (5%)
  other arithmetic  5.31 us (3%)
  between operations  4.24 us (2%)
    ppermute x21, waiting for transfers between devices, send_z(): return lax.ppermute(value, 'col', pairs)  75.2 us
    all_to_all x4, starting transfers between devices, exchange(): return lax.all_to_all(value, 'row', 0, 0, tiled=True)  21.2 us
    ppermute x21, starting transfers between devices, send_z(): return lax.ppermute(value, 'col', pairs)  18.2 us
    ppermute x2, starting transfers between devices, local(): other = lax.ppermute(mine, 'col', [(i, i ^ 1) for i in range(n_col)])  13 us
    all_to_all x4, waiting for transfers between devices, exchange(): return lax.all_to_all(value, 'row', 0, 0, tiled=True)  11.9 us
    pallas_call x2, Pallas kernels, local(): pl.pallas_call(functools.partial(late_kernel, n_row, step), out_shape=jax...  6.05 us
    squeeze x1, local copies, waits for them, and re-layouts, local(): inverses = (lower_inv[step], upper_inv[step])  3.8 us
  transfers between devices with their start and end apart: 27, of which 7 were waited for; matrix products, arithmetic and copies ran while one was open for 8% of the time, Pallas kernels for 2%

profile of v3, /device:TPU:33, one launch (start us, length us, event | category | flops | bytes accessed | tf_op | source)
XLA Modules:
  0.0 176.1 jit_solution(4768363508446283218)
XLA Ops:
  0.0 1.3 fusion.6
  6.7 1.7 constant_dynamic-slice_fusion.42
  8.4 18.2 %conditional.2 = (f32[128,256]{1,0:T(8,128)}, f32[32,256]{1,0:T(8,128)S(1)}, f32[1,128,256]{2,1,0:T(8,128)S(1)}) conditional(s32[]{:T(128)} %clamp.7, (s32[]{:T(128)}, s32[]{:T(128)}, f32[512,256]{1,0:T(8,128)}, f32[256,256]{1,0:T(8,128)}, s32[]{:T(128)}) %tuple.49, (s32[]{:T(128)}, s32[]{:T(128)}, ...), branch_computations={%region_0.1_spmd, %region_1.2_spmd, %region_2.3_spmd, %region_3.4_... | conditional | flops 98334 | bytes 4915780 | solution.py:106
  12.2 6.8 %all-to-all-start = ((f32[16,16,256]{2,1,0:T(8,128)}), f32[16,16,256]{2,1,0:T(8,128)S(1)}, u32[]{:S(2)}, u32[]{:S(2)}) async-start(f32[16,16,256]{2,1,0:T(8,128)} %bitcast), calls=%async_computation | async-start | bytes 524288 | tf_op jit(solution)/shard_map/cond/branch_0_fun/all_to_all | solution.py:87
  20.6 5.9 %all-to-all-done = f32[16,16,256]{2,1,0:T(8,128)S(1)} async-done(((f32[16,16,256]{2,1,0:T(8,128)}), f32[16,16,256]{2,1,0:T(8,128)S(1)}, u32[]{:S(2)}, u32[]{:S(2)}) %all-to-all-start) | async-done | bytes 262176 | tf_op jit(solution)/shard_map/cond/branch_0_fun/all_to_all | solution.py:87
  29.4 4.2 %all-to-all-start.8 = ((f32[16,32,256]{2,1,0:T(8,128)}), f32[16,32,256]{2,1,0:T(8,128)}, u32[]{:S(2)}, u32[]{:S(2)}) async-start(f32[16,32,256]{2,1,0:T(8,128)} %tile.4), calls=%async_computation.8 | async-start | bytes 1048576 | tf_op jit(solution)/shard_map/all_to_all | solution.py:87
  37.9 3.8 %slice_bitcast_fusion = (f32[512,512]{1,0:T(8,128)S(1)}, f32[512,512]{1,0:T(8,128)S(1)}, f32[512,512]{1,0:T(8,128)}, f32[512,512]{1,0:T(8,128)S(1)}) fusion(f32[2,512,512]{2,1,0:T(8,128)} %param.19, f32[2,512,512]{2,1,0:T(8,128)} %param.18), kind=kLoop, calls=%fused_computation.50 | loop fusion | bytes 8388608 | tf_op jit(solution)/shard_map/squeeze | solution.py:154
  41.7 35.9 %collective-permute-done.35 = f32[256,256]{1,0:T(8,128)S(1)} collective-permute-done((f32[256,256]{1,0:T(8,128)S(1)}, f32[256,256]{1,0:T(8,128)S(1)}, u32[]{:S(2)}, u32[]{:S(2)}) %collective-permute-start.35) | collective-permute-done | bytes 262176 | tf_op jit(solution)/shard_map/ppermute | solution.py:81
  79.1 6.2 %collective-permute-start.37 = (f32[512,256]{1,0:T(8,128)}, f32[512,256]{1,0:T(8,128)}, u32[]{:S(2)}, u32[]{:S(2)}) collective-permute-start(f32[512,256]{1,0:T(8,128)} %fusion.1.mine_ref), channel_id=1, source_target_pairs={{0,1},{1,0},{2,3},{3,2},{4,5},{5,4},{6,7},{7,6},{8,9},{9,8},{10,11... | collective-permute-start | bytes 1572872 | tf_op jit(solution)/shard_map/ppermute | solution.py:156
  86.5 2.3 %early.2 = (f32[512,256]{1,0:T(8,128)S(1)}, f32[512,512]{1,0:T(8,128)S(1)}) custom-call(f32[512,256]{1,0:T(8,128)} %bitcast.39.gathered_ref, f32[512,256]{1,0:T(8,128)} %fusion.1.mine_ref, f32[512,512]{1,0:T(8,128)S(1)} %copy-done, f32[512,512]{1,0:T(8,128)S(1)} %get-tuple-element.208.upper_ref), custom_call_target="tpu_custom_call" | custom-call | flops 805306368 | bytes 3145728 | tf_op jit(solution)/shard_map/early/pallas_call | solution.py:157
  88.8 3.0 %late.2.block_ref = f32[512,256]{1,0:T(8,128)} custom-call(s32[8]{0:T(128)S(1)} %pad_add_fusion.flags, f32[512,256]{1,0:T(8,128)} %collective-permute-done.37.other_ref, f32[512,512]{1,0:T(8,128)S(1)} %get-tuple-element.209.part_ref, f32[512,256]{1,0:T(8,128)S(1)} %get-tuple-element.210.rows_ref, f32[512,512]{1,0:T(8,128)S(1)} %get-tuple-element.208.upper_ref, ...), custom_call_target="tpu_custom_call" | custom-call | flops 805306368 | bytes 3145728 | tf_op jit(solution)/shard_map/late/pallas_call | solution.py:170
  91.9 19.9 %conditional.3 = (f32[128,256]{1,0:T(8,128)}, f32[32,256]{1,0:T(8,128)S(1)}, f32[1,128,256]{2,1,0:T(8,128)S(1)}) conditional(s32[]{:T(128)} %clamp.6, (s32[]{:T(128)}, s32[]{:T(128)}, f32[512,256]{1,0:T(8,128)}, s32[]{:T(128)}, s32[]{:T(128)}) %tuple.51, (s32[]{:T(128)}, s32[]{:T(128)}, f32[512,256]{1,0:T(8,128)}, ...), branch_computations={%region_4.5_spmd, %region_5.6_spmd, %region_6.7_spmd, %region_7.8_... | conditional | flops 98337 | bytes 5440106 | solution.py:106
  95.0 1.7 constant_dynamic-slice_fusion.38
  96.6 6.6 %all-to-all-start.7 = ((f32[16,16,256]{2,1,0:T(8,128)}), f32[16,16,256]{2,1,0:T(8,128)S(1)}, u32[]{:S(2)}, u32[]{:S(2)}) async-start(f32[16,16,256]{2,1,0:T(8,128)} %bitcast.21), calls=%async_computation.7 | async-start | bytes 524288 | tf_op jit(solution)/shard_map/cond/branch_3_fun/all_to_all | solution.py:87
  103.3 1.6 select_select_fusion.7
  105.8 6.0 %all-to-all-done.7 = f32[16,16,256]{2,1,0:T(8,128)S(1)} async-done(((f32[16,16,256]{2,1,0:T(8,128)}), f32[16,16,256]{2,1,0:T(8,128)S(1)}, u32[]{:S(2)}, u32[]{:S(2)}) %all-to-all-start.7) | async-done | bytes 262176 | tf_op jit(solution)/shard_map/cond/branch_3_fun/all_to_all | solution.py:87
  114.0 1.5 collective-permute-start.41
  115.5 1.5 collective-permute-start.42
  121.1 3.6 %all-to-all-start.9 = ((f32[16,32,256]{2,1,0:T(8,128)}), f32[16,32,256]{2,1,0:T(8,128)S(1)}, u32[]{:S(2)}, u32[]{:S(2)}) async-start(f32[16,32,256]{2,1,0:T(8,128)} %tile.5), calls=%async_computation.9 | async-start | bytes 1048576 | tf_op jit(solution)/shard_map/all_to_all | solution.py:87
  124.7 37.3 %collective-permute-done.43 = f32[256,256]{1,0:T(8,128)} collective-permute-done((f32[256,256]{1,0:T(8,128)}, f32[256,256]{1,0:T(8,128)}, u32[]{:S(2)}, u32[]{:S(2)}) %collective-permute-start.43) | collective-permute-done | bytes 262176 | tf_op jit(solution)/shard_map/ppermute | solution.py:81
  162.0 1.3 collective-permute-done.44
  163.3 1.3 fusion.3.mine_ref
  164.6 6.8 %collective-permute-start.45 = (f32[512,256]{1,0:T(8,128)S(1)}, f32[512,256]{1,0:T(8,128)}, u32[]{:S(2)}, u32[]{:S(2)}) collective-permute-start(f32[512,256]{1,0:T(8,128)S(1)} %fusion.3.mine_ref), channel_id=1, source_target_pairs={{0,1},{1,0},{2,3},{3,2},{4,5},{5,4},{6,7},{7,6},{8,9},{9,8},{10,11... | collective-permute-start | bytes 1572872 | tf_op jit(solution)/shard_map/ppermute | solution.py:156
  173.1 3.0 %late.3 = f32[512,256]{1,0:T(8,128)} custom-call(s32[8]{0:T(128)S(1)} %pad_add_fusion.flags, f32[512,256]{1,0:T(8,128)} %collective-permute-done.45.other_ref, f32[512,512]{1,0:T(8,128)S(1)} %get-tuple-element.219.part_ref, f32[512,256]{1,0:T(8,128)S(1)} %get-tuple-element.220.rows_ref, f32[512,512]{1,0:T(8,128)S(1)} %get-tuple-element.218.upper_ref, ...), custom_call_target="tpu_custom_call" | custom-call | flops 805306368 | bytes 3145728 | tf_op jit(solution)/shard_map/late/pallas_call | solution.py:170
  (74 shorter events, 28.5 us)
Async XLA Ops:
  9.5 9.5 %collective-permute-start = (f32[128,256]{1,0:T(8,128)S(1)}, f32[128,256]{1,0:T(8,128)S(1)}, u32[]{:S(2)}, u32[]{:S(2)}) collective-permute-start(f32[128,256]{1,0:T(8,128)S(1)} %get-tuple-element.224), channel_id=1, source_target_pairs={{0,22},{1,23},{8,30},{9,31},{16,6},{17,7},{24,14},{25,15},{32,54},... | collective-permute-start | bytes 393224 | tf_op jit(solution)/shard_map/cond/branch_0_fun/ppermute | solution.py:81
  10.2 8.8 %collective-permute-start.1 = (f32[128,256]{1,0:T(8,128)S(1)}, f32[128,256]{1,0:T(8,128)S(1)}, u32[]{:S(2)}, u32[]{:S(2)}) collective-permute-start(f32[128,256]{1,0:T(8,128)S(1)} %get-tuple-element.223), channel_id=1, source_target_pairs={{0,30},{1,31},{8,6},{9,7},{16,14},{17,15},{24,22},{25,23},{32,62},... | collective-permute-start | bytes 393224 | tf_op jit(solution)/shard_map/cond/branch_0_fun/ppermute | solution.py:81
  10.8 8.2 %collective-permute-start.2 = (f32[128,256]{1,0:T(8,128)S(1)}, f32[128,256]{1,0:T(8,128)S(1)}, u32[]{:S(2)}, u32[]{:S(2)}) collective-permute-start(f32[128,256]{1,0:T(8,128)S(1)} %get-tuple-element.222), channel_id=1, source_target_pairs={{0,14},{1,15},{8,22},{9,23},{16,30},{17,31},{24,6},{25,7},{32,46},... | collective-permute-start | bytes 393224 | tf_op jit(solution)/shard_map/cond/branch_0_fun/ppermute | solution.py:81
  11.5 7.5 %collective-permute-start.3 = (f32[128,256]{1,0:T(8,128)S(1)}, f32[128,256]{1,0:T(8,128)S(1)}, u32[]{:S(2)}, u32[]{:S(2)}) collective-permute-start(f32[128,256]{1,0:T(8,128)S(1)} %get-tuple-element.221), channel_id=1, source_target_pairs={{0,6},{1,7},{8,14},{9,15},{16,22},{17,23},{24,30},{25,31},{32,38},... | collective-permute-start | bytes 393224 | tf_op jit(solution)/shard_map/cond/branch_0_fun/ppermute | solution.py:81
  12.2 14.3 %all-to-all-start = ((f32[16,16,256]{2,1,0:T(8,128)}), f32[16,16,256]{2,1,0:T(8,128)S(1)}, u32[]{:S(2)}, u32[]{:S(2)}) async-start(f32[16,16,256]{2,1,0:T(8,128)} %bitcast), calls=%async_computation | async-start | bytes 524288 | tf_op jit(solution)/shard_map/cond/branch_0_fun/all_to_all | solution.py:87
  26.5 7.2 %collective-permute-start.30 = (f32[128,256]{1,0:T(8,128)}, f32[128,256]{1,0:T(8,128)S(1)}, u32[]{:S(2)}, u32[]{:S(2)}) collective-permute-start(f32[128,256]{1,0:T(8,128)} %get-tuple-element.204), channel_id=1, source_target_pairs={{6,30},{7,31},{14,6},{15,7},{22,14},{23,15},{30,22},{31,23},{38,62... | collective-permute-start | bytes 393224 | tf_op jit(solution)/shard_map/ppermute | solution.py:81
  27.2 6.6 %collective-permute-start.31 = (f32[128,256]{1,0:T(8,128)}, f32[128,256]{1,0:T(8,128)S(1)}, u32[]{:S(2)}, u32[]{:S(2)}) collective-permute-start(f32[128,256]{1,0:T(8,128)} %get-tuple-element.204), channel_id=1, source_target_pairs={{6,22},{7,23},{14,30},{15,31},{22,6},{23,7},{30,14},{31,15},{38,54... | collective-permute-start | bytes 393224 | tf_op jit(solution)/shard_map/ppermute | solution.py:81
  27.9 5.9 %collective-permute-start.32 = (f32[128,256]{1,0:T(8,128)}, f32[128,256]{1,0:T(8,128)S(1)}, u32[]{:S(2)}, u32[]{:S(2)}) collective-permute-start(f32[128,256]{1,0:T(8,128)} %get-tuple-element.204), channel_id=1, source_target_pairs={{6,14},{7,15},{14,22},{15,23},{22,30},{23,31},{30,6},{31,7},{38,46... | collective-permute-start | bytes 393224 | tf_op jit(solution)/shard_map/ppermute | solution.py:81
  29.4 55.9 %all-to-all-start.8 = ((f32[16,32,256]{2,1,0:T(8,128)}), f32[16,32,256]{2,1,0:T(8,128)}, u32[]{:S(2)}, u32[]{:S(2)}) async-start(f32[16,32,256]{2,1,0:T(8,128)} %tile.4), calls=%async_computation.8 | async-start | bytes 1048576 | tf_op jit(solution)/shard_map/all_to_all | solution.py:87
  33.8 7.9 %collective-permute-start.33 = (f32[512,256]{1,0:T(8,128)S(1)}, f32[512,256]{1,0:T(8,128)S(1)}, u32[]{:S(2)}, u32[]{:S(2)}) collective-permute-start(f32[512,256]{1,0:T(8,128)S(1)} %bitcast.64), channel_id=1, source_target_pairs={{6,8},{7,9},{14,16},{15,17},{22,24},{23,25},{30,0},{31,1},{38,40},... | collective-permute-start | bytes 1572872 | tf_op jit(solution)/shard_map/ppermute | solution.py:81
  34.5 43.7 %collective-permute-start.34 = (f32[512,256]{1,0:T(8,128)S(1)}, f32[512,256]{1,0:T(8,128)S(1)}, u32[]{:S(2)}, u32[]{:S(2)}) collective-permute-start(f32[512,256]{1,0:T(8,128)S(1)} %bitcast.65), channel_id=1, source_target_pairs={{6,4},{7,5},{14,12},{15,13},{22,20},{23,21},{30,28},{31,29},{38,36... | collective-permute-start | bytes 1572872 | tf_op jit(solution)/shard_map/ppermute | solution.py:81
  35.3 42.4 %collective-permute-start.35 = (f32[256,256]{1,0:T(8,128)S(1)}, f32[256,256]{1,0:T(8,128)S(1)}, u32[]{:S(2)}, u32[]{:S(2)}) collective-permute-start(f32[256,256]{1,0:T(8,128)S(1)} %bitcast.76), channel_id=1, source_target_pairs={{6,10},{7,11},{14,18},{15,19},{22,26},{23,27},{30,2},{31,3},{38,42... | collective-permute-start | bytes 786440 | tf_op jit(solution)/shard_map/ppermute | solution.py:81
  36.6 41.6 %collective-permute-start.36 = (f32[256,256]{1,0:T(8,128)S(1)}, f32[256,256]{1,0:T(8,128)S(1)}, u32[]{:S(2)}, u32[]{:S(2)}) collective-permute-start(f32[256,256]{1,0:T(8,128)S(1)} %bitcast.75), channel_id=1, source_target_pairs={{6,2},{7,3},{14,10},{15,11},{22,18},{23,19},{30,26},{31,27},{38,34... | collective-permute-start | bytes 786440 | tf_op jit(solution)/shard_map/ppermute | solution.py:81
  79.1 9.7 %collective-permute-start.37 = (f32[512,256]{1,0:T(8,128)}, f32[512,256]{1,0:T(8,128)}, u32[]{:S(2)}, u32[]{:S(2)}) collective-permute-start(f32[512,256]{1,0:T(8,128)} %fusion.1.mine_ref), channel_id=1, source_target_pairs={{0,1},{1,0},{2,3},{3,2},{4,5},{5,4},{6,7},{7,6},{8,9},{9,8},{10,11... | collective-permute-start | bytes 1572872 | tf_op jit(solution)/shard_map/ppermute | solution.py:156
  92.9 10.3 %collective-permute-start.27 = (f32[128,256]{1,0:T(8,128)S(1)}, f32[128,256]{1,0:T(8,128)S(1)}, u32[]{:S(2)}, u32[]{:S(2)}) collective-permute-start(f32[128,256]{1,0:T(8,128)S(1)} %get-tuple-element.250), channel_id=1, source_target_pairs={{6,22},{7,23},{14,30},{15,31},{22,6},{23,7},{30,14},{31,15},{38,54... | collective-permute-start | bytes 393224 | tf_op jit(solution)/shard_map/cond/branch_3_fun/ppermute | solution.py:81
  93.6 9.7 %collective-permute-start.28 = (f32[128,256]{1,0:T(8,128)S(1)}, f32[128,256]{1,0:T(8,128)S(1)}, u32[]{:S(2)}, u32[]{:S(2)}) collective-permute-start(f32[128,256]{1,0:T(8,128)S(1)} %get-tuple-element.249), channel_id=1, source_target_pairs={{6,30},{7,31},{14,6},{15,7},{22,14},{23,15},{30,22},{31,23},{38,62... | collective-permute-start | bytes 393224 | tf_op jit(solution)/shard_map/cond/branch_3_fun/ppermute | solution.py:81
  94.3 9.0 %collective-permute-start.29 = (f32[128,256]{1,0:T(8,128)S(1)}, f32[128,256]{1,0:T(8,128)S(1)}, u32[]{:S(2)}, u32[]{:S(2)}) collective-permute-start(f32[128,256]{1,0:T(8,128)S(1)} %get-tuple-element.248), channel_id=1, source_target_pairs={{6,14},{7,15},{14,22},{15,23},{22,30},{23,31},{30,6},{31,7},{38,46... | collective-permute-start | bytes 393224 | tf_op jit(solution)/shard_map/cond/branch_3_fun/ppermute | solution.py:81
  96.6 15.1 %all-to-all-start.7 = ((f32[16,16,256]{2,1,0:T(8,128)}), f32[16,16,256]{2,1,0:T(8,128)S(1)}, u32[]{:S(2)}, u32[]{:S(2)}) async-start(f32[16,16,256]{2,1,0:T(8,128)} %bitcast.21), calls=%async_computation.7 | async-start | bytes 524288 | tf_op jit(solution)/shard_map/cond/branch_3_fun/all_to_all | solution.py:87
  114.0 10.7 %collective-permute-start.41 = (f32[512,256]{1,0:T(8,128)S(1)}, f32[512,256]{1,0:T(8,128)}, u32[]{:S(2)}, u32[]{:S(2)}) collective-permute-start(f32[512,256]{1,0:T(8,128)S(1)} %bitcast.62), channel_id=1, source_target_pairs={{6,8},{7,9},{14,16},{15,17},{22,24},{23,25},{30,0},{31,1},{38,40},... | collective-permute-start | bytes 1572872 | tf_op jit(solution)/shard_map/ppermute | solution.py:81
  115.5 47.8 %collective-permute-start.42 = (f32[512,256]{1,0:T(8,128)S(1)}, f32[512,256]{1,0:T(8,128)}, u32[]{:S(2)}, u32[]{:S(2)}) collective-permute-start(f32[512,256]{1,0:T(8,128)S(1)} %bitcast.63), channel_id=1, source_target_pairs={{6,4},{7,5},{14,12},{15,13},{22,20},{23,21},{30,28},{31,29},{38,36... | collective-permute-start | bytes 1572872 | tf_op jit(solution)/shard_map/ppermute | solution.py:81
  117.7 44.3 %collective-permute-start.43 = (f32[256,256]{1,0:T(8,128)}, f32[256,256]{1,0:T(8,128)}, u32[]{:S(2)}, u32[]{:S(2)}) collective-permute-start(f32[256,256]{1,0:T(8,128)} %bitcast.46), channel_id=1, source_target_pairs={{6,10},{7,11},{14,18},{15,19},{22,26},{23,27},{30,2},{31,3},{38,42... | collective-permute-start | bytes 786440 | tf_op jit(solution)/shard_map/ppermute | solution.py:81
  118.9 44.3 %collective-permute-start.44 = (f32[256,256]{1,0:T(8,128)S(1)}, f32[256,256]{1,0:T(8,128)}, u32[]{:S(2)}, u32[]{:S(2)}) collective-permute-start(f32[256,256]{1,0:T(8,128)S(1)} %bitcast.74), channel_id=1, source_target_pairs={{6,2},{7,3},{14,10},{15,11},{22,18},{23,19},{30,26},{31,27},{38,34... | collective-permute-start | bytes 786440 | tf_op jit(solution)/shard_map/ppermute | solution.py:81
  121.1 50.4 %all-to-all-start.9 = ((f32[16,32,256]{2,1,0:T(8,128)}), f32[16,32,256]{2,1,0:T(8,128)S(1)}, u32[]{:S(2)}, u32[]{:S(2)}) async-start(f32[16,32,256]{2,1,0:T(8,128)} %tile.5), calls=%async_computation.9 | async-start | bytes 1048576 | tf_op jit(solution)/shard_map/all_to_all | solution.py:87
  164.6 8.5 %collective-permute-start.45 = (f32[512,256]{1,0:T(8,128)S(1)}, f32[512,256]{1,0:T(8,128)}, u32[]{:S(2)}, u32[]{:S(2)}) collective-permute-start(f32[512,256]{1,0:T(8,128)S(1)} %fusion.3.mine_ref), channel_id=1, source_target_pairs={{0,1},{1,0},{2,3},{3,2},{4,5},{5,4},{6,7},{7,6},{8,9},{9,8},{10,11... | collective-permute-start | bytes 1572872 | tf_op jit(solution)/shard_map/ppermute | solution.py:156
  (7 other events, 58.9 us)

commit v4 on v3

--- a/solution.py
+++ b/solution.py
@@ -7,7 +7,7 @@
 from jax.experimental.pallas import tpu as pltpu
 from jax.sharding import PartitionSpec as P
 
-VMEM_BYTES = 40 * 1024 * 1024
+VMEM_BYTES = 20 * 1024 * 1024
 
 
 def split(value):
@@ -86,46 +86,40 @@
     def exchange(value):
         return lax.all_to_all(value, "row", 0, 0, tiled=True)
 
-    def to_leaders(place):
-        hops = [hop if hop >= -7 else 8 for hop in (3 - place, 7 - place, -1 - place, -5 - place)]
-
-        def run(block, chunk_at, own, dist, plane):
-            quarter = None
-            for n, hop in enumerate(hops):
-                at = (((plane >> 2) + (0, 1, 3, 2)[n]) & 3) * part_rows
-                part = lax.dynamic_slice_in_dim(block, at, part_rows, 0)
-                got = part if hop == 0 else from_class(part, place, 4, hop)
-                quarter = got if n == 0 else jnp.where(dist == hop % n_z, got, quarter)
+    def to_leaders(sends):
+        def run(block, chunk_at, own_at, dist):
+            got = [from_class(block, place, spacing, hop) for place, spacing, hop in sends]
+            own = lax.dynamic_slice_in_dim(block, own_at, size, 0)
             chunk = lax.dynamic_slice_in_dim(exchange(own), chunk_at, 2 * piece, 0)
-            return quarter, chunk
+            tiled, middle = lax.optimization_barrier((jnp.tile(chunk, (n_row, 1)), block))
+            for (_, _, hop), value in zip(sends, got):
+                middle = jnp.where(dist == hop % n_z, value, middle)
+            return middle, middle[:size], middle[size:], tiled
 
         return run
 
-    def fetch(block, inverses, which, chunk_at, own_at, dist, plane):
-        own = lax.dynamic_slice_in_dim(block, own_at, size, 0)
-        quarter, chunk = lax.switch(which, leads, block, chunk_at, own, dist, plane)
-        around = [quarter] + [from_class(quarter, 3, 4, hop) for hop in (-4, 8, 4)]
-        middle = jnp.zeros((4,) + quarter.shape, quarter.dtype)
-        for n in range(4):
-            middle = lax.dynamic_update_index_in_dim(
-                middle, around[n], ((my_z >> 2) + n) & 3, 0
-            )
-        middle = middle.reshape(block.shape)
+    def fetch(block, later, which, chunk_at, own_at, dist):
+        middle, upper_half, lower_half, tiled = lax.switch(which, leads, block, chunk_at, own_at, dist)
         up = from_class(middle, 3, 4, 1)
         down = from_class(middle, 3, 4, -1)
-        top = from_class(middle[:size], 3, 4, 2)
-        bottom = from_class(middle[size:], 3, 4, -2)
-        gathered = exchange(jnp.tile(chunk, (n_row, 1)))
+        top = from_class(upper_half, 3, 4, 2)
+        bottom = from_class(lower_half, 3, 4, -2)
+        gathered = exchange(tiled)
         near = my_z & 3
-        up, inverses = lax.optimization_barrier((up, inverses))
+        up, later = lax.optimization_barrier((up, later))
         both = jnp.concatenate([top, bottom], axis=0)
         columns = jnp.where(
             near == 3, middle, jnp.where(near == 0, up, jnp.where(near == 2, down, both))
         )
-        return columns, gathered, inverses
+        return columns, gathered, later
 
-    part_rows = matrix.shape[0] // 4
-    leads = [to_leaders(place) for place in range(4)]
+    leads = []
+    for place in (0, 1, 2, 4, 5, 6):
+        hops = [hop - place % 4 for hop in (7, -5, 3, -1)]
+        hops.sort(key=abs, reverse=True)
+        leads.append(to_leaders([(place, 8 if abs(hop) > 3 else 4, hop) for hop in hops]))
+    for place in range(3, n_z, 4):
+        leads.append(to_leaders([(place, n_z, hop) for hop in (8, 4, -4)]))
     whole = pl.BlockSpec(memory_space=pltpu.VMEM)
     scalars = pl.BlockSpec(memory_space=pltpu.SMEM)
     params = pltpu.CompilerParams(vmem_limit_bytes=VMEM_BYTES)
@@ -141,18 +135,19 @@
         plane = first >> 1
         dist = (my_z - plane) & (n_z - 1)
         places += [
-            plane & 3,
+            jnp.where(plane & 3 == 3, 6 + (plane >> 2), (plane & 3) + 3 * ((plane & 7) >> 2)),
             (first & (n_row - 1)) * piece,
             (first >> (n_row.bit_length() - 1)) * size,
             dist,
-            plane,
         ]
-    flags, places = lax.optimization_barrier((flags, places))
+    places = lax.optimization_barrier(places)
 
     block = matrix
     for step in range(panel_index.shape[0]):
-        inverses = lower_inv[step], upper_inv[step]
-        mine, gathered, (lower, upper) = fetch(block, inverses, *places[5 * step : 5 * step + 5])
+        later = lower_inv[step], upper_inv[step], flags
+        mine, gathered, (lower, upper, flags) = fetch(
+            block, later, *places[4 * step : 4 * step + 4]
+        )
         other = lax.ppermute(mine, "col", [(i, i ^ 1) for i in range(n_col)])
         rows, part = pl.pallas_call(
             functools.partial(early_kernel, n_row),

time: 178 us -> 144 us (0.81)
  the two profiles are of different devices: /device:TPU:33 before, /device:TPU:35 now
where the time goes in v4:
time: 144 us; the launch traced here: 143 us
  waiting for transfers between devices  54.4 us (38%)
  starting transfers between devices  48.8 us (34%)
  local copies, waits for them, and re-layouts  19.7 us (14%)
  Pallas kernels  9.46 us (7%)
  other arithmetic  6.18 us (4%)
  between operations  4.2 us (3%)
    ppermute x15, waiting for transfers between devices, send_z(): return lax.ppermute(value, 'col', pairs)  39.9 us
    all_to_all x4, starting transfers between devices, exchange(): return lax.all_to_all(value, 'row', 0, 0, tiled=True)  23.5 us
    ppermute x15, starting transfers between devices, send_z(): return lax.ppermute(value, 'col', pairs)  17.6 us
    all_to_all x4, waiting for transfers between devices, exchange(): return lax.all_to_all(value, 'row', 0, 0, tiled=True)  13.9 us
    ppermute x2, starting transfers between devices, local(): other = lax.ppermute(mine, 'col', [(i, i ^ 1) for i in range(n_col)])  7.62 us
    pallas_call x2, Pallas kernels, local(): pl.pallas_call(functools.partial(late_kernel, n_row, step), out_shape=jax...  6.14 us
    cond x6, local copies, waits for them, and re-layouts  5.85 us
    squeeze x1, local copies, waits for them, and re-layouts, local(): later = (lower_inv[step], upper_inv[step], flags)  3.63 us
  transfers between devices with their start and end apart: 21, of which 5 were waited for; matrix products, arithmetic and copies ran while one was open for 12% of the time, Pallas kernels for 2%

profile of v4, /device:TPU:35, one launch (start us, length us, event | category | flops | bytes accessed | tf_op | source)
XLA Modules:
  0.0 142.8 jit_solution(6623453103045163379)
XLA Ops:
  5.4 24.0 %conditional.2 = (f32[512,256]{1,0:T(8,128)}, f32[512,256]{1,0:T(8,128)}, f32[512,256]{1,0:T(8,128)}, f32[512,256]{1,0:T(8,128)}, f32[512,256]{1,0:T(8,128)}, /*index=5*/f32[512,256]{1,0:T(8,128)}) conditional(s32[]{:T(128)} %clamp.7, (s32[]{:T(128)}, f32[512,256]{1,0:T(8,128)}, s32[]{:T(128)}, s32[]{:T(128)}) %tuple.131, ...), branch_computations={%region_0.1_spmd, %region_1.2_spmd, %region_2.3_spmd, %region_3.4_... | conditional | flops 524298 | bytes 17662336 | solution.py:102
  8.3 1.7 %constant_dynamic-slice_fusion.1 = f32[256,256]{1,0:T(8,128)} fusion(f32[512,256]{1,0:T(8,128)} %get-tuple-element.358, s32[]{:T(128)S(6)} %select_n.400), kind=kLoop, calls=%fused_computation.2 | loop fusion | bytes 524292 | tf_op jit(solution)/shard_map/cond/branch_0_fun/dynamic_slice | solution.py:92
  10.0 6.9 %all-to-all-start = ((f32[16,16,256]{2,1,0:T(8,128)}), f32[16,16,256]{2,1,0:T(8,128)S(1)}, u32[]{:S(2)}, u32[]{:S(2)}) async-start(f32[16,16,256]{2,1,0:T(8,128)} %bitcast), calls=%async_computation | async-start | bytes 524288 | tf_op jit(solution)/shard_map/cond/branch_0_fun/all_to_all | solution.py:87
  16.9 6.8 %all-to-all-done = f32[16,16,256]{2,1,0:T(8,128)S(1)} async-done(((f32[16,16,256]{2,1,0:T(8,128)}), f32[16,16,256]{2,1,0:T(8,128)S(1)}, u32[]{:S(2)}, u32[]{:S(2)}) %all-to-all-start) | async-done | bytes 262176 | tf_op jit(solution)/shard_map/cond/branch_0_fun/all_to_all | solution.py:87
  24.6 1.9 %copy.10 = f32[512,256]{1,0:T(8,128)} copy(f32[512,256]{1,0:T(8,128)} %bitcast.2) | data formatting | bytes 1048576 | tf_op jit(solution)/shard_map/cond
  27.4 1.9 %copy.8 = f32[512,256]{1,0:T(8,128)} copy(f32[512,256]{1,0:T(8,128)} %select_select_fusion) | data formatting | bytes 1048576 | tf_op jit(solution)/shard_map/cond
  29.3 1.6 %collective-permute-start.73 = (f32[512,256]{1,0:T(8,128)}, f32[512,256]{1,0:T(8,128)}, u32[]{:S(2)}, u32[]{:S(2)}) collective-permute-start(f32[512,256]{1,0:T(8,128)} %get-tuple-element.323), channel_id=1, source_target_pairs={{6,4},{7,5},{14,12},{15,13},{22,20},{23,21},{30,28},{31,29},{38,36... | collective-permute-start | bytes 1572872 | tf_op jit(solution)/shard_map/ppermute | solution.py:81
  32.4 4.9 %all-to-all-start.20 = ((f32[16,32,256]{2,1,0:T(8,128)}), f32[16,32,256]{2,1,0:T(8,128)}, u32[]{:S(2)}, u32[]{:S(2)}) async-start(f32[16,32,256]{2,1,0:T(8,128)} %bitcast.69), calls=%async_computation.20 | async-start | bytes 1048576 | tf_op jit(solution)/shard_map/all_to_all | solution.py:87
  37.2 1.8 %fusion.5 = (f32[256,256]{1,0:T(8,128)}, f32[256,256]{1,0:T(8,128)S(1)}) fusion(f32[512,256]{1,0:T(8,128)} %get-tuple-element.323), kind=kLoop, calls=%fused_computation.72 | loop fusion | bytes 1048576 | tf_op jit(solution)/shard_map/cond/branch_0_fun/slice | solution.py:97
  41.8 3.6 %slice_bitcast_fusion = (f32[512,512]{1,0:T(8,128)S(1)}, f32[512,512]{1,0:T(8,128)S(1)}, f32[512,512]{1,0:T(8,128)}, f32[512,512]{1,0:T(8,128)S(1)}) fusion(f32[2,512,512]{2,1,0:T(8,128)} %param.31, f32[2,512,512]{2,1,0:T(8,128)} %param.30), kind=kLoop, calls=%fused_computation.60 | loop fusion | bytes 8388608 | tf_op jit(solution)/shard_map/squeeze | solution.py:147
  45.4 22.8 %collective-permute-done.74 = f32[256,256]{1,0:T(8,128)} collective-permute-done((f32[256,256]{1,0:T(8,128)}, f32[256,256]{1,0:T(8,128)}, u32[]{:S(2)}, u32[]{:S(2)}) %collective-permute-start.74) | collective-permute-done | bytes 262176 | tf_op jit(solution)/shard_map/ppermute | solution.py:81
  68.2 2.0 %fusion.1.mine_ref = f32[512,256]{1,0:T(8,128)} fusion(f32[512,256]{1,0:T(8,128)} %get-tuple-element.323, f32[512,256]{1,0:T(8,128)} %collective-permute-done.72, f32[512,256]{1,0:T(8,128)} %collective-permute-done.73, f32[256,256]{1,0:T(8,128)} %collective-permute-done.75, f32[256,256]{1,0:T(8,128)} %collective-permute-done.74, pred[]{:T(512)S(6)} %eq.238, ...), kind=kLoop, calls=%fused_computation.66 | loop fusion | flops 524288 | bytes 2621443 | tf_op jit(solution)/shard_map/jit(_where)/select_n | solution.py:111
  70.2 4.3 %collective-permute-start.76 = (f32[512,256]{1,0:T(8,128)}, f32[512,256]{1,0:T(8,128)}, u32[]{:S(2)}, u32[]{:S(2)}) collective-permute-start(f32[512,256]{1,0:T(8,128)} %fusion.1.mine_ref), channel_id=1, source_target_pairs={{0,1},{1,0},{2,3},{3,2},{4,5},{5,4},{6,7},{7,6},{8,9},{9,8},{10,11... | collective-permute-start | bytes 1572872 | tf_op jit(solution)/shard_map/ppermute | solution.py:151
  75.8 2.3 %early.2 = (f32[512,256]{1,0:T(8,128)S(1)}, f32[512,512]{1,0:T(8,128)S(1)}) custom-call(f32[512,256]{1,0:T(8,128)} %bitcast.70.gathered_ref, f32[512,256]{1,0:T(8,128)} %fusion.1.mine_ref, f32[512,512]{1,0:T(8,128)S(1)} %copy-done, f32[512,512]{1,0:T(8,128)S(1)} %get-tuple-element.328.upper_ref), custom_call_target="tpu_custom_call" | custom-call | flops 805306368 | bytes 3145728 | tf_op jit(solution)/shard_map/early/pallas_call | solution.py:152
  78.1 3.0 %late.2.block_ref = f32[512,256]{1,0:T(8,128)} custom-call(s32[8]{0:T(128)S(1)} %pad_add_fusion.flags, f32[512,256]{1,0:T(8,128)} %collective-permute-done.76.other_ref, f32[512,512]{1,0:T(8,128)S(1)} %get-tuple-element.329.part_ref, f32[512,256]{1,0:T(8,128)S(1)} %get-tuple-element.330.rows_ref, f32[512,512]{1,0:T(8,128)S(1)} %get-tuple-element.328.upper_ref, ...), custom_call_target="tpu_custom_call" | custom-call | flops 805306368 | bytes 3145728 | tf_op jit(solution)/shard_map/late/pallas_call | solution.py:165
  81.1 24.3 %conditional.3 = (f32[512,256]{1,0:T(8,128)}, f32[512,256]{1,0:T(8,128)S(1)}, f32[512,256]{1,0:T(8,128)}, f32[512,256]{1,0:T(8,128)}, f32[512,256]{1,0:T(8,128)S(1)}, /*index=5*/f32[512,256]{1,0:T(8,128)}) conditional(s32[]{:T(128)} %clamp.6, (s32[]{:T(128)}, f32[512,256]{1,0:T(8,128)}, s32[]{:T(128)}, ...), branch_computations={%region_10.11_spmd, %region_11.12_spmd, %region_12.13_spmd, %regio... | conditional | flops 524298 | bytes 15565156 | solution.py:102
  84.7 1.7 %constant_dynamic-slice_fusion.39 = f32[256,256]{1,0:T(8,128)} fusion(f32[512,256]{1,0:T(8,128)} %get-tuple-element.472, s32[]{:T(128)S(6)} %select_n.575), kind=kLoop, calls=%fused_computation.59 | loop fusion | bytes 524292 | tf_op jit(solution)/shard_map/cond/branch_9_fun/dynamic_slice | solution.py:92
  86.4 6.9 %all-to-all-start.19 = ((f32[16,16,256]{2,1,0:T(8,128)}), f32[16,16,256]{2,1,0:T(8,128)S(1)}, u32[]{:S(2)}, u32[]{:S(2)}) async-start(f32[16,16,256]{2,1,0:T(8,128)} %bitcast.57), calls=%async_computation.19 | async-start | bytes 524288 | tf_op jit(solution)/shard_map/cond/branch_9_fun/all_to_all | solution.py:87
  93.3 7.2 %all-to-all-done.19 = f32[16,16,256]{2,1,0:T(8,128)S(1)} async-done(((f32[16,16,256]{2,1,0:T(8,128)}), f32[16,16,256]{2,1,0:T(8,128)S(1)}, u32[]{:S(2)}, u32[]{:S(2)}) %all-to-all-start.19) | async-done | bytes 262176 | tf_op jit(solution)/shard_map/cond/branch_9_fun/all_to_all | solution.py:87
  102.4 2.0 %select_select_fusion.19 = f32[512,256]{1,0:T(8,128)} fusion(f32[512,256]{1,0:T(8,128)} %collective-permute-done.69, f32[512,256]{1,0:T(8,128)} %collective-permute-done.70, f32[512,256]{1,0:T(8,128)S(1)} %collective-permute-done.71, f32[512,256]{1,0:T(8,128)} %get-tuple-element.472, pred[]{:T(512)S(6)} %eq.228, pred[]{:T(512)S(6)} %eq.227, pred[]{:T(512)S(6)} %eq.226), kind=kLoop, calls=%fused_computation.57 | loop fusion | flops 393216 | bytes 2621443 | tf_op jit(solution)/shard_map/cond/branch_9_fun/jit(_where)/select_n | solution.py:96
  111.6 4.8 %all-to-all-start.21 = ((f32[16,32,256]{2,1,0:T(8,128)}), f32[16,32,256]{2,1,0:T(8,128)S(1)}, u32[]{:S(2)}, u32[]{:S(2)}) async-start(f32[16,32,256]{2,1,0:T(8,128)} %bitcast.80), calls=%async_computation.21 | async-start | bytes 1048576 | tf_op jit(solution)/shard_map/all_to_all | solution.py:87
  116.5 17.0 %collective-permute-done.79 = f32[256,256]{1,0:T(8,128)} collective-permute-done((f32[256,256]{1,0:T(8,128)}, f32[256,256]{1,0:T(8,128)}, u32[]{:S(2)}, u32[]{:S(2)}) %collective-permute-start.79) | collective-permute-done | bytes 262176 | tf_op jit(solution)/shard_map/ppermute | solution.py:81
  134.7 3.3 %collective-permute-start.81 = (f32[512,256]{1,0:T(8,128)S(1)}, f32[512,256]{1,0:T(8,128)}, u32[]{:S(2)}, u32[]{:S(2)}) collective-permute-start(f32[512,256]{1,0:T(8,128)S(1)} %fusion.3.mine_ref), channel_id=1, source_target_pairs={{0,1},{1,0},{2,3},{3,2},{4,5},{5,4},{6,7},{7,6},{8,9},{9,8},{10,11... | collective-permute-start | bytes 1572872 | tf_op jit(solution)/shard_map/ppermute | solution.py:151
  139.7 3.1 %late.3 = f32[512,256]{1,0:T(8,128)} custom-call(s32[8]{0:T(128)S(1)} %pad_add_fusion.flags, f32[512,256]{1,0:T(8,128)} %collective-permute-done.81.other_ref, f32[512,512]{1,0:T(8,128)S(1)} %get-tuple-element.339.part_ref, f32[512,256]{1,0:T(8,128)S(1)} %get-tuple-element.340.rows_ref, f32[512,512]{1,0:T(8,128)S(1)} %get-tuple-element.338.upper_ref, ...), custom_call_target="tpu_custom_call" | custom-call | flops 805306368 | bytes 3145728 | tf_op jit(solution)/shard_map/late/pallas_call | solution.py:165
  (60 shorter events, 27.1 us)
Async XLA Ops:
  5.4 21.1 %copy-start.1 = (f32[512,256]{1,0:T(8,128)S(1)}, f32[512,256]{1,0:T(8,128)}, u32[]{:S(2)}) copy-start(f32[512,256]{1,0:T(8,128)} %get-tuple-element.358) | copy-start | bytes 1572868 | tf_op jit(solution)/shard_map/cond
  5.4 21.0 %collective-permute-start.3 = (f32[512,256]{1,0:T(8,128)}, f32[512,256]{1,0:T(8,128)S(1)}, u32[]{:S(2)}, u32[]{:S(2)}) collective-permute-start(f32[512,256]{1,0:T(8,128)} %get-tuple-element.358), channel_id=1, source_target_pairs={{0,14},{1,15},{16,30},{17,31},{32,46},{33,47},{48,62},{49,63},{64,... | collective-permute-start | bytes 1572872 | tf_op jit(solution)/shard_map/cond/branch_0_fun/ppermute | solution.py:81
  6.2 20.2 %collective-permute-start.2 = (f32[512,256]{1,0:T(8,128)}, f32[512,256]{1,0:T(8,128)S(1)}, u32[]{:S(2)}, u32[]{:S(2)}) collective-permute-start(f32[512,256]{1,0:T(8,128)} %get-tuple-element.358), channel_id=1, source_target_pairs={{0,22},{1,23},{16,6},{17,7},{32,54},{33,55},{48,38},{49,39},{64,86... | collective-permute-start | bytes 1572872 | tf_op jit(solution)/shard_map/cond/branch_0_fun/ppermute | solution.py:81
  6.9 19.5 %collective-permute-start.1 = (f32[512,256]{1,0:T(8,128)}, f32[512,256]{1,0:T(8,128)S(1)}, u32[]{:S(2)}, u32[]{:S(2)}) collective-permute-start(f32[512,256]{1,0:T(8,128)} %get-tuple-element.358), channel_id=1, source_target_pairs={{0,6},{1,7},{8,14},{9,15},{16,22},{17,23},{24,30},{25,31},{32,38},... | collective-permute-start | bytes 1572872 | tf_op jit(solution)/shard_map/cond/branch_0_fun/ppermute | solution.py:81
  7.6 18.8 %collective-permute-start = (f32[512,256]{1,0:T(8,128)}, f32[512,256]{1,0:T(8,128)S(1)}, u32[]{:S(2)}, u32[]{:S(2)}) collective-permute-start(f32[512,256]{1,0:T(8,128)} %get-tuple-element.358), channel_id=1, source_target_pairs={{0,30},{1,31},{8,6},{9,7},{16,14},{17,15},{24,22},{25,23},{32,62},... | collective-permute-start | bytes 1572872 | tf_op jit(solution)/shard_map/cond/branch_0_fun/ppermute | solution.py:81
  10.0 13.7 %all-to-all-start = ((f32[16,16,256]{2,1,0:T(8,128)}), f32[16,16,256]{2,1,0:T(8,128)S(1)}, u32[]{:S(2)}, u32[]{:S(2)}) async-start(f32[16,16,256]{2,1,0:T(8,128)} %bitcast), calls=%async_computation | async-start | bytes 524288 | tf_op jit(solution)/shard_map/cond/branch_0_fun/all_to_all | solution.py:87
  29.3 12.4 %copy-start.15 = (s32[2,1]{0,1:T(1,128)S(1)}, s32[2,1]{0,1:T(1,128)}, u32[]{:S(2)}) copy-start(s32[2,1]{0,1:T(1,128)} %param.28) | copy-start | bytes 28
  29.3 38.9 %collective-permute-start.73 = (f32[512,256]{1,0:T(8,128)}, f32[512,256]{1,0:T(8,128)}, u32[]{:S(2)}, u32[]{:S(2)}) collective-permute-start(f32[512,256]{1,0:T(8,128)} %get-tuple-element.323), channel_id=1, source_target_pairs={{6,4},{7,5},{14,12},{15,13},{22,20},{23,21},{30,28},{31,29},{38,36... | collective-permute-start | bytes 1572872 | tf_op jit(solution)/shard_map/ppermute | solution.py:81
  30.9 14.5 %collective-permute-start.72 = (f32[512,256]{1,0:T(8,128)}, f32[512,256]{1,0:T(8,128)}, u32[]{:S(2)}, u32[]{:S(2)}) collective-permute-start(f32[512,256]{1,0:T(8,128)} %get-tuple-element.323), channel_id=1, source_target_pairs={{6,8},{7,9},{14,16},{15,17},{22,24},{23,25},{30,0},{31,1},{38,40},... | collective-permute-start | bytes 1572872 | tf_op jit(solution)/shard_map/ppermute | solution.py:81
  32.4 42.2 %all-to-all-start.20 = ((f32[16,32,256]{2,1,0:T(8,128)}), f32[16,32,256]{2,1,0:T(8,128)}, u32[]{:S(2)}, u32[]{:S(2)}) async-start(f32[16,32,256]{2,1,0:T(8,128)} %bitcast.69), calls=%async_computation.20 | async-start | bytes 1048576 | tf_op jit(solution)/shard_map/all_to_all | solution.py:87
  39.0 29.2 %collective-permute-start.74 = (f32[256,256]{1,0:T(8,128)}, f32[256,256]{1,0:T(8,128)}, u32[]{:S(2)}, u32[]{:S(2)}) collective-permute-start(f32[256,256]{1,0:T(8,128)} %get-tuple-element.347), channel_id=1, source_target_pairs={{6,10},{7,11},{14,18},{15,19},{22,26},{23,27},{30,2},{31,3},{38,42... | collective-permute-start | bytes 786440 | tf_op jit(solution)/shard_map/ppermute | solution.py:81
  40.3 27.9 %collective-permute-start.75 = (f32[256,256]{1,0:T(8,128)S(1)}, f32[256,256]{1,0:T(8,128)}, u32[]{:S(2)}, u32[]{:S(2)}) collective-permute-start(f32[256,256]{1,0:T(8,128)S(1)} %get-tuple-element.348), channel_id=1, source_target_pairs={{6,2},{7,3},{14,10},{15,11},{22,18},{23,19},{30,26},{31,27},{38,34... | collective-permute-start | bytes 786440 | tf_op jit(solution)/shard_map/ppermute | solution.py:81
  70.2 7.9 %collective-permute-start.76 = (f32[512,256]{1,0:T(8,128)}, f32[512,256]{1,0:T(8,128)}, u32[]{:S(2)}, u32[]{:S(2)}) collective-permute-start(f32[512,256]{1,0:T(8,128)} %fusion.1.mine_ref), channel_id=1, source_target_pairs={{0,1},{1,0},{2,3},{3,2},{4,5},{5,4},{6,7},{7,6},{8,9},{9,8},{10,11... | collective-permute-start | bytes 1572872 | tf_op jit(solution)/shard_map/ppermute | solution.py:151
  81.1 21.3 %collective-permute-start.71 = (f32[512,256]{1,0:T(8,128)}, f32[512,256]{1,0:T(8,128)S(1)}, u32[]{:S(2)}, u32[]{:S(2)}) collective-permute-start(f32[512,256]{1,0:T(8,128)} %get-tuple-element.472), channel_id=1, source_target_pairs={{30,14},{31,15},{62,46},{63,47},{94,78},{95,79},{126,110},{127,111... | collective-permute-start | bytes 1572872 | tf_op jit(solution)/shard_map/cond/branch_9_fun/ppermute | solution.py:81
  81.8 20.6 %collective-permute-start.70 = (f32[512,256]{1,0:T(8,128)}, f32[512,256]{1,0:T(8,128)}, u32[]{:S(2)}, u32[]{:S(2)}) collective-permute-start(f32[512,256]{1,0:T(8,128)} %get-tuple-element.472), channel_id=1, source_target_pairs={{30,6},{31,7},{62,38},{63,39},{94,70},{95,71},{126,102},{127,103},... | collective-permute-start | bytes 1572872 | tf_op jit(solution)/shard_map/cond/branch_9_fun/ppermute | solution.py:81
  83.3 19.1 %collective-permute-start.69 = (f32[512,256]{1,0:T(8,128)}, f32[512,256]{1,0:T(8,128)}, u32[]{:S(2)}, u32[]{:S(2)}) collective-permute-start(f32[512,256]{1,0:T(8,128)} %get-tuple-element.472), channel_id=1, source_target_pairs={{30,22},{31,23},{62,54},{63,55},{94,86},{95,87},{126,118},{127,119... | collective-permute-start | bytes 1572872 | tf_op jit(solution)/shard_map/cond/branch_9_fun/ppermute | solution.py:81
  86.4 14.1 %all-to-all-start.19 = ((f32[16,16,256]{2,1,0:T(8,128)}), f32[16,16,256]{2,1,0:T(8,128)S(1)}, u32[]{:S(2)}, u32[]{:S(2)}) async-start(f32[16,16,256]{2,1,0:T(8,128)} %bitcast.57), calls=%async_computation.19 | async-start | bytes 524288 | tf_op jit(solution)/shard_map/cond/branch_9_fun/all_to_all | solution.py:87
  105.4 28.1 %copy-start.12 = (f32[512,256]{1,0:T(8,128)}, f32[512,256]{1,0:T(8,128)S(1)}, u32[]{:S(2)}) copy-start(f32[512,256]{1,0:T(8,128)S(1)} %get-tuple-element.333) | copy-start | bytes 1572868
  105.4 11.1 %collective-permute-start.77 = (f32[512,256]{1,0:T(8,128)S(1)}, f32[512,256]{1,0:T(8,128)}, u32[]{:S(2)}, u32[]{:S(2)}) collective-permute-start(f32[512,256]{1,0:T(8,128)S(1)} %get-tuple-element.333), channel_id=1, source_target_pairs={{6,8},{7,9},{14,16},{15,17},{22,24},{23,25},{30,0},{31,1},{38,40},... | collective-permute-start | bytes 1572872 | tf_op jit(solution)/shard_map/ppermute | solution.py:81
  106.9 26.7 %collective-permute-start.78 = (f32[512,256]{1,0:T(8,128)S(1)}, f32[512,256]{1,0:T(8,128)}, u32[]{:S(2)}, u32[]{:S(2)}) collective-permute-start(f32[512,256]{1,0:T(8,128)S(1)} %get-tuple-element.333), channel_id=1, source_target_pairs={{6,4},{7,5},{14,12},{15,13},{22,20},{23,21},{30,28},{31,29},{38,36... | collective-permute-start | bytes 1572872 | tf_op jit(solution)/shard_map/ppermute | solution.py:81
  109.0 24.5 %collective-permute-start.79 = (f32[256,256]{1,0:T(8,128)}, f32[256,256]{1,0:T(8,128)}, u32[]{:S(2)}, u32[]{:S(2)}) collective-permute-start(f32[256,256]{1,0:T(8,128)} %get-tuple-element.345), channel_id=1, source_target_pairs={{6,10},{7,11},{14,18},{15,19},{22,26},{23,27},{30,2},{31,3},{38,42... | collective-permute-start | bytes 786440 | tf_op jit(solution)/shard_map/ppermute | solution.py:81
  110.3 23.2 %collective-permute-start.80 = (f32[256,256]{1,0:T(8,128)S(1)}, f32[256,256]{1,0:T(8,128)}, u32[]{:S(2)}, u32[]{:S(2)}) collective-permute-start(f32[256,256]{1,0:T(8,128)S(1)} %get-tuple-element.346), channel_id=1, source_target_pairs={{6,2},{7,3},{14,10},{15,11},{22,18},{23,19},{30,26},{31,27},{38,34... | collective-permute-start | bytes 786440 | tf_op jit(solution)/shard_map/ppermute | solution.py:81
  111.6 26.4 %all-to-all-start.21 = ((f32[16,32,256]{2,1,0:T(8,128)}), f32[16,32,256]{2,1,0:T(8,128)S(1)}, u32[]{:S(2)}, u32[]{:S(2)}) async-start(f32[16,32,256]{2,1,0:T(8,128)} %bitcast.80), calls=%async_computation.21 | async-start | bytes 1048576 | tf_op jit(solution)/shard_map/all_to_all | solution.py:87
  134.7 4.9 %collective-permute-start.81 = (f32[512,256]{1,0:T(8,128)S(1)}, f32[512,256]{1,0:T(8,128)}, u32[]{:S(2)}, u32[]{:S(2)}) collective-permute-start(f32[512,256]{1,0:T(8,128)S(1)} %fusion.3.mine_ref), channel_id=1, source_target_pairs={{0,1},{1,0},{2,3},{3,2},{4,5},{5,4},{6,7},{7,6},{8,9},{9,8},{10,11... | collective-permute-start | bytes 1572872 | tf_op jit(solution)/shard_map/ppermute | solution.py:151
  (5 other events, 34.4 us)

commit v5 on v4

--- a/solution.py
+++ b/solution.py
@@ -37,7 +37,18 @@
 
 
 def late_kernel(
-    n_row, step, flags, other_ref, part_ref, rows_ref, upper_ref, block_ref, out_ref, cols
+    n_row,
+    step,
+    n_steps,
+    flags,
+    other_ref,
+    part_ref,
+    rows_ref,
+    upper_ref,
+    block_ref,
+    out_ref,
+    own_ref,
+    cols,
 ):
     size = rows_ref.shape[1]
     my_row, my_col = lax.axis_index("row"), lax.axis_index("col")
@@ -49,6 +60,7 @@
     rows = rows_ref[...]
     kept = split(jnp.where(col_hit, rows, jnp.float32(0.0)))
     owner = (my_col >> 1) == (first >> 1)
+    next_slot = lax.div(flags[6 + (step + 1) % n_steps], n_row)
     for slot in range(2):
         at = slice(slot * size, (slot + 1) * size)
         row_hit = flags[2 * step + slot] > 0
@@ -66,6 +78,10 @@
             new = jnp.where(here, rows[member * size : (member + 1) * size], new)
         out_ref[at] = new
 
+        @pl.when(next_slot == slot)
+        def _():
+            own_ref[...] = out_ref[at]
+
 
 def local(matrix, row_struct, col_struct, panel_index, lower_inv, upper_inv):
     n_row = lax.axis_size("row")
@@ -87,23 +103,24 @@
         return lax.all_to_all(value, "row", 0, 0, tiled=True)
 
     def to_leaders(sends):
-        def run(block, chunk_at, own_at, dist):
+        def run(block, own, chunk_at, dist):
             got = [from_class(block, place, spacing, hop) for place, spacing, hop in sends]
-            own = lax.dynamic_slice_in_dim(block, own_at, size, 0)
             chunk = lax.dynamic_slice_in_dim(exchange(own), chunk_at, 2 * piece, 0)
             tiled, middle = lax.optimization_barrier((jnp.tile(chunk, (n_row, 1)), block))
             for (_, _, hop), value in zip(sends, got):
                 middle = jnp.where(dist == hop % n_z, value, middle)
-            return middle, middle[:size], middle[size:], tiled
+            return middle, tiled
 
         return run
 
-    def fetch(block, later, which, chunk_at, own_at, dist):
-        middle, upper_half, lower_half, tiled = lax.switch(which, leads, block, chunk_at, own_at, dist)
+    def fetch(step, block, own, later, which, chunk_at, dist):
+        middle, tiled = lax.switch(which, leads, block, own, chunk_at, dist)
+        tiled, later = lax.optimization_barrier((tiled, later))
+        later = later[0][step], later[1][step], later[2]
         up = from_class(middle, 3, 4, 1)
         down = from_class(middle, 3, 4, -1)
-        top = from_class(upper_half, 3, 4, 2)
-        bottom = from_class(lower_half, 3, 4, -2)
+        top = from_class(middle[:size], 3, 4, 2)
+        bottom = from_class(middle[size:], 3, 4, -2)
         gathered = exchange(tiled)
         near = my_z & 3
         up, later = lax.optimization_barrier((up, later))
@@ -137,16 +154,17 @@
         places += [
             jnp.where(plane & 3 == 3, 6 + (plane >> 2), (plane & 3) + 3 * ((plane & 7) >> 2)),
             (first & (n_row - 1)) * piece,
-            (first >> (n_row.bit_length() - 1)) * size,
             dist,
         ]
-    places = lax.optimization_barrier(places)
+    own_at = (panel_index[0] >> (n_row.bit_length() - 1)) * size
+    places, own_at = lax.optimization_barrier((places, own_at))
+    own = lax.dynamic_slice_in_dim(matrix, own_at, size, 0)
 
     block = matrix
     for step in range(panel_index.shape[0]):
-        later = lower_inv[step], upper_inv[step], flags
+        later = lower_inv, upper_inv, flags
         mine, gathered, (lower, upper, flags) = fetch(
-            block, later, *places[4 * step : 4 * step + 4]
+            step, block, own, later, *places[3 * step : 3 * step + 3]
         )
         other = lax.ppermute(mine, "col", [(i, i ^ 1) for i in range(n_col)])
         rows, part = pl.pallas_call(
@@ -162,11 +180,14 @@
             cost_estimate=cost,
             name="early",
         )(gathered, mine, lower, upper)
-        block = pl.pallas_call(
-            functools.partial(late_kernel, n_row, step),
-            out_shape=jax.ShapeDtypeStruct(matrix.shape, f32),
+        block, own = pl.pallas_call(
+            functools.partial(late_kernel, n_row, step, panel_index.shape[0]),
+            out_shape=(
+                jax.ShapeDtypeStruct(matrix.shape, f32),
+                jax.ShapeDtypeStruct((size, size), f32),
+            ),
             in_specs=[scalars] + [whole] * 5,
-            out_specs=whole,
+            out_specs=(whole, whole),
             scratch_shapes=[pltpu.VMEM((2 * size, width), f32)],
             compiler_params=params,
             cost_estimate=cost,

time: 144 us -> 139 us (0.965)
  starting transfers between devices: 48.8 us -> 62.8 us
  local copies, waits for them, and re-layouts: 19.7 us -> 10.7 us
  waiting for transfers between devices: 54.4 us -> 47.6 us
  other arithmetic: 6.18 us -> 3.8 us
    ppermute x15, starting transfers between devices: 17.6 us -> 30.2 us  [send_z(): return lax.ppermute(value, 'col', pairs)]
    ppermute x15, waiting for transfers between devices: 39.9 us -> 32.6 us  [send_z(): return lax.ppermute(value, 'col', pairs)]
    cond x6 -> x0, local copies, waits for them, and re-layouts: 5.85 us -> none
    select_n x2, other arithmetic: 3.15 us -> 1.32 us  [fetch(): jnp.where(near == 3, middle, jnp.where(near == 0, up, jnp.where(near == 2...]
    all_to_all x4, starting transfers between devices: 23.5 us -> 25.3 us  [exchange(): return lax.all_to_all(value, 'row', 0, 0, tiled=True)]
    dynamic_slice x2 -> x1, local copies, waits for them, and re-layouts: 3.36 us -> 1.69 us  [local(): own = lax.dynamic_slice_in_dim(matrix, own_at, size, 0)]
    squeeze x1 -> x3, local copies, waits for them, and re-layouts: 3.63 us -> 4.31 us  [fetch(): later = (later[0][step], later[1][step], later[2])]
  transfers between devices with their start and end apart: 21 -> 21, of which waited for: 5 -> 8; matrix products, arithmetic and copies ran while one was open for 12% -> 6% of each run, Pallas kernels for 2% -> 1%
where the time goes in v5:
time: 139 us; the launch traced here: 137 us
  starting transfers between devices  62.8 us (45%)
  waiting for transfers between devices  47.6 us (34%)
  local copies, waits for them, and re-layouts  10.7 us (8%)
  Pallas kernels  9.25 us (7%)
  other arithmetic  3.8 us (3%)
  between operations  3.2 us (2%)
    ppermute x15, waiting for transfers between devices, send_z(): return lax.ppermute(value, 'col', pairs)  32.6 us
    ppermute x15, starting transfers between devices, send_z(): return lax.ppermute(value, 'col', pairs)  30.2 us
    all_to_all x4, starting transfers between devices, exchange(): return lax.all_to_all(value, 'row', 0, 0, tiled=True)  25.3 us
    all_to_all x4, waiting for transfers between devices, exchange(): return lax.all_to_all(value, 'row', 0, 0, tiled=True)  13.8 us
    ppermute x2, starting transfers between devices, local(): other = lax.ppermute(mine, 'col', [(i, i ^ 1) for i in range(n_col)])  7.29 us
    pallas_call x2, Pallas kernels, local(): pl.pallas_call(functools.partial(late_kernel, n_row, step, panel_index.sh...  7.2 us
    squeeze x3, local copies, waits for them, and re-layouts, fetch(): later = (later[0][step], later[1][step], later[2])  4.31 us
  transfers between devices with their start and end apart: 21, of which 8 were waited for; matrix products, arithmetic and copies ran while one was open for 6% of the time, Pallas kernels for 1%

profile of v5, /device:TPU:35, one launch (start us, length us, event | category | flops | bytes accessed | tf_op | source)
XLA Modules:
  0.0 137.4 jit_solution(10633560736946437721)
XLA Ops:
  4.3 1.7 %constant_dynamic-slice_fusion.20 = f32[256,256]{1,0:T(8,128)} fusion(f32[512,256]{1,0:T(8,128)} %block_ref.1, s32[]{:T(128)S(6)} %select_n.536), kind=kLoop, calls=%fused_computation.51 | loop fusion | bytes 524292 | tf_op jit(solution)/shard_map/dynamic_slice | solution.py:161
  6.0 37.8 %conditional.2 = (f32[512,256]{1,0:T(8,128)S(1)}, f32[512,256]{1,0:T(8,128)}) conditional(s32[]{:T(128)} %clamp.7, (s32[]{:T(128)}, f32[512,256]{1,0:T(8,128)}, f32[256,256]{1,0:T(8,128)}, s32[]{:T(128)}) %tuple.111, (s32[]{:T(128)}, f32[512,256]{1,0:T(8,128)}, f32[256,256]{1,0:T(8,128)}, s32[]{:T(128)}) %tuple.111, ...), branch_computations={%region_0.1_spmd, %region_1.2_spmd, %region_2.3_spmd, %region_3.4_... | conditional | flops 524295 | bytes 12943646 | solution.py:117
  6.0 11.7 %collective-permute-start.7 = (f32[512,256]{1,0:T(8,128)}, f32[512,256]{1,0:T(8,128)S(1)}, u32[]{:S(2)}, u32[]{:S(2)}) collective-permute-start(f32[512,256]{1,0:T(8,128)} %get-tuple-element.175), channel_id=1, source_target_pairs={{2,14},{3,15},{18,30},{19,31},{34,46},{35,47},{50,62},{51,63},{66,... | collective-permute-start | bytes 1572872 | tf_op jit(solution)/shard_map/cond/branch_1_fun/ppermute | solution.py:97
  17.7 2.8 %collective-permute-start.6 = (f32[512,256]{1,0:T(8,128)}, f32[512,256]{1,0:T(8,128)S(1)}, u32[]{:S(2)}, u32[]{:S(2)}) collective-permute-start(f32[512,256]{1,0:T(8,128)} %get-tuple-element.175), channel_id=1, source_target_pairs={{2,22},{3,23},{18,6},{19,7},{34,54},{35,55},{50,38},{51,39},{66,86... | collective-permute-start | bytes 1572872 | tf_op jit(solution)/shard_map/cond/branch_1_fun/ppermute | solution.py:97
  23.2 6.9 %all-to-all-start.1 = ((f32[16,16,256]{2,1,0:T(8,128)}), f32[16,16,256]{2,1,0:T(8,128)S(1)}, u32[]{:S(2)}, u32[]{:S(2)}) async-start(f32[16,16,256]{2,1,0:T(8,128)} %bitcast.3), calls=%async_computation.1 | async-start | bytes 524288 | tf_op jit(solution)/shard_map/cond/branch_1_fun/all_to_all | solution.py:103
  30.1 6.8 %all-to-all-done.1 = f32[16,16,256]{2,1,0:T(8,128)S(1)} async-done(((f32[16,16,256]{2,1,0:T(8,128)}), f32[16,16,256]{2,1,0:T(8,128)S(1)}, u32[]{:S(2)}, u32[]{:S(2)}) %all-to-all-start.1) | async-done | bytes 262176 | tf_op jit(solution)/shard_map/cond/branch_1_fun/all_to_all | solution.py:103
  37.7 2.0 %collective-permute-done.5 = f32[512,256]{1,0:T(8,128)S(1)} collective-permute-done((f32[512,256]{1,0:T(8,128)}, f32[512,256]{1,0:T(8,128)S(1)}, u32[]{:S(2)}, u32[]{:S(2)}) %collective-permute-start.5) | collective-permute-done | bytes 524320 | tf_op jit(solution)/shard_map/cond/branch_1_fun/ppermute | solution.py:97
  39.8 2.8 %collective-permute-done.4 = f32[512,256]{1,0:T(8,128)S(1)} collective-permute-done((f32[512,256]{1,0:T(8,128)}, f32[512,256]{1,0:T(8,128)S(1)}, u32[]{:S(2)}, u32[]{:S(2)}) %collective-permute-start.4) | collective-permute-done | bytes 524320 | tf_op jit(solution)/shard_map/cond/branch_1_fun/ppermute | solution.py:97
  43.9 1.5 %collective-permute-start.73 = (f32[512,256]{1,0:T(8,128)S(1)}, f32[512,256]{1,0:T(8,128)}, u32[]{:S(2)}, u32[]{:S(2)}) collective-permute-start(f32[512,256]{1,0:T(8,128)S(1)} %get-tuple-element.325), channel_id=1, source_target_pairs={{6,4},{7,5},{14,12},{15,13},{22,20},{23,21},{30,28},{31,29},{38,36... | collective-permute-start | bytes 1572872 | tf_op jit(solution)/shard_map/ppermute | solution.py:97
  45.3 1.5 %collective-permute-start.72 = (f32[512,256]{1,0:T(8,128)S(1)}, f32[512,256]{1,0:T(8,128)}, u32[]{:S(2)}, u32[]{:S(2)}) collective-permute-start(f32[512,256]{1,0:T(8,128)S(1)} %get-tuple-element.325), channel_id=1, source_target_pairs={{6,8},{7,9},{14,16},{15,17},{22,24},{23,25},{30,0},{31,1},{38,40},... | collective-permute-start | bytes 1572872 | tf_op jit(solution)/shard_map/ppermute | solution.py:97
  47.0 6.9 %all-to-all-start.20 = ((f32[16,32,256]{2,1,0:T(8,128)}), f32[16,32,256]{2,1,0:T(8,128)S(1)}, u32[]{:S(2)}, u32[]{:S(2)}) async-start(f32[16,32,256]{2,1,0:T(8,128)} %bitcast.68), calls=%async_computation.20 | async-start | bytes 1048576 | tf_op jit(solution)/shard_map/all_to_all | solution.py:103
  57.2 1.7 %slice_bitcast_fusion.2 = (f32[512,512]{1,0:T(8,128)S(1)}, f32[512,512]{1,0:T(8,128)S(1)}) fusion(f32[2,512,512]{2,1,0:T(8,128)} %param.31, f32[2,512,512]{2,1,0:T(8,128)} %param.30), kind=kLoop, calls=%fused_computation.42 | loop fusion | bytes 4194304 | tf_op jit(solution)/shard_map/squeeze | solution.py:119
  59.0 9.4 %collective-permute-done.74 = f32[256,256]{1,0:T(8,128)} collective-permute-done((f32[256,256]{1,0:T(8,128)}, f32[256,256]{1,0:T(8,128)}, u32[]{:S(2)}, u32[]{:S(2)}) %collective-permute-start.74) | collective-permute-done | bytes 262176 | tf_op jit(solution)/shard_map/ppermute | solution.py:97
  69.6 3.6 %collective-permute-start.76 = (f32[512,256]{1,0:T(8,128)S(1)}, f32[512,256]{1,0:T(8,128)}, u32[]{:S(2)}, u32[]{:S(2)}) collective-permute-start(f32[512,256]{1,0:T(8,128)S(1)} %fusion.1.mine_ref), channel_id=1, source_target_pairs={{0,1},{1,0},{2,3},{3,2},{4,5},{5,4},{6,7},{7,6},{8,9},{9,8},{10,11... | collective-permute-start | bytes 1572872 | tf_op jit(solution)/shard_map/ppermute | solution.py:169
  74.8 3.5 %late.2 = (f32[512,256]{1,0:T(8,128)}, f32[256,256]{1,0:T(8,128)}) custom-call(s32[8]{0:T(128)S(1)} %pad_add_fusion.flags, f32[512,256]{1,0:T(8,128)} %collective-permute-done.76.other_ref, f32[512,512]{1,0:T(8,128)S(1)} %get-tuple-element.335.part_ref, f32[512,256]{1,0:T(8,128)S(1)} %get-tuple-element.336.rows_ref, ...), custom_call_target="tpu_custom_call" | custom-call | flops 805306368 | bytes 3145728 | tf_op jit(solution)/shard_map/late/pallas_call | solution.py:183
  78.3 18.1 %conditional.3 = (f32[512,256]{1,0:T(8,128)S(1)}, f32[512,256]{1,0:T(8,128)}) conditional(s32[]{:T(128)} %clamp.6, (s32[]{:T(128)}, f32[512,256]{1,0:T(8,128)}, f32[256,256]{1,0:T(8,128)}, s32[]{:T(128)}) %tuple.114, (s32[]{:T(128)}, f32[512,256]{1,0:T(8,128)}, f32[256,256]{1,0:T(8,128)}, s32[]{:T(128)}) %tuple.114, ...), branch_computations={%region_10.11_spmd, %region_11.12_spmd, %region_12.13_spmd, %regio... | conditional | flops 524295 | bytes 12943646 | solution.py:117
  80.4 6.9 %all-to-all-start.19 = ((f32[16,16,256]{2,1,0:T(8,128)}), f32[16,16,256]{2,1,0:T(8,128)S(1)}, u32[]{:S(2)}, u32[]{:S(2)}) async-start(f32[16,16,256]{2,1,0:T(8,128)} %bitcast.57), calls=%async_computation.19 | async-start | bytes 524288 | tf_op jit(solution)/shard_map/cond/branch_9_fun/all_to_all | solution.py:103
  87.3 7.0 %all-to-all-done.19 = f32[16,16,256]{2,1,0:T(8,128)S(1)} async-done(((f32[16,16,256]{2,1,0:T(8,128)}), f32[16,16,256]{2,1,0:T(8,128)S(1)}, u32[]{:S(2)}, u32[]{:S(2)}) %all-to-all-start.19) | async-done | bytes 262176 | tf_op jit(solution)/shard_map/cond/branch_9_fun/all_to_all | solution.py:103
  97.2 1.5 %collective-permute-start.78 = (f32[512,256]{1,0:T(8,128)S(1)}, f32[512,256]{1,0:T(8,128)}, u32[]{:S(2)}, u32[]{:S(2)}) collective-permute-start(f32[512,256]{1,0:T(8,128)S(1)} %get-tuple-element.340), channel_id=1, source_target_pairs={{6,4},{7,5},{14,12},{15,13},{22,20},{23,21},{30,28},{31,29},{38,36... | collective-permute-start | bytes 1572872 | tf_op jit(solution)/shard_map/ppermute | solution.py:97
  98.7 1.5 %collective-permute-start.77 = (f32[512,256]{1,0:T(8,128)S(1)}, f32[512,256]{1,0:T(8,128)}, u32[]{:S(2)}, u32[]{:S(2)}) collective-permute-start(f32[512,256]{1,0:T(8,128)S(1)} %get-tuple-element.340), channel_id=1, source_target_pairs={{6,8},{7,9},{14,16},{15,17},{22,24},{23,25},{30,0},{31,1},{38,40},... | collective-permute-start | bytes 1572872 | tf_op jit(solution)/shard_map/ppermute | solution.py:97
  100.1 4.5 %all-to-all-start.21 = ((f32[16,32,256]{2,1,0:T(8,128)}), f32[16,32,256]{2,1,0:T(8,128)S(1)}, u32[]{:S(2)}, u32[]{:S(2)}) async-start(f32[16,32,256]{2,1,0:T(8,128)} %bitcast.72), calls=%async_computation.21 | async-start | bytes 1048576 | tf_op jit(solution)/shard_map/all_to_all | solution.py:103
  109.9 18.3 %collective-permute-done.79 = f32[256,256]{1,0:T(8,128)S(1)} collective-permute-done((f32[256,256]{1,0:T(8,128)}, f32[256,256]{1,0:T(8,128)S(1)}, u32[]{:S(2)}, u32[]{:S(2)}) %collective-permute-start.79) | collective-permute-done | bytes 262176 | tf_op jit(solution)/shard_map/ppermute | solution.py:97
  128.3 3.7 %collective-permute-start.81 = (f32[512,256]{1,0:T(8,128)S(1)}, f32[512,256]{1,0:T(8,128)}, u32[]{:S(2)}, u32[]{:S(2)}) collective-permute-start(f32[512,256]{1,0:T(8,128)S(1)} %fusion.3.mine_ref), channel_id=1, source_target_pairs={{0,1},{1,0},{2,3},{3,2},{4,5},{5,4},{6,7},{7,6},{8,9},{9,8},{10,11... | collective-permute-start | bytes 1572872 | tf_op jit(solution)/shard_map/ppermute | solution.py:169
  133.7 3.7 %late.3 = (f32[512,256]{1,0:T(8,128)}, f32[256,256]{1,0:T(8,128)}) custom-call(s32[8]{0:T(128)S(1)} %pad_add_fusion.flags, f32[512,256]{1,0:T(8,128)} %collective-permute-done.81.other_ref, f32[512,512]{1,0:T(8,128)S(1)} %get-tuple-element.350.part_ref, f32[512,256]{1,0:T(8,128)S(1)} %get-tuple-element.351.rows_ref, ...), custom_call_target="tpu_custom_call" | custom-call | flops 805306368 | bytes 3145728 | tf_op jit(solution)/shard_map/late/pallas_call | solution.py:183
  (53 shorter events, 24.2 us)
Async XLA Ops:
  6.0 40.8 %copy-start.5 = (s32[2,2]{1,0:T(2,128)S(1)}, s32[2,2]{1,0:T(2,128)}, u32[]{:S(2)}) copy-start(s32[2,2]{1,0:T(2,128)} %param.27) | copy-start | bytes 52
  6.0 40.9 %copy-start.3 = (s32[2]{0:T(128)S(1)}, s32[2]{0:T(128)}, u32[]{:S(2)}) copy-start(s32[2]{0:T(128)} %param.29) | copy-start | bytes 28
  6.0 40.9 %copy-start.4 = (s32[2,1]{0,1:T(1,128)S(1)}, s32[2,1]{0,1:T(1,128)}, u32[]{:S(2)}) copy-start(s32[2,1]{0,1:T(1,128)} %param.28) | copy-start | bytes 28
  6.0 31.7 %collective-permute-start.7 = (f32[512,256]{1,0:T(8,128)}, f32[512,256]{1,0:T(8,128)S(1)}, u32[]{:S(2)}, u32[]{:S(2)}) collective-permute-start(f32[512,256]{1,0:T(8,128)} %get-tuple-element.175), channel_id=1, source_target_pairs={{2,14},{3,15},{18,30},{19,31},{34,46},{35,47},{50,62},{51,63},{66,... | collective-permute-start | bytes 1572872 | tf_op jit(solution)/shard_map/cond/branch_1_fun/ppermute | solution.py:97
  17.7 20.0 %collective-permute-start.6 = (f32[512,256]{1,0:T(8,128)}, f32[512,256]{1,0:T(8,128)S(1)}, u32[]{:S(2)}, u32[]{:S(2)}) collective-permute-start(f32[512,256]{1,0:T(8,128)} %get-tuple-element.175), channel_id=1, source_target_pairs={{2,22},{3,23},{18,6},{19,7},{34,54},{35,55},{50,38},{51,39},{66,86... | collective-permute-start | bytes 1572872 | tf_op jit(solution)/shard_map/cond/branch_1_fun/ppermute | solution.py:97
  20.5 19.3 %collective-permute-start.5 = (f32[512,256]{1,0:T(8,128)}, f32[512,256]{1,0:T(8,128)S(1)}, u32[]{:S(2)}, u32[]{:S(2)}) collective-permute-start(f32[512,256]{1,0:T(8,128)} %get-tuple-element.175), channel_id=1, source_target_pairs={{2,6},{3,7},{10,14},{11,15},{18,22},{19,23},{26,30},{27,31},{34,38... | collective-permute-start | bytes 1572872 | tf_op jit(solution)/shard_map/cond/branch_1_fun/ppermute | solution.py:97
  21.9 20.8 %collective-permute-start.4 = (f32[512,256]{1,0:T(8,128)}, f32[512,256]{1,0:T(8,128)S(1)}, u32[]{:S(2)}, u32[]{:S(2)}) collective-permute-start(f32[512,256]{1,0:T(8,128)} %get-tuple-element.175), channel_id=1, source_target_pairs={{2,30},{3,31},{10,6},{11,7},{18,14},{19,15},{26,22},{27,23},{34,62... | collective-permute-start | bytes 1572872 | tf_op jit(solution)/shard_map/cond/branch_1_fun/ppermute | solution.py:97
  23.2 13.7 %all-to-all-start.1 = ((f32[16,16,256]{2,1,0:T(8,128)}), f32[16,16,256]{2,1,0:T(8,128)S(1)}, u32[]{:S(2)}, u32[]{:S(2)}) async-start(f32[16,16,256]{2,1,0:T(8,128)} %bitcast.3), calls=%async_computation.1 | async-start | bytes 524288 | tf_op jit(solution)/shard_map/cond/branch_1_fun/all_to_all | solution.py:103
  43.9 24.5 %collective-permute-start.73 = (f32[512,256]{1,0:T(8,128)S(1)}, f32[512,256]{1,0:T(8,128)}, u32[]{:S(2)}, u32[]{:S(2)}) collective-permute-start(f32[512,256]{1,0:T(8,128)S(1)} %get-tuple-element.325), channel_id=1, source_target_pairs={{6,4},{7,5},{14,12},{15,13},{22,20},{23,21},{30,28},{31,29},{38,36... | collective-permute-start | bytes 1572872 | tf_op jit(solution)/shard_map/ppermute | solution.py:97
  45.3 13.6 %collective-permute-start.72 = (f32[512,256]{1,0:T(8,128)S(1)}, f32[512,256]{1,0:T(8,128)}, u32[]{:S(2)}, u32[]{:S(2)}) collective-permute-start(f32[512,256]{1,0:T(8,128)S(1)} %get-tuple-element.325), channel_id=1, source_target_pairs={{6,8},{7,9},{14,16},{15,17},{22,24},{23,25},{30,0},{31,1},{38,40},... | collective-permute-start | bytes 1572872 | tf_op jit(solution)/shard_map/ppermute | solution.py:97
  47.0 26.2 %all-to-all-start.20 = ((f32[16,32,256]{2,1,0:T(8,128)}), f32[16,32,256]{2,1,0:T(8,128)S(1)}, u32[]{:S(2)}, u32[]{:S(2)}) async-start(f32[16,32,256]{2,1,0:T(8,128)} %bitcast.68), calls=%async_computation.20 | async-start | bytes 1048576 | tf_op jit(solution)/shard_map/all_to_all | solution.py:103
  54.6 13.8 %collective-permute-start.74 = (f32[256,256]{1,0:T(8,128)}, f32[256,256]{1,0:T(8,128)}, u32[]{:S(2)}, u32[]{:S(2)}) collective-permute-start(f32[256,256]{1,0:T(8,128)} %get-tuple-element.355), channel_id=1, source_target_pairs={{6,10},{7,11},{14,18},{15,19},{22,26},{23,27},{30,2},{31,3},{38,42... | collective-permute-start | bytes 786440 | tf_op jit(solution)/shard_map/ppermute | solution.py:97
  55.9 12.5 %collective-permute-start.75 = (f32[256,256]{1,0:T(8,128)S(1)}, f32[256,256]{1,0:T(8,128)}, u32[]{:S(2)}, u32[]{:S(2)}) collective-permute-start(f32[256,256]{1,0:T(8,128)S(1)} %get-tuple-element.356), channel_id=1, source_target_pairs={{6,2},{7,3},{14,10},{15,11},{22,18},{23,19},{30,26},{31,27},{38,34... | collective-permute-start | bytes 786440 | tf_op jit(solution)/shard_map/ppermute | solution.py:97
  69.6 5.2 %collective-permute-start.76 = (f32[512,256]{1,0:T(8,128)S(1)}, f32[512,256]{1,0:T(8,128)}, u32[]{:S(2)}, u32[]{:S(2)}) collective-permute-start(f32[512,256]{1,0:T(8,128)S(1)} %fusion.1.mine_ref), channel_id=1, source_target_pairs={{0,1},{1,0},{2,3},{3,2},{4,5},{5,4},{6,7},{7,6},{8,9},{9,8},{10,11... | collective-permute-start | bytes 1572872 | tf_op jit(solution)/shard_map/ppermute | solution.py:169
  78.3 16.9 %collective-permute-start.71 = (f32[512,256]{1,0:T(8,128)}, f32[512,256]{1,0:T(8,128)S(1)}, u32[]{:S(2)}, u32[]{:S(2)}) collective-permute-start(f32[512,256]{1,0:T(8,128)} %get-tuple-element.283), channel_id=1, source_target_pairs={{30,14},{31,15},{62,46},{63,47},{94,78},{95,79},{126,110},{127,111... | collective-permute-start | bytes 1572872 | tf_op jit(solution)/shard_map/cond/branch_9_fun/ppermute | solution.py:97
  79.0 16.2 %collective-permute-start.70 = (f32[512,256]{1,0:T(8,128)}, f32[512,256]{1,0:T(8,128)S(1)}, u32[]{:S(2)}, u32[]{:S(2)}) collective-permute-start(f32[512,256]{1,0:T(8,128)} %get-tuple-element.283), channel_id=1, source_target_pairs={{30,6},{31,7},{62,38},{63,39},{94,70},{95,71},{126,102},{127,103},... | collective-permute-start | bytes 1572872 | tf_op jit(solution)/shard_map/cond/branch_9_fun/ppermute | solution.py:97
  79.7 15.5 %collective-permute-start.69 = (f32[512,256]{1,0:T(8,128)}, f32[512,256]{1,0:T(8,128)S(1)}, u32[]{:S(2)}, u32[]{:S(2)}) collective-permute-start(f32[512,256]{1,0:T(8,128)} %get-tuple-element.283), channel_id=1, source_target_pairs={{30,22},{31,23},{62,54},{63,55},{94,86},{95,87},{126,118},{127,119... | collective-permute-start | bytes 1572872 | tf_op jit(solution)/shard_map/cond/branch_9_fun/ppermute | solution.py:97
  80.4 13.9 %all-to-all-start.19 = ((f32[16,16,256]{2,1,0:T(8,128)}), f32[16,16,256]{2,1,0:T(8,128)S(1)}, u32[]{:S(2)}, u32[]{:S(2)}) async-start(f32[16,16,256]{2,1,0:T(8,128)} %bitcast.57), calls=%async_computation.19 | async-start | bytes 524288 | tf_op jit(solution)/shard_map/cond/branch_9_fun/all_to_all | solution.py:103
  97.2 30.9 %collective-permute-start.78 = (f32[512,256]{1,0:T(8,128)S(1)}, f32[512,256]{1,0:T(8,128)}, u32[]{:S(2)}, u32[]{:S(2)}) collective-permute-start(f32[512,256]{1,0:T(8,128)S(1)} %get-tuple-element.340), channel_id=1, source_target_pairs={{6,4},{7,5},{14,12},{15,13},{22,20},{23,21},{30,28},{31,29},{38,36... | collective-permute-start | bytes 1572872 | tf_op jit(solution)/shard_map/ppermute | solution.py:97
  98.7 11.2 %collective-permute-start.77 = (f32[512,256]{1,0:T(8,128)S(1)}, f32[512,256]{1,0:T(8,128)}, u32[]{:S(2)}, u32[]{:S(2)}) collective-permute-start(f32[512,256]{1,0:T(8,128)S(1)} %get-tuple-element.340), channel_id=1, source_target_pairs={{6,8},{7,9},{14,16},{15,17},{22,24},{23,25},{30,0},{31,1},{38,40},... | collective-permute-start | bytes 1572872 | tf_op jit(solution)/shard_map/ppermute | solution.py:97
  100.1 31.9 %all-to-all-start.21 = ((f32[16,32,256]{2,1,0:T(8,128)}), f32[16,32,256]{2,1,0:T(8,128)S(1)}, u32[]{:S(2)}, u32[]{:S(2)}) async-start(f32[16,32,256]{2,1,0:T(8,128)} %bitcast.72), calls=%async_computation.21 | async-start | bytes 1048576 | tf_op jit(solution)/shard_map/all_to_all | solution.py:103
  104.7 23.5 %collective-permute-start.79 = (f32[256,256]{1,0:T(8,128)}, f32[256,256]{1,0:T(8,128)S(1)}, u32[]{:S(2)}, u32[]{:S(2)}) collective-permute-start(f32[256,256]{1,0:T(8,128)} %get-tuple-element.353), channel_id=1, source_target_pairs={{6,10},{7,11},{14,18},{15,19},{22,26},{23,27},{30,2},{31,3},{38,42... | collective-permute-start | bytes 786440 | tf_op jit(solution)/shard_map/ppermute | solution.py:97
  106.0 22.2 %collective-permute-start.80 = (f32[256,256]{1,0:T(8,128)S(1)}, f32[256,256]{1,0:T(8,128)S(1)}, u32[]{:S(2)}, u32[]{:S(2)}) collective-permute-start(f32[256,256]{1,0:T(8,128)S(1)} %get-tuple-element.354), channel_id=1, source_target_pairs={{6,2},{7,3},{14,10},{15,11},{22,18},{23,19},{30,26},{31,27},{38,34... | collective-permute-start | bytes 786440 | tf_op jit(solution)/shard_map/ppermute | solution.py:97
  128.3 5.4 %collective-permute-start.81 = (f32[512,256]{1,0:T(8,128)S(1)}, f32[512,256]{1,0:T(8,128)}, u32[]{:S(2)}, u32[]{:S(2)}) collective-permute-start(f32[512,256]{1,0:T(8,128)S(1)} %fusion.3.mine_ref), channel_id=1, source_target_pairs={{0,1},{1,0},{2,3},{3,2},{4,5},{5,4},{6,7},{7,6},{8,9},{9,8},{10,11... | collective-permute-start | bytes 1572872 | tf_op jit(solution)/shard_map/ppermute | solution.py:169
  (3 other events, 28.9 us)

commit v6 on v5

--- a/solution.py
+++ b/solution.py
@@ -105,6 +105,8 @@
     def to_leaders(sends):
         def run(block, own, chunk_at, dist):
             got = [from_class(block, place, spacing, hop) for place, spacing, hop in sends]
+            if own.ndim == 0:
+                own = lax.dynamic_slice_in_dim(block, own, size, 0)
             chunk = lax.dynamic_slice_in_dim(exchange(own), chunk_at, 2 * piece, 0)
             tiled, middle = lax.optimization_barrier((jnp.tile(chunk, (n_row, 1)), block))
             for (_, _, hop), value in zip(sends, got):
@@ -157,8 +159,7 @@
             dist,
         ]
     own_at = (panel_index[0] >> (n_row.bit_length() - 1)) * size
-    places, own_at = lax.optimization_barrier((places, own_at))
-    own = lax.dynamic_slice_in_dim(matrix, own_at, size, 0)
+    places, own = lax.optimization_barrier((places, own_at))
 
     block = matrix
     for step in range(panel_index.shape[0]):
@@ -183,8 +184,8 @@
         block, own = pl.pallas_call(
             functools.partial(late_kernel, n_row, step, panel_index.shape[0]),
             out_shape=(
-                jax.ShapeDtypeStruct(matrix.shape, f32),
-                jax.ShapeDtypeStruct((size, size), f32),
+                pltpu.VMEM(matrix.shape, f32),
+                pltpu.VMEM((size, size), f32),
             ),
             in_specs=[scalars] + [whole] * 5,
             out_specs=(whole, whole),

time: 139 us -> 141 us (1.014)
  starting transfers between devices: 62.8 us -> 46.6 us
  waiting for transfers between devices: 47.6 us -> 63.1 us
  local copies, waits for them, and re-layouts: 10.7 us -> 12.5 us
    ppermute x15, waiting for transfers between devices: 32.6 us -> 48.7 us  [send_z(): return lax.ppermute(value, 'col', pairs)]
    ppermute x15, starting transfers between devices: 30.2 us -> 15.8 us  [send_z(): return lax.ppermute(value, 'col', pairs)]
    all_to_all x4, starting transfers between devices: 25.3 us -> 22.4 us  [exchange(): return lax.all_to_all(value, 'row', 0, 0, tiled=True)]
  transfers between devices with their start and end apart: 21 -> 21, of which waited for: 8 -> 6; matrix products, arithmetic and copies ran while one was open for 6% -> 8% of each run, Pallas kernels for 1% -> 2%
where the time goes in v6:
time: 141 us; the launch traced here: 140 us
  waiting for transfers between devices  63.1 us (45%)
  starting transfers between devices  46.6 us (33%)
  local copies, waits for them, and re-layouts  12.5 us (9%)
  Pallas kernels  9.99 us (7%)
  other arithmetic  4.34 us (3%)
  between operations  3.34 us (2%)
    ppermute x15, waiting for transfers between devices, send_z(): return lax.ppermute(value, 'col', pairs)  48.7 us
    all_to_all x4, starting transfers between devices, exchange(): return lax.all_to_all(value, 'row', 0, 0, tiled=True)  22.4 us
    ppermute x15, starting transfers between devices, send_z(): return lax.ppermute(value, 'col', pairs)  15.8 us
    all_to_all x4, waiting for transfers between devices, exchange(): return lax.all_to_all(value, 'row', 0, 0, tiled=True)  13.8 us
    ppermute x2, starting transfers between devices, local(): other = lax.ppermute(mine, 'col', [(i, i ^ 1) for i in range(n_col)])  8.4 us
    pallas_call x2, Pallas kernels, local(): pl.pallas_call(functools.partial(late_kernel, n_row, step, panel_index.sh...  6.88 us
    squeeze x3, local copies, waits for them, and re-layouts, fetch(): later = (later[0][step], later[1][step], later[2])  4.31 us
    pallas_call x2, Pallas kernels, local(): pl.pallas_call(functools.partial(early_kernel, n_row), out_shape=(jax.Sha...  3.11 us
  transfers between devices with their start and end apart: 21, of which 6 were waited for; matrix products, arithmetic and copies ran while one was open for 8% of the time, Pallas kernels for 2%

profile of v6, /device:TPU:35, one launch (start us, length us, event | category | flops | bytes accessed | tf_op | source)
XLA Modules:
  0.0 140.0 jit_solution(8090392033184654879)
XLA Ops:
  0.0 1.3 fusion.6
  4.5 20.3 %conditional.2 = (f32[512,256]{1,0:T(8,128)S(1)}, f32[512,256]{1,0:T(8,128)}) conditional(s32[]{:T(128)} %clamp.7, (s32[]{:T(128)}, f32[512,256]{1,0:T(8,128)}, s32[]{:T(128)}, s32[]{:T(128)}) %tuple.111, (s32[]{:T(128)}, f32[512,256]{1,0:T(8,128)}, s32[]{:T(128)}, s32[]{:T(128)}) %tuple.111, (s32[]{:T(128)}, ...), branch_computations={%region_0.1_spmd, %region_1.2_spmd, %region_2.3_spmd, %region_3.4_... | conditional | flops 524298 | bytes 13467972 | solution.py:119
  7.3 1.7 %constant_dynamic-slice_fusion.7 = f32[256,256]{1,0:T(8,128)} fusion(f32[512,256]{1,0:T(8,128)} %get-tuple-element.187, s32[]{:T(128)S(6)} %select_n.414), kind=kLoop, calls=%fused_computation.11 | loop fusion | bytes 524292 | tf_op jit(solution)/shard_map/cond/branch_3_fun/dynamic_slice | solution.py:109
  9.0 6.9 %all-to-all-start.3 = ((f32[16,16,256]{2,1,0:T(8,128)}), f32[16,16,256]{2,1,0:T(8,128)S(1)}, u32[]{:S(2)}, u32[]{:S(2)}) async-start(f32[16,16,256]{2,1,0:T(8,128)} %bitcast.9), calls=%async_computation.3 | async-start | bytes 524288 | tf_op jit(solution)/shard_map/cond/branch_3_fun/all_to_all | solution.py:103
  16.0 6.8 %all-to-all-done.3 = f32[16,16,256]{2,1,0:T(8,128)S(1)} async-done(((f32[16,16,256]{2,1,0:T(8,128)}), f32[16,16,256]{2,1,0:T(8,128)S(1)}, u32[]{:S(2)}, u32[]{:S(2)}) %all-to-all-start.3) | async-done | bytes 262176 | tf_op jit(solution)/shard_map/cond/branch_3_fun/all_to_all | solution.py:103
  24.8 1.5 %collective-permute-start.73 = (f32[512,256]{1,0:T(8,128)S(1)}, f32[512,256]{1,0:T(8,128)}, u32[]{:S(2)}, u32[]{:S(2)}) collective-permute-start(f32[512,256]{1,0:T(8,128)S(1)} %get-tuple-element.325), channel_id=1, source_target_pairs={{6,4},{7,5},{14,12},{15,13},{22,20},{23,21},{30,28},{31,29},{38,36... | collective-permute-start | bytes 1572872 | tf_op jit(solution)/shard_map/ppermute | solution.py:97
  26.3 1.5 %collective-permute-start.72 = (f32[512,256]{1,0:T(8,128)S(1)}, f32[512,256]{1,0:T(8,128)}, u32[]{:S(2)}, u32[]{:S(2)}) collective-permute-start(f32[512,256]{1,0:T(8,128)S(1)} %get-tuple-element.325), channel_id=1, source_target_pairs={{6,8},{7,9},{14,16},{15,17},{22,24},{23,25},{30,0},{31,1},{38,40},... | collective-permute-start | bytes 1572872 | tf_op jit(solution)/shard_map/ppermute | solution.py:97
  27.9 4.3 %all-to-all-start.20 = ((f32[16,32,256]{2,1,0:T(8,128)}), f32[16,32,256]{2,1,0:T(8,128)S(1)}, u32[]{:S(2)}, u32[]{:S(2)}) async-start(f32[16,32,256]{2,1,0:T(8,128)} %bitcast.68), calls=%async_computation.20 | async-start | bytes 1048576 | tf_op jit(solution)/shard_map/all_to_all | solution.py:103
  35.5 1.7 %slice_bitcast_fusion.2 = (f32[512,512]{1,0:T(8,128)S(1)}, f32[512,512]{1,0:T(8,128)S(1)}) fusion(f32[2,512,512]{2,1,0:T(8,128)} %param.31, f32[2,512,512]{2,1,0:T(8,128)} %param.30), kind=kLoop, calls=%fused_computation.52 | loop fusion | bytes 4194304 | tf_op jit(solution)/shard_map/squeeze | solution.py:121
  37.3 28.2 %collective-permute-done.74 = f32[256,256]{1,0:T(8,128)} collective-permute-done((f32[256,256]{1,0:T(8,128)}, f32[256,256]{1,0:T(8,128)}, u32[]{:S(2)}, u32[]{:S(2)}) %collective-permute-start.74) | collective-permute-done | bytes 262176 | tf_op jit(solution)/shard_map/ppermute | solution.py:97
  66.9 4.7 %collective-permute-start.76 = (f32[512,256]{1,0:T(8,128)S(1)}, f32[512,256]{1,0:T(8,128)}, u32[]{:S(2)}, u32[]{:S(2)}) collective-permute-start(f32[512,256]{1,0:T(8,128)S(1)} %fusion.1.mine_ref), channel_id=1, source_target_pairs={{0,1},{1,0},{2,3},{3,2},{4,5},{5,4},{6,7},{7,6},{8,9},{9,8},{10,11... | collective-permute-start | bytes 1572872 | tf_op jit(solution)/shard_map/ppermute | solution.py:170
  73.3 3.5 %late.2 = (f32[512,256]{1,0:T(8,128)S(1)}, f32[256,256]{1,0:T(8,128)}) custom-call(s32[8]{0:T(128)S(1)} %pad_add_fusion.flags, f32[512,256]{1,0:T(8,128)} %collective-permute-done.76.other_ref, f32[512,512]{1,0:T(8,128)S(1)} %get-tuple-element.335.part_ref, f32[512,256]{1,0:T(8,128)S(1)} %get-tuple-element.336.rows_ref, ...), custom_call_target="tpu_custom_call" | custom-call | flops 805306368 | bytes 3145728 | tf_op jit(solution)/shard_map/late/pallas_call | solution.py:184
  76.8 17.6 %conditional.3 = (f32[512,256]{1,0:T(8,128)}, f32[512,256]{1,0:T(8,128)}) conditional(s32[]{:T(128)} %clamp.6, (s32[]{:T(128)}, f32[512,256]{1,0:T(8,128)S(1)}, f32[256,256]{1,0:T(8,128)}, s32[]{:T(128)}) %tuple.114, (s32[]{:T(128)}, f32[512,256]{1,0:T(8,128)S(1)}, f32[256,256]{1,0:T(8,128)}, s32[]{:T(128)}) %tuple.114, ...), branch_computations={%region_10.11_spmd, %region_11.12_spmd, %region_12.13_spmd, %regio... | conditional | flops 524295 | bytes 12943646 | solution.py:119
  78.9 6.7 %all-to-all-start.19 = ((f32[16,16,256]{2,1,0:T(8,128)}), f32[16,16,256]{2,1,0:T(8,128)S(1)}, u32[]{:S(2)}, u32[]{:S(2)}) async-start(f32[16,16,256]{2,1,0:T(8,128)} %bitcast.57), calls=%async_computation.19 | async-start | bytes 524288 | tf_op jit(solution)/shard_map/cond/branch_9_fun/all_to_all | solution.py:103
  85.6 7.0 %all-to-all-done.19 = f32[16,16,256]{2,1,0:T(8,128)S(1)} async-done(((f32[16,16,256]{2,1,0:T(8,128)}), f32[16,16,256]{2,1,0:T(8,128)S(1)}, u32[]{:S(2)}, u32[]{:S(2)}) %all-to-all-start.19) | async-done | bytes 262176 | tf_op jit(solution)/shard_map/cond/branch_9_fun/all_to_all | solution.py:103
  94.4 1.8 %fusion.4 = (f32[256,256]{1,0:T(8,128)}, f32[256,256]{1,0:T(8,128)S(1)}) fusion(f32[512,256]{1,0:T(8,128)} %get-tuple-element.340), kind=kLoop, calls=%fused_computation.61 | loop fusion | bytes 1048576 | tf_op jit(solution)/shard_map/slice | solution.py:124
  96.2 1.5 %collective-permute-start.78 = (f32[512,256]{1,0:T(8,128)}, f32[512,256]{1,0:T(8,128)}, u32[]{:S(2)}, u32[]{:S(2)}) collective-permute-start(f32[512,256]{1,0:T(8,128)} %get-tuple-element.340), channel_id=1, source_target_pairs={{6,4},{7,5},{14,12},{15,13},{22,20},{23,21},{30,28},{31,29},{38,36... | collective-permute-start | bytes 1572872 | tf_op jit(solution)/shard_map/ppermute | solution.py:97
  97.7 1.5 %collective-permute-start.77 = (f32[512,256]{1,0:T(8,128)}, f32[512,256]{1,0:T(8,128)}, u32[]{:S(2)}, u32[]{:S(2)}) collective-permute-start(f32[512,256]{1,0:T(8,128)} %get-tuple-element.340), channel_id=1, source_target_pairs={{6,8},{7,9},{14,16},{15,17},{22,24},{23,25},{30,0},{31,1},{38,40},... | collective-permute-start | bytes 1572872 | tf_op jit(solution)/shard_map/ppermute | solution.py:97
  99.1 4.5 %all-to-all-start.21 = ((f32[16,32,256]{2,1,0:T(8,128)}), f32[16,32,256]{2,1,0:T(8,128)S(1)}, u32[]{:S(2)}, u32[]{:S(2)}) async-start(f32[16,32,256]{2,1,0:T(8,128)} %bitcast.72), calls=%async_computation.21 | async-start | bytes 1048576 | tf_op jit(solution)/shard_map/all_to_all | solution.py:103
  106.2 1.3 slice_bitcast_fusion.1.lower_ref
  108.9 20.2 %collective-permute-done.79 = f32[256,256]{1,0:T(8,128)S(1)} collective-permute-done((f32[256,256]{1,0:T(8,128)}, f32[256,256]{1,0:T(8,128)S(1)}, u32[]{:S(2)}, u32[]{:S(2)}) %collective-permute-start.79) | collective-permute-done | bytes 262176 | tf_op jit(solution)/shard_map/ppermute | solution.py:97
  130.0 3.7 %collective-permute-start.81 = (f32[512,256]{1,0:T(8,128)}, f32[512,256]{1,0:T(8,128)}, u32[]{:S(2)}, u32[]{:S(2)}) collective-permute-start(f32[512,256]{1,0:T(8,128)} %fusion.3.mine_ref), channel_id=1, source_target_pairs={{0,1},{1,0},{2,3},{3,2},{4,5},{5,4},{6,7},{7,6},{8,9},{9,8},{10,11... | collective-permute-start | bytes 1572872 | tf_op jit(solution)/shard_map/ppermute | solution.py:170
  133.8 2.1 %early.3 = (f32[512,256]{1,0:T(8,128)S(1)}, f32[512,512]{1,0:T(8,128)S(1)}) custom-call(f32[512,256]{1,0:T(8,128)S(1)} %bitcast.79, f32[512,256]{1,0:T(8,128)} %fusion.3.mine_ref, f32[512,512]{1,0:T(8,128)S(1)} %slice_bitcast_fusion.1.lower_ref, f32[512,512]{1,0:T(8,128)S(1)} %slice_bitcast_fusion.upper_ref), custom_call_target="tpu_custom_call" | custom-call | flops 805306368 | bytes 3145728 | tf_op jit(solution)/shard_map/early/pallas_call | solution.py:171
  135.8 3.4 %late.3 = (f32[512,256]{1,0:T(8,128)S(1)}, f32[256,256]{1,0:T(8,128)}) custom-call(s32[8]{0:T(128)S(1)} %pad_add_fusion.flags, f32[512,256]{1,0:T(8,128)} %collective-permute-done.81.other_ref, f32[512,512]{1,0:T(8,128)S(1)} %get-tuple-element.350.part_ref, f32[512,256]{1,0:T(8,128)S(1)} %get-tuple-element.351.rows_ref, ...), custom_call_target="tpu_custom_call" | custom-call | flops 805306368 | bytes 3145728 | tf_op jit(solution)/shard_map/late/pallas_call | solution.py:184
  (52 shorter events, 20.9 us)
Async XLA Ops:
  4.5 23.3 %copy-start.4 = (s32[2,2]{1,0:T(2,128)S(1)}, s32[2,2]{1,0:T(2,128)}, u32[]{:S(2)}) copy-start(s32[2,2]{1,0:T(2,128)} %param.27) | copy-start | bytes 52
  4.5 23.4 %copy-start.2 = (s32[2]{0:T(128)S(1)}, s32[2]{0:T(128)}, u32[]{:S(2)}) copy-start(s32[2]{0:T(128)} %param.29) | copy-start | bytes 28
  4.5 23.4 %copy-start.3 = (s32[2,1]{0,1:T(1,128)S(1)}, s32[2,1]{0,1:T(1,128)}, u32[]{:S(2)}) copy-start(s32[2,1]{0,1:T(1,128)} %param.28) | copy-start | bytes 28
  4.5 19.0 %collective-permute-start.15 = (f32[512,256]{1,0:T(8,128)}, f32[512,256]{1,0:T(8,128)S(1)}, u32[]{:S(2)}, u32[]{:S(2)}) collective-permute-start(f32[512,256]{1,0:T(8,128)} %get-tuple-element.187), channel_id=1, source_target_pairs={{8,22},{9,23},{24,6},{25,7},{40,54},{41,55},{56,38},{57,39},{72,86... | collective-permute-start | bytes 1572872 | tf_op jit(solution)/shard_map/cond/branch_3_fun/ppermute | solution.py:97
  5.2 18.3 %collective-permute-start.14 = (f32[512,256]{1,0:T(8,128)}, f32[512,256]{1,0:T(8,128)S(1)}, u32[]{:S(2)}, u32[]{:S(2)}) collective-permute-start(f32[512,256]{1,0:T(8,128)} %get-tuple-element.187), channel_id=1, source_target_pairs={{8,30},{9,31},{24,14},{25,15},{40,62},{41,63},{56,46},{57,47},{72,... | collective-permute-start | bytes 1572872 | tf_op jit(solution)/shard_map/cond/branch_3_fun/ppermute | solution.py:97
  5.9 17.6 %collective-permute-start.13 = (f32[512,256]{1,0:T(8,128)}, f32[512,256]{1,0:T(8,128)S(1)}, u32[]{:S(2)}, u32[]{:S(2)}) collective-permute-start(f32[512,256]{1,0:T(8,128)} %get-tuple-element.187), channel_id=1, source_target_pairs={{0,6},{1,7},{8,14},{9,15},{16,22},{17,23},{24,30},{25,31},{32,38},... | collective-permute-start | bytes 1572872 | tf_op jit(solution)/shard_map/cond/branch_3_fun/ppermute | solution.py:97
  6.6 16.9 %collective-permute-start.12 = (f32[512,256]{1,0:T(8,128)}, f32[512,256]{1,0:T(8,128)S(1)}, u32[]{:S(2)}, u32[]{:S(2)}) collective-permute-start(f32[512,256]{1,0:T(8,128)} %get-tuple-element.187), channel_id=1, source_target_pairs={{0,30},{1,31},{8,6},{9,7},{16,14},{17,15},{24,22},{25,23},{32,62},... | collective-permute-start | bytes 1572872 | tf_op jit(solution)/shard_map/cond/branch_3_fun/ppermute | solution.py:97
  9.0 13.7 %all-to-all-start.3 = ((f32[16,16,256]{2,1,0:T(8,128)}), f32[16,16,256]{2,1,0:T(8,128)S(1)}, u32[]{:S(2)}, u32[]{:S(2)}) async-start(f32[16,16,256]{2,1,0:T(8,128)} %bitcast.9), calls=%async_computation.3 | async-start | bytes 524288 | tf_op jit(solution)/shard_map/cond/branch_3_fun/all_to_all | solution.py:103
  24.8 40.9 %collective-permute-start.73 = (f32[512,256]{1,0:T(8,128)S(1)}, f32[512,256]{1,0:T(8,128)}, u32[]{:S(2)}, u32[]{:S(2)}) collective-permute-start(f32[512,256]{1,0:T(8,128)S(1)} %get-tuple-element.325), channel_id=1, source_target_pairs={{6,4},{7,5},{14,12},{15,13},{22,20},{23,21},{30,28},{31,29},{38,36... | collective-permute-start | bytes 1572872 | tf_op jit(solution)/shard_map/ppermute | solution.py:97
  26.3 11.0 %collective-permute-start.72 = (f32[512,256]{1,0:T(8,128)S(1)}, f32[512,256]{1,0:T(8,128)}, u32[]{:S(2)}, u32[]{:S(2)}) collective-permute-start(f32[512,256]{1,0:T(8,128)S(1)} %get-tuple-element.325), channel_id=1, source_target_pairs={{6,8},{7,9},{14,16},{15,17},{22,24},{23,25},{30,0},{31,1},{38,40},... | collective-permute-start | bytes 1572872 | tf_op jit(solution)/shard_map/ppermute | solution.py:97
  27.9 43.7 %all-to-all-start.20 = ((f32[16,32,256]{2,1,0:T(8,128)}), f32[16,32,256]{2,1,0:T(8,128)S(1)}, u32[]{:S(2)}, u32[]{:S(2)}) async-start(f32[16,32,256]{2,1,0:T(8,128)} %bitcast.68), calls=%async_computation.20 | async-start | bytes 1048576 | tf_op jit(solution)/shard_map/all_to_all | solution.py:103
  32.9 32.6 %collective-permute-start.74 = (f32[256,256]{1,0:T(8,128)}, f32[256,256]{1,0:T(8,128)}, u32[]{:S(2)}, u32[]{:S(2)}) collective-permute-start(f32[256,256]{1,0:T(8,128)} %get-tuple-element.355), channel_id=1, source_target_pairs={{6,10},{7,11},{14,18},{15,19},{22,26},{23,27},{30,2},{31,3},{38,42... | collective-permute-start | bytes 786440 | tf_op jit(solution)/shard_map/ppermute | solution.py:97
  34.2 31.5 %collective-permute-start.75 = (f32[256,256]{1,0:T(8,128)S(1)}, f32[256,256]{1,0:T(8,128)}, u32[]{:S(2)}, u32[]{:S(2)}) collective-permute-start(f32[256,256]{1,0:T(8,128)S(1)} %get-tuple-element.356), channel_id=1, source_target_pairs={{6,2},{7,3},{14,10},{15,11},{22,18},{23,19},{30,26},{31,27},{38,34... | collective-permute-start | bytes 786440 | tf_op jit(solution)/shard_map/ppermute | solution.py:97
  66.9 6.3 %collective-permute-start.76 = (f32[512,256]{1,0:T(8,128)S(1)}, f32[512,256]{1,0:T(8,128)}, u32[]{:S(2)}, u32[]{:S(2)}) collective-permute-start(f32[512,256]{1,0:T(8,128)S(1)} %fusion.1.mine_ref), channel_id=1, source_target_pairs={{0,1},{1,0},{2,3},{3,2},{4,5},{5,4},{6,7},{7,6},{8,9},{9,8},{10,11... | collective-permute-start | bytes 1572872 | tf_op jit(solution)/shard_map/ppermute | solution.py:170
  76.8 16.7 %collective-permute-start.71 = (f32[512,256]{1,0:T(8,128)S(1)}, f32[512,256]{1,0:T(8,128)S(1)}, u32[]{:S(2)}, u32[]{:S(2)}) collective-permute-start(f32[512,256]{1,0:T(8,128)S(1)} %get-tuple-element.283), channel_id=1, source_target_pairs={{30,14},{31,15},{62,46},{63,47},{94,78},{95,79},{126,110},{127,111... | collective-permute-start | bytes 1572872 | tf_op jit(solution)/shard_map/cond/branch_9_fun/ppermute | solution.py:97
  77.5 16.0 %collective-permute-start.70 = (f32[512,256]{1,0:T(8,128)S(1)}, f32[512,256]{1,0:T(8,128)S(1)}, u32[]{:S(2)}, u32[]{:S(2)}) collective-permute-start(f32[512,256]{1,0:T(8,128)S(1)} %get-tuple-element.283), channel_id=1, source_target_pairs={{30,6},{31,7},{62,38},{63,39},{94,70},{95,71},{126,102},{127,103},... | collective-permute-start | bytes 1572872 | tf_op jit(solution)/shard_map/cond/branch_9_fun/ppermute | solution.py:97
  78.2 15.3 %collective-permute-start.69 = (f32[512,256]{1,0:T(8,128)S(1)}, f32[512,256]{1,0:T(8,128)S(1)}, u32[]{:S(2)}, u32[]{:S(2)}) collective-permute-start(f32[512,256]{1,0:T(8,128)S(1)} %get-tuple-element.283), channel_id=1, source_target_pairs={{30,22},{31,23},{62,54},{63,55},{94,86},{95,87},{126,118},{127,119... | collective-permute-start | bytes 1572872 | tf_op jit(solution)/shard_map/cond/branch_9_fun/ppermute | solution.py:97
  78.9 13.7 %all-to-all-start.19 = ((f32[16,16,256]{2,1,0:T(8,128)}), f32[16,16,256]{2,1,0:T(8,128)S(1)}, u32[]{:S(2)}, u32[]{:S(2)}) async-start(f32[16,16,256]{2,1,0:T(8,128)} %bitcast.57), calls=%async_computation.19 | async-start | bytes 524288 | tf_op jit(solution)/shard_map/cond/branch_9_fun/all_to_all | solution.py:103
  96.2 32.8 %collective-permute-start.78 = (f32[512,256]{1,0:T(8,128)}, f32[512,256]{1,0:T(8,128)}, u32[]{:S(2)}, u32[]{:S(2)}) collective-permute-start(f32[512,256]{1,0:T(8,128)} %get-tuple-element.340), channel_id=1, source_target_pairs={{6,4},{7,5},{14,12},{15,13},{22,20},{23,21},{30,28},{31,29},{38,36... | collective-permute-start | bytes 1572872 | tf_op jit(solution)/shard_map/ppermute | solution.py:97
  97.7 11.2 %collective-permute-start.77 = (f32[512,256]{1,0:T(8,128)}, f32[512,256]{1,0:T(8,128)}, u32[]{:S(2)}, u32[]{:S(2)}) collective-permute-start(f32[512,256]{1,0:T(8,128)} %get-tuple-element.340), channel_id=1, source_target_pairs={{6,8},{7,9},{14,16},{15,17},{22,24},{23,25},{30,0},{31,1},{38,40},... | collective-permute-start | bytes 1572872 | tf_op jit(solution)/shard_map/ppermute | solution.py:97
  99.1 34.6 %all-to-all-start.21 = ((f32[16,32,256]{2,1,0:T(8,128)}), f32[16,32,256]{2,1,0:T(8,128)S(1)}, u32[]{:S(2)}, u32[]{:S(2)}) async-start(f32[16,32,256]{2,1,0:T(8,128)} %bitcast.72), calls=%async_computation.21 | async-start | bytes 1048576 | tf_op jit(solution)/shard_map/all_to_all | solution.py:103
  103.7 25.4 %collective-permute-start.79 = (f32[256,256]{1,0:T(8,128)}, f32[256,256]{1,0:T(8,128)S(1)}, u32[]{:S(2)}, u32[]{:S(2)}) collective-permute-start(f32[256,256]{1,0:T(8,128)} %get-tuple-element.353), channel_id=1, source_target_pairs={{6,10},{7,11},{14,18},{15,19},{22,26},{23,27},{30,2},{31,3},{38,42... | collective-permute-start | bytes 786440 | tf_op jit(solution)/shard_map/ppermute | solution.py:97
  104.9 24.1 %collective-permute-start.80 = (f32[256,256]{1,0:T(8,128)S(1)}, f32[256,256]{1,0:T(8,128)S(1)}, u32[]{:S(2)}, u32[]{:S(2)}) collective-permute-start(f32[256,256]{1,0:T(8,128)S(1)} %get-tuple-element.354), channel_id=1, source_target_pairs={{6,2},{7,3},{14,10},{15,11},{22,18},{23,19},{30,26},{31,27},{38,34... | collective-permute-start | bytes 786440 | tf_op jit(solution)/shard_map/ppermute | solution.py:97
  130.0 5.9 %collective-permute-start.81 = (f32[512,256]{1,0:T(8,128)}, f32[512,256]{1,0:T(8,128)}, u32[]{:S(2)}, u32[]{:S(2)}) collective-permute-start(f32[512,256]{1,0:T(8,128)} %fusion.3.mine_ref), channel_id=1, source_target_pairs={{0,1},{1,0},{2,3},{3,2},{4,5},{5,4},{6,7},{7,6},{8,9},{9,8},{10,11... | collective-permute-start | bytes 1572872 | tf_op jit(solution)/shard_map/ppermute | solution.py:170
  (2 other events, 14.1 us)

commit v7 on v6

--- a/solution.py
+++ b/solution.py
@@ -49,13 +49,20 @@
     out_ref,
     own_ref,
     cols,
+    other,
+    sems,
 ):
     size = rows_ref.shape[1]
     my_row, my_col = lax.axis_index("row"), lax.axis_index("col")
     core = my_col & 1
     first = flags[6 + step]
+    copies = []
+    for slot in range(2):
+        at = pl.ds(slot * size, size)
+        copies.append(pltpu.make_async_copy(other_ref.at[at], other.at[at], sems.at[slot]))
+        copies[slot].start()
     half = pl.ds(pl.multiple_of((1 - core) * size, size), size)
-    cols[...] = part_ref[...] + dot(split(other_ref[...]), split(upper_ref[half]))
+    upper = split(upper_ref[half])
     col_hit = flags[4 + step] > 0
     rows = rows_ref[...]
     kept = split(jnp.where(col_hit, rows, jnp.float32(0.0)))
@@ -64,6 +71,8 @@
     for slot in range(2):
         at = slice(slot * size, (slot + 1) * size)
         row_hit = flags[2 * step + slot] > 0
+        copies[slot].wait()
+        cols[at] = part_ref[at] + dot(split(other[at]), upper)
         whole = cols[at]
         masked = jnp.where(row_hit, whole, jnp.float32(0.0))
         new = block_ref[at] - dot(split(masked), kept)
@@ -103,10 +112,13 @@
         return lax.all_to_all(value, "row", 0, 0, tiled=True)
 
     def to_leaders(sends):
-        def run(block, own, chunk_at, dist):
+        def run(block, own, first):
+            dist = (my_z - (first >> 1)) & (n_z - 1)
             got = [from_class(block, place, spacing, hop) for place, spacing, hop in sends]
-            if own.ndim == 0:
-                own = lax.dynamic_slice_in_dim(block, own, size, 0)
+            if own is None:
+                own_at = (first >> (n_row.bit_length() - 1)) * size
+                own = lax.dynamic_slice_in_dim(block, own_at.astype(jnp.uint32), size, 0)
+            chunk_at = ((first & (n_row - 1)) * piece).astype(jnp.uint32)
             chunk = lax.dynamic_slice_in_dim(exchange(own), chunk_at, 2 * piece, 0)
             tiled, middle = lax.optimization_barrier((jnp.tile(chunk, (n_row, 1)), block))
             for (_, _, hop), value in zip(sends, got):
@@ -115,10 +127,15 @@
 
         return run
 
-    def fetch(step, block, own, later, which, chunk_at, dist):
-        middle, tiled = lax.switch(which, leads, block, own, chunk_at, dist)
+    def fetch(step, block, own, later):
+        first = later[3][step]
+        plane = first >> 1
+        which = jnp.where(
+            plane & 3 == 3, 6 + (plane >> 2), (plane & 3) + 3 * ((plane >> 2) & 1)
+        )
+        middle, tiled = lax.switch(which, leads, block, own, first)
         tiled, later = lax.optimization_barrier((tiled, later))
-        later = later[0][step], later[1][step], later[2]
+        later = later[0][step], later[1][step], later[2], later[3]
         up = from_class(middle, 3, 4, 1)
         down = from_class(middle, 3, 4, -1)
         top = from_class(middle[:size], 3, 4, 2)
@@ -141,6 +158,7 @@
         leads.append(to_leaders([(place, n_z, hop) for hop in (8, 4, -4)]))
     whole = pl.BlockSpec(memory_space=pltpu.VMEM)
     scalars = pl.BlockSpec(memory_space=pltpu.SMEM)
+    outside = pl.BlockSpec(memory_space=pl.ANY)
     params = pltpu.CompilerParams(vmem_limit_bytes=VMEM_BYTES)
     cost = pl.CostEstimate(
         flops=6 * width * width * width, bytes_accessed=12 * width * width, transcendentals=0
@@ -148,25 +166,10 @@
     f32 = jnp.float32
     flags = jnp.concatenate([row_struct.reshape(-1), col_struct.reshape(-1), panel_index])
 
-    places = []
+    block, own, panels = matrix, None, panel_index
     for step in range(panel_index.shape[0]):
-        first = panel_index[step]
-        plane = first >> 1
-        dist = (my_z - plane) & (n_z - 1)
-        places += [
-            jnp.where(plane & 3 == 3, 6 + (plane >> 2), (plane & 3) + 3 * ((plane & 7) >> 2)),
-            (first & (n_row - 1)) * piece,
-            dist,
-        ]
-    own_at = (panel_index[0] >> (n_row.bit_length() - 1)) * size
-    places, own = lax.optimization_barrier((places, own_at))
-
-    block = matrix
-    for step in range(panel_index.shape[0]):
-        later = lower_inv, upper_inv, flags
-        mine, gathered, (lower, upper, flags) = fetch(
-            step, block, own, later, *places[3 * step : 3 * step + 3]
-        )
+        later = lower_inv, upper_inv, flags, panels
+        mine, gathered, (lower, upper, flags, panels) = fetch(step, block, own, later)
         other = lax.ppermute(mine, "col", [(i, i ^ 1) for i in range(n_col)])
         rows, part = pl.pallas_call(
             functools.partial(early_kernel, n_row),
@@ -187,9 +190,13 @@
                 pltpu.VMEM(matrix.shape, f32),
                 pltpu.VMEM((size, size), f32),
             ),
-            in_specs=[scalars] + [whole] * 5,
+            in_specs=[scalars, outside] + [whole] * 4,
             out_specs=(whole, whole),
-            scratch_shapes=[pltpu.VMEM((2 * size, width), f32)],
+            scratch_shapes=[
+                pltpu.VMEM((2 * size, width), f32),
+                pltpu.VMEM((2 * size, size), f32),
+                pltpu.SemaphoreType.DMA((2,)),
+            ],
             compiler_params=params,
             cost_estimate=cost,
             name="late",

time: 141 us -> 139 us (0.986)
  waiting for transfers between devices: 63.1 us -> 58.8 us
  loops' own time: 0.14 us -> 3.27 us
  between operations: 3.34 us -> 1.46 us
  Pallas kernels: 9.99 us -> 11.4 us
    another operation x2, loops' own time: 0.14 us -> 3.27 us  [fetch(): middle, tiled = lax.switch(which, leads, block, own, first)]
    all_to_all x4, waiting for transfers between devices: 13.8 us -> 11.5 us  [exchange(): return lax.all_to_all(value, 'row', 0, 0, tiled=True)]
    ppermute x15, waiting for transfers between devices: 48.7 us -> 47.3 us  [send_z(): return lax.ppermute(value, 'col', pairs)]
    pallas_call x2, Pallas kernels: 6.88 us -> 8.3 us  [local(): pl.pallas_call(functools.partial(late_kernel, n_row, step, panel_index.sh...]
  transfers between devices with their start and end apart: 21 -> 21, of which waited for: 6 -> 4; matrix products, arithmetic and copies ran while one was open for 8% -> 9% of each run, Pallas kernels for 2% -> 2%
where the time goes in v7:
time: 139 us; the launch traced here: 138 us
  waiting for transfers between devices  58.8 us (42%)
  starting transfers between devices  46.4 us (33%)
  local copies, waits for them, and re-layouts  11.7 us (8%)
  Pallas kernels  11.4 us (8%)
  other arithmetic  5 us (4%)
  loops' own time  3.27 us (2%)
  between operations  1.46 us (1%)
    ppermute x15, waiting for transfers between devices, send_z(): return lax.ppermute(value, 'col', pairs)  47.3 us
    all_to_all x4, starting transfers between devices, exchange(): return lax.all_to_all(value, 'row', 0, 0, tiled=True)  22.9 us
    ppermute x15, starting transfers between devices, send_z(): return lax.ppermute(value, 'col', pairs)  15.8 us
    all_to_all x4, waiting for transfers between devices, exchange(): return lax.all_to_all(value, 'row', 0, 0, tiled=True)  11.5 us
    pallas_call x2, Pallas kernels, local(): pl.pallas_call(functools.partial(late_kernel, n_row, step, panel_index.sh...  8.3 us
    ppermute x2, starting transfers between devices, local(): other = lax.ppermute(mine, 'col', [(i, i ^ 1) for i in range(n_col)])  7.66 us
    squeeze x3, local copies, waits for them, and re-layouts, fetch(): later = (later[0][step], later[1][step], later[2], later[3])  4.31 us
    another operation x2, loops' own time, fetch(): middle, tiled = lax.switch(which, leads, block, own, first)  3.27 us
  transfers between devices with their start and end apart: 21, of which 4 were waited for; matrix products, arithmetic and copies ran while one was open for 9% of the time, Pallas kernels for 2%

profile of v7, /device:TPU:35, one launch (start us, length us, event | category | flops | bytes accessed | tf_op | source)
XLA Modules:
  0.0 138.0 jit_solution(1510785535519587701)
XLA Ops:
  0.7 21.0 %conditional.2 = (f32[512,256]{1,0:T(8,128)S(1)}, f32[512,256]{1,0:T(8,128)}) conditional(s32[]{:T(128)} %clamp.6, (s32[]{:T(128)}, s32[]{:T(128)}, f32[512,256]{1,0:T(8,128)}) %tuple.139, (s32[]{:T(128)}, s32[]{:T(128)}, f32[512,256]{1,0:T(8,128)}) %tuple.140, (s32[]{:T(128)}, s32[]{:T(128)}, ...), branch_computations={%region_0.1_spmd, %region_1.2_spmd, %region_2.3_spmd, %region_3.4_... | conditional | flops 524301 | bytes 13468004 | solution.py:136
  4.2 1.7 %constant_dynamic-slice_fusion.1 = f32[256,256]{1,0:T(8,128)} fusion(f32[512,256]{1,0:T(8,128)} %get-tuple-element.148, u32[]{:T(128)S(6)} %convert_element_type.60), kind=kLoop, calls=%fused_computation.2 | loop fusion | bytes 524292 | tf_op jit(solution)/shard_map/cond/branch_0_fun/dynamic_slice | solution.py:120
  5.8 6.9 %all-to-all-start = ((f32[16,16,256]{2,1,0:T(8,128)}), f32[16,16,256]{2,1,0:T(8,128)S(1)}, u32[]{:S(2)}, u32[]{:S(2)}) async-start(f32[16,16,256]{2,1,0:T(8,128)} %bitcast), calls=%async_computation | async-start | bytes 524288 | tf_op jit(solution)/shard_map/cond/branch_0_fun/all_to_all | solution.py:112
  14.1 5.4 %all-to-all-done = f32[16,16,256]{2,1,0:T(8,128)S(1)} async-done(((f32[16,16,256]{2,1,0:T(8,128)}), f32[16,16,256]{2,1,0:T(8,128)S(1)}, u32[]{:S(2)}, u32[]{:S(2)}) %all-to-all-start) | async-done | bytes 262176 | tf_op jit(solution)/shard_map/cond/branch_0_fun/all_to_all | solution.py:112
  21.7 1.5 %collective-permute-start.73 = (f32[512,256]{1,0:T(8,128)S(1)}, f32[512,256]{1,0:T(8,128)}, u32[]{:S(2)}, u32[]{:S(2)}) collective-permute-start(f32[512,256]{1,0:T(8,128)S(1)} %get-tuple-element.284), channel_id=1, source_target_pairs={{6,4},{7,5},{14,12},{15,13},{22,20},{23,21},{30,28},{31,29},{38,36... | collective-permute-start | bytes 1572872 | tf_op jit(solution)/shard_map/ppermute | solution.py:106
  23.1 1.5 %collective-permute-start.72 = (f32[512,256]{1,0:T(8,128)S(1)}, f32[512,256]{1,0:T(8,128)}, u32[]{:S(2)}, u32[]{:S(2)}) collective-permute-start(f32[512,256]{1,0:T(8,128)S(1)} %get-tuple-element.284), channel_id=1, source_target_pairs={{6,8},{7,9},{14,16},{15,17},{22,24},{23,25},{30,0},{31,1},{38,40},... | collective-permute-start | bytes 1572872 | tf_op jit(solution)/shard_map/ppermute | solution.py:106
  25.4 4.2 %all-to-all-start.20 = ((f32[16,32,256]{2,1,0:T(8,128)}), f32[16,32,256]{2,1,0:T(8,128)S(1)}, u32[]{:S(2)}, u32[]{:S(2)}) async-start(f32[16,32,256]{2,1,0:T(8,128)} %bitcast.65), calls=%async_computation.20 | async-start | bytes 1048576 | tf_op jit(solution)/shard_map/all_to_all | solution.py:112
  33.0 1.7 %slice_bitcast_fusion.2 = (f32[512,512]{1,0:T(8,128)S(1)}, f32[512,512]{1,0:T(8,128)S(1)}) fusion(f32[2,512,512]{2,1,0:T(8,128)} %param.31, f32[2,512,512]{2,1,0:T(8,128)} %param.30), kind=kLoop, calls=%fused_computation.52 | loop fusion | bytes 4194304 | tf_op jit(solution)/shard_map/squeeze | solution.py:138
  34.7 26.6 %collective-permute-done.74 = f32[256,256]{1,0:T(8,128)} collective-permute-done((f32[256,256]{1,0:T(8,128)}, f32[256,256]{1,0:T(8,128)}, u32[]{:S(2)}, u32[]{:S(2)}) %collective-permute-start.74) | collective-permute-done | bytes 262176 | tf_op jit(solution)/shard_map/ppermute | solution.py:106
  62.6 4.4 %collective-permute-start.76 = (f32[512,256]{1,0:T(8,128)S(1)}, f32[512,256]{1,0:T(8,128)}, u32[]{:S(2)}, u32[]{:S(2)}) collective-permute-start(f32[512,256]{1,0:T(8,128)S(1)} %fusion.1.mine_ref), channel_id=1, source_target_pairs={{0,1},{1,0},{2,3},{3,2},{4,5},{5,4},{6,7},{7,6},{8,9},{9,8},{10,11... | collective-permute-start | bytes 1572872 | tf_op jit(solution)/shard_map/ppermute | solution.py:173
  69.2 4.1 %late.2 = (f32[512,256]{1,0:T(8,128)S(1)}, f32[256,256]{1,0:T(8,128)}) custom-call(s32[8]{0:T(128)S(1)} %pad_add_fusion.flags, f32[512,256]{1,0:T(8,128)} %collective-permute-done.76.other_ref, f32[512,512]{1,0:T(8,128)S(1)} %get-tuple-element.296.part_ref, f32[512,256]{1,0:T(8,128)S(1)} %get-tuple-element.297.rows_ref, ...), custom_call_target="tpu_custom_call" | custom-call | flops 805306368 | bytes 3145728 | tf_op jit(solution)/shard_map/late/pallas_call | solution.py:187
  73.4 18.0 %conditional.3 = (f32[512,256]{1,0:T(8,128)}, f32[512,256]{1,0:T(8,128)}) conditional(s32[]{:T(128)} %clamp.7, (s32[]{:T(128)}, s32[]{:T(128)}, f32[512,256]{1,0:T(8,128)S(1)}, f32[256,256]{1,0:T(8,128)}) %tuple.113, (s32[]{:T(128)}, s32[]{:T(128)}, f32[512,256]{1,0:T(8,128)S(1)}, f32[256,256]{1,0:T(8,128)}) %tuple.113, ...), branch_computations={%region_10.11_spmd, %region_11.12_spmd, %region_12.13_spmd, %regio... | conditional | flops 524298 | bytes 12943680 | solution.py:136
  75.5 6.9 %all-to-all-start.19 = ((f32[16,16,256]{2,1,0:T(8,128)}), f32[16,16,256]{2,1,0:T(8,128)S(1)}, u32[]{:S(2)}, u32[]{:S(2)}) async-start(f32[16,16,256]{2,1,0:T(8,128)} %bitcast.57), calls=%async_computation.19 | async-start | bytes 524288 | tf_op jit(solution)/shard_map/cond/branch_9_fun/all_to_all | solution.py:112
  83.6 6.0 %all-to-all-done.19 = f32[16,16,256]{2,1,0:T(8,128)S(1)} async-done(((f32[16,16,256]{2,1,0:T(8,128)}), f32[16,16,256]{2,1,0:T(8,128)S(1)}, u32[]{:S(2)}, u32[]{:S(2)}) %all-to-all-start.19) | async-done | bytes 262176 | tf_op jit(solution)/shard_map/cond/branch_9_fun/all_to_all | solution.py:112
  91.4 1.8 %fusion.4 = (f32[256,256]{1,0:T(8,128)}, f32[256,256]{1,0:T(8,128)S(1)}) fusion(f32[512,256]{1,0:T(8,128)} %get-tuple-element.300), kind=kLoop, calls=%fused_computation.61 | loop fusion | bytes 1048576 | tf_op jit(solution)/shard_map/slice | solution.py:141
  93.2 1.5 %collective-permute-start.78 = (f32[512,256]{1,0:T(8,128)}, f32[512,256]{1,0:T(8,128)}, u32[]{:S(2)}, u32[]{:S(2)}) collective-permute-start(f32[512,256]{1,0:T(8,128)} %get-tuple-element.300), channel_id=1, source_target_pairs={{6,4},{7,5},{14,12},{15,13},{22,20},{23,21},{30,28},{31,29},{38,36... | collective-permute-start | bytes 1572872 | tf_op jit(solution)/shard_map/ppermute | solution.py:106
  94.6 1.4 %collective-permute-start.77 = (f32[512,256]{1,0:T(8,128)}, f32[512,256]{1,0:T(8,128)}, u32[]{:S(2)}, u32[]{:S(2)}) collective-permute-start(f32[512,256]{1,0:T(8,128)} %get-tuple-element.300), channel_id=1, source_target_pairs={{6,8},{7,9},{14,16},{15,17},{22,24},{23,25},{30,0},{31,1},{38,40},... | collective-permute-start | bytes 1572872 | tf_op jit(solution)/shard_map/ppermute | solution.py:106
  96.1 4.8 %all-to-all-start.21 = ((f32[16,32,256]{2,1,0:T(8,128)}), f32[16,32,256]{2,1,0:T(8,128)S(1)}, u32[]{:S(2)}, u32[]{:S(2)}) async-start(f32[16,32,256]{2,1,0:T(8,128)} %bitcast.69), calls=%async_computation.21 | async-start | bytes 1048576 | tf_op jit(solution)/shard_map/all_to_all | solution.py:112
  103.5 1.3 slice_bitcast_fusion.1.lower_ref
  104.8 1.3 slice_bitcast_fusion.upper_ref
  106.1 20.6 %collective-permute-done.79 = f32[256,256]{1,0:T(8,128)S(1)} collective-permute-done((f32[256,256]{1,0:T(8,128)}, f32[256,256]{1,0:T(8,128)S(1)}, u32[]{:S(2)}, u32[]{:S(2)}) %collective-permute-start.79) | collective-permute-done | bytes 262176 | tf_op jit(solution)/shard_map/ppermute | solution.py:106
  127.7 3.3 %collective-permute-start.81 = (f32[512,256]{1,0:T(8,128)}, f32[512,256]{1,0:T(8,128)}, u32[]{:S(2)}, u32[]{:S(2)}) collective-permute-start(f32[512,256]{1,0:T(8,128)} %fusion.3.mine_ref), channel_id=1, source_target_pairs={{0,1},{1,0},{2,3},{3,2},{4,5},{5,4},{6,7},{7,6},{8,9},{9,8},{10,11... | collective-permute-start | bytes 1572872 | tf_op jit(solution)/shard_map/ppermute | solution.py:173
  130.9 2.1 %early.3 = (f32[512,256]{1,0:T(8,128)S(1)}, f32[512,512]{1,0:T(8,128)S(1)}) custom-call(f32[512,256]{1,0:T(8,128)S(1)} %bitcast.77, f32[512,256]{1,0:T(8,128)} %fusion.3.mine_ref, f32[512,512]{1,0:T(8,128)S(1)} %slice_bitcast_fusion.1.lower_ref, f32[512,512]{1,0:T(8,128)S(1)} %slice_bitcast_fusion.upper_ref), custom_call_target="tpu_custom_call" | custom-call | flops 805306368 | bytes 3145728 | tf_op jit(solution)/shard_map/early/pallas_call | solution.py:174
  133.0 4.2 %late.3 = (f32[512,256]{1,0:T(8,128)S(1)}, f32[256,256]{1,0:T(8,128)}) custom-call(s32[8]{0:T(128)S(1)} %pad_add_fusion.flags, f32[512,256]{1,0:T(8,128)} %collective-permute-done.81.other_ref, f32[512,512]{1,0:T(8,128)S(1)} %get-tuple-element.310.part_ref, f32[512,256]{1,0:T(8,128)S(1)} %get-tuple-element.311.rows_ref, ...), custom_call_target="tpu_custom_call" | custom-call | flops 805306368 | bytes 3145728 | tf_op jit(solution)/shard_map/late/pallas_call | solution.py:187
  (52 shorter events, 20.0 us)
Async XLA Ops:
  0.7 23.9 %copy-start.4 = (s32[2,2]{1,0:T(2,128)S(1)}, s32[2,2]{1,0:T(2,128)}, u32[]{:S(2)}) copy-start(s32[2,2]{1,0:T(2,128)} %param.27) | copy-start | bytes 52
  0.7 24.0 %copy-start.2 = (s32[2,1]{0,1:T(1,128)S(1)}, s32[2,1]{0,1:T(1,128)}, u32[]{:S(2)}) copy-start(s32[2,1]{0,1:T(1,128)} %param.28) | copy-start | bytes 28
  0.7 19.7 %collective-permute-start.3 = (f32[512,256]{1,0:T(8,128)}, f32[512,256]{1,0:T(8,128)S(1)}, u32[]{:S(2)}, u32[]{:S(2)}) collective-permute-start(f32[512,256]{1,0:T(8,128)} %get-tuple-element.148), channel_id=1, source_target_pairs={{0,14},{1,15},{16,30},{17,31},{32,46},{33,47},{48,62},{49,63},{64,... | collective-permute-start | bytes 1572872 | tf_op jit(solution)/shard_map/cond/branch_0_fun/ppermute | solution.py:106
  1.4 19.0 %collective-permute-start.2 = (f32[512,256]{1,0:T(8,128)}, f32[512,256]{1,0:T(8,128)S(1)}, u32[]{:S(2)}, u32[]{:S(2)}) collective-permute-start(f32[512,256]{1,0:T(8,128)} %get-tuple-element.148), channel_id=1, source_target_pairs={{0,22},{1,23},{16,6},{17,7},{32,54},{33,55},{48,38},{49,39},{64,86... | collective-permute-start | bytes 1572872 | tf_op jit(solution)/shard_map/cond/branch_0_fun/ppermute | solution.py:106
  2.1 18.3 %collective-permute-start.1 = (f32[512,256]{1,0:T(8,128)}, f32[512,256]{1,0:T(8,128)S(1)}, u32[]{:S(2)}, u32[]{:S(2)}) collective-permute-start(f32[512,256]{1,0:T(8,128)} %get-tuple-element.148), channel_id=1, source_target_pairs={{0,6},{1,7},{8,14},{9,15},{16,22},{17,23},{24,30},{25,31},{32,38},... | collective-permute-start | bytes 1572872 | tf_op jit(solution)/shard_map/cond/branch_0_fun/ppermute | solution.py:106
  2.8 17.6 %collective-permute-start = (f32[512,256]{1,0:T(8,128)}, f32[512,256]{1,0:T(8,128)S(1)}, u32[]{:S(2)}, u32[]{:S(2)}) collective-permute-start(f32[512,256]{1,0:T(8,128)} %get-tuple-element.148), channel_id=1, source_target_pairs={{0,30},{1,31},{8,6},{9,7},{16,14},{17,15},{24,22},{25,23},{32,62},... | collective-permute-start | bytes 1572872 | tf_op jit(solution)/shard_map/cond/branch_0_fun/ppermute | solution.py:106
  5.8 13.7 %all-to-all-start = ((f32[16,16,256]{2,1,0:T(8,128)}), f32[16,16,256]{2,1,0:T(8,128)S(1)}, u32[]{:S(2)}, u32[]{:S(2)}) async-start(f32[16,16,256]{2,1,0:T(8,128)} %bitcast), calls=%async_computation | async-start | bytes 524288 | tf_op jit(solution)/shard_map/cond/branch_0_fun/all_to_all | solution.py:112
  21.7 39.7 %collective-permute-start.73 = (f32[512,256]{1,0:T(8,128)S(1)}, f32[512,256]{1,0:T(8,128)}, u32[]{:S(2)}, u32[]{:S(2)}) collective-permute-start(f32[512,256]{1,0:T(8,128)S(1)} %get-tuple-element.284), channel_id=1, source_target_pairs={{6,4},{7,5},{14,12},{15,13},{22,20},{23,21},{30,28},{31,29},{38,36... | collective-permute-start | bytes 1572872 | tf_op jit(solution)/shard_map/ppermute | solution.py:106
  23.1 11.6 %collective-permute-start.72 = (f32[512,256]{1,0:T(8,128)S(1)}, f32[512,256]{1,0:T(8,128)}, u32[]{:S(2)}, u32[]{:S(2)}) collective-permute-start(f32[512,256]{1,0:T(8,128)S(1)} %get-tuple-element.284), channel_id=1, source_target_pairs={{6,8},{7,9},{14,16},{15,17},{22,24},{23,25},{30,0},{31,1},{38,40},... | collective-permute-start | bytes 1572872 | tf_op jit(solution)/shard_map/ppermute | solution.py:106
  25.4 42.8 %all-to-all-start.20 = ((f32[16,32,256]{2,1,0:T(8,128)}), f32[16,32,256]{2,1,0:T(8,128)S(1)}, u32[]{:S(2)}, u32[]{:S(2)}) async-start(f32[16,32,256]{2,1,0:T(8,128)} %bitcast.65), calls=%async_computation.20 | async-start | bytes 1048576 | tf_op jit(solution)/shard_map/all_to_all | solution.py:112
  30.4 31.0 %collective-permute-start.74 = (f32[256,256]{1,0:T(8,128)}, f32[256,256]{1,0:T(8,128)}, u32[]{:S(2)}, u32[]{:S(2)}) collective-permute-start(f32[256,256]{1,0:T(8,128)} %get-tuple-element.315), channel_id=1, source_target_pairs={{6,10},{7,11},{14,18},{15,19},{22,26},{23,27},{30,2},{31,3},{38,42... | collective-permute-start | bytes 786440 | tf_op jit(solution)/shard_map/ppermute | solution.py:106
  31.7 29.7 %collective-permute-start.75 = (f32[256,256]{1,0:T(8,128)S(1)}, f32[256,256]{1,0:T(8,128)}, u32[]{:S(2)}, u32[]{:S(2)}) collective-permute-start(f32[256,256]{1,0:T(8,128)S(1)} %get-tuple-element.316), channel_id=1, source_target_pairs={{6,2},{7,3},{14,10},{15,11},{22,18},{23,19},{30,26},{31,27},{38,34... | collective-permute-start | bytes 786440 | tf_op jit(solution)/shard_map/ppermute | solution.py:106
  34.7 32.3 %copy-start.3 = (s32[2]{0:T(128)S(1)}, s32[2]{0:T(128)}, u32[]{:S(2)}) copy-start(s32[2]{0:T(128)} %param.29) | copy-start | bytes 28
  62.6 6.6 %collective-permute-start.76 = (f32[512,256]{1,0:T(8,128)S(1)}, f32[512,256]{1,0:T(8,128)}, u32[]{:S(2)}, u32[]{:S(2)}) collective-permute-start(f32[512,256]{1,0:T(8,128)S(1)} %fusion.1.mine_ref), channel_id=1, source_target_pairs={{0,1},{1,0},{2,3},{3,2},{4,5},{5,4},{6,7},{7,6},{8,9},{9,8},{10,11... | collective-permute-start | bytes 1572872 | tf_op jit(solution)/shard_map/ppermute | solution.py:173
  73.4 17.0 %collective-permute-start.71 = (f32[512,256]{1,0:T(8,128)S(1)}, f32[512,256]{1,0:T(8,128)S(1)}, u32[]{:S(2)}, u32[]{:S(2)}) collective-permute-start(f32[512,256]{1,0:T(8,128)S(1)} %get-tuple-element.253), channel_id=1, source_target_pairs={{30,14},{31,15},{62,46},{63,47},{94,78},{95,79},{126,110},{127,111... | collective-permute-start | bytes 1572872 | tf_op jit(solution)/shard_map/cond/branch_9_fun/ppermute | solution.py:106
  74.1 16.3 %collective-permute-start.70 = (f32[512,256]{1,0:T(8,128)S(1)}, f32[512,256]{1,0:T(8,128)S(1)}, u32[]{:S(2)}, u32[]{:S(2)}) collective-permute-start(f32[512,256]{1,0:T(8,128)S(1)} %get-tuple-element.253), channel_id=1, source_target_pairs={{30,6},{31,7},{62,38},{63,39},{94,70},{95,71},{126,102},{127,103},... | collective-permute-start | bytes 1572872 | tf_op jit(solution)/shard_map/cond/branch_9_fun/ppermute | solution.py:106
  74.8 15.6 %collective-permute-start.69 = (f32[512,256]{1,0:T(8,128)S(1)}, f32[512,256]{1,0:T(8,128)S(1)}, u32[]{:S(2)}, u32[]{:S(2)}) collective-permute-start(f32[512,256]{1,0:T(8,128)S(1)} %get-tuple-element.253), channel_id=1, source_target_pairs={{30,22},{31,23},{62,54},{63,55},{94,86},{95,87},{126,118},{127,119... | collective-permute-start | bytes 1572872 | tf_op jit(solution)/shard_map/cond/branch_9_fun/ppermute | solution.py:106
  75.5 14.1 %all-to-all-start.19 = ((f32[16,16,256]{2,1,0:T(8,128)}), f32[16,16,256]{2,1,0:T(8,128)S(1)}, u32[]{:S(2)}, u32[]{:S(2)}) async-start(f32[16,16,256]{2,1,0:T(8,128)} %bitcast.57), calls=%async_computation.19 | async-start | bytes 524288 | tf_op jit(solution)/shard_map/cond/branch_9_fun/all_to_all | solution.py:112
  93.2 33.5 %collective-permute-start.78 = (f32[512,256]{1,0:T(8,128)}, f32[512,256]{1,0:T(8,128)}, u32[]{:S(2)}, u32[]{:S(2)}) collective-permute-start(f32[512,256]{1,0:T(8,128)} %get-tuple-element.300), channel_id=1, source_target_pairs={{6,4},{7,5},{14,12},{15,13},{22,20},{23,21},{30,28},{31,29},{38,36... | collective-permute-start | bytes 1572872 | tf_op jit(solution)/shard_map/ppermute | solution.py:106
  94.6 11.5 %collective-permute-start.77 = (f32[512,256]{1,0:T(8,128)}, f32[512,256]{1,0:T(8,128)}, u32[]{:S(2)}, u32[]{:S(2)}) collective-permute-start(f32[512,256]{1,0:T(8,128)} %get-tuple-element.300), channel_id=1, source_target_pairs={{6,8},{7,9},{14,16},{15,17},{22,24},{23,25},{30,0},{31,1},{38,40},... | collective-permute-start | bytes 1572872 | tf_op jit(solution)/shard_map/ppermute | solution.py:106
  96.1 34.9 %all-to-all-start.21 = ((f32[16,32,256]{2,1,0:T(8,128)}), f32[16,32,256]{2,1,0:T(8,128)S(1)}, u32[]{:S(2)}, u32[]{:S(2)}) async-start(f32[16,32,256]{2,1,0:T(8,128)} %bitcast.69), calls=%async_computation.21 | async-start | bytes 1048576 | tf_op jit(solution)/shard_map/all_to_all | solution.py:112
  100.9 25.8 %collective-permute-start.79 = (f32[256,256]{1,0:T(8,128)}, f32[256,256]{1,0:T(8,128)S(1)}, u32[]{:S(2)}, u32[]{:S(2)}) collective-permute-start(f32[256,256]{1,0:T(8,128)} %get-tuple-element.313), channel_id=1, source_target_pairs={{6,10},{7,11},{14,18},{15,19},{22,26},{23,27},{30,2},{31,3},{38,42... | collective-permute-start | bytes 786440 | tf_op jit(solution)/shard_map/ppermute | solution.py:106
  102.2 24.5 %collective-permute-start.80 = (f32[256,256]{1,0:T(8,128)S(1)}, f32[256,256]{1,0:T(8,128)S(1)}, u32[]{:S(2)}, u32[]{:S(2)}) collective-permute-start(f32[256,256]{1,0:T(8,128)S(1)} %get-tuple-element.314), channel_id=1, source_target_pairs={{6,2},{7,3},{14,10},{15,11},{22,18},{23,19},{30,26},{31,27},{38,34... | collective-permute-start | bytes 786440 | tf_op jit(solution)/shard_map/ppermute | solution.py:106
  127.7 5.4 %collective-permute-start.81 = (f32[512,256]{1,0:T(8,128)}, f32[512,256]{1,0:T(8,128)}, u32[]{:S(2)}, u32[]{:S(2)}) collective-permute-start(f32[512,256]{1,0:T(8,128)} %fusion.3.mine_ref), channel_id=1, source_target_pairs={{0,1},{1,0},{2,3},{3,2},{4,5},{5,4},{6,7},{7,6},{8,9},{9,8},{10,11... | collective-permute-start | bytes 1572872 | tf_op jit(solution)/shard_map/ppermute | solution.py:173
  (2 other events, 14.1 us)

commit v8 on v7

--- a/solution.py
+++ b/solution.py
@@ -47,22 +47,15 @@
     upper_ref,
     block_ref,
     out_ref,
-    own_ref,
-    cols,
-    other,
-    sems,
+    *rest,
 ):
+    own_ref, cols = rest if step + 1 < n_steps else (None, *rest)
     size = rows_ref.shape[1]
     my_row, my_col = lax.axis_index("row"), lax.axis_index("col")
     core = my_col & 1
     first = flags[6 + step]
-    copies = []
-    for slot in range(2):
-        at = pl.ds(slot * size, size)
-        copies.append(pltpu.make_async_copy(other_ref.at[at], other.at[at], sems.at[slot]))
-        copies[slot].start()
     half = pl.ds(pl.multiple_of((1 - core) * size, size), size)
-    upper = split(upper_ref[half])
+    cols[...] = part_ref[...] + dot(split(other_ref[...]), split(upper_ref[half]))
     col_hit = flags[4 + step] > 0
     rows = rows_ref[...]
     kept = split(jnp.where(col_hit, rows, jnp.float32(0.0)))
@@ -71,8 +64,6 @@
     for slot in range(2):
         at = slice(slot * size, (slot + 1) * size)
         row_hit = flags[2 * step + slot] > 0
-        copies[slot].wait()
-        cols[at] = part_ref[at] + dot(split(other[at]), upper)
         whole = cols[at]
         masked = jnp.where(row_hit, whole, jnp.float32(0.0))
         new = block_ref[at] - dot(split(masked), kept)
@@ -87,9 +78,11 @@
             new = jnp.where(here, rows[member * size : (member + 1) * size], new)
         out_ref[at] = new
 
-        @pl.when(next_slot == slot)
-        def _():
-            own_ref[...] = out_ref[at]
+        if own_ref is not None:
+
+            @pl.when(next_slot == slot)
+            def _():
+                own_ref[...] = out_ref[at]
 
 
 def local(matrix, row_struct, col_struct, panel_index, lower_inv, upper_inv):
@@ -158,7 +151,6 @@
         leads.append(to_leaders([(place, n_z, hop) for hop in (8, 4, -4)]))
     whole = pl.BlockSpec(memory_space=pltpu.VMEM)
     scalars = pl.BlockSpec(memory_space=pltpu.SMEM)
-    outside = pl.BlockSpec(memory_space=pl.ANY)
     params = pltpu.CompilerParams(vmem_limit_bytes=VMEM_BYTES)
     cost = pl.CostEstimate(
         flops=6 * width * width * width, bytes_accessed=12 * width * width, transcendentals=0
@@ -184,23 +176,24 @@
             cost_estimate=cost,
             name="early",
         )(gathered, mine, lower, upper)
-        block, own = pl.pallas_call(
-            functools.partial(late_kernel, n_row, step, panel_index.shape[0]),
+        n_steps = panel_index.shape[0]
+        n_out = 2 if step + 1 < n_steps else 1
+        block, *own = pl.pallas_call(
+            functools.partial(late_kernel, n_row, step, n_steps),
             out_shape=(
-                pltpu.VMEM(matrix.shape, f32),
-                pltpu.VMEM((size, size), f32),
-            ),
-            in_specs=[scalars, outside] + [whole] * 4,
-            out_specs=(whole, whole),
+                jax.ShapeDtypeStruct(matrix.shape, f32),
+                jax.ShapeDtypeStruct((size, size), f32),
+            )[:n_out],
+            in_specs=[scalars] + [whole] * 5,
+            out_specs=(whole, whole)[:n_out],
             scratch_shapes=[
                 pltpu.VMEM((2 * size, width), f32),
-                pltpu.VMEM((2 * size, size), f32),
-                pltpu.SemaphoreType.DMA((2,)),
             ],
             compiler_params=params,
             cost_estimate=cost,
             name="late",
         )(flags, other, part, rows, upper, block)
+        own = own[0] if own else None
     return block
 
 

time: 139 us -> 134 us (0.964)
  Pallas kernels: 11.4 us -> 8.88 us
  local copies, waits for them, and re-layouts: 11.7 us -> 9.98 us
    pallas_call x2, Pallas kernels: 8.3 us -> 6.83 us  [local(): pl.pallas_call(functools.partial(late_kernel, n_row, step, n_steps), out_...]
  transfers between devices with their start and end apart: 21 -> 21, of which waited for: 4 -> 5; matrix products, arithmetic and copies ran while one was open for 9% -> 8% of each run, Pallas kernels for 2% -> 2%
where the time goes in v8:
time: 134 us; the launch traced here: 133 us
  waiting for transfers between devices  58.9 us (44%)
  starting transfers between devices  46.2 us (34%)
  local copies, waits for them, and re-layouts  9.98 us (7%)
  Pallas kernels  8.88 us (7%)
  other arithmetic  4.47 us (3%)
  loops' own time  3.27 us (2%)
  between operations  1.48 us (1%)
    ppermute x15, waiting for transfers between devices, send_z(): return lax.ppermute(value, 'col', pairs)  46.8 us
    all_to_all x4, starting transfers between devices, exchange(): return lax.all_to_all(value, 'row', 0, 0, tiled=True)  22.9 us
    ppermute x15, starting transfers between devices, send_z(): return lax.ppermute(value, 'col', pairs)  15.8 us
    all_to_all x4, waiting for transfers between devices, exchange(): return lax.all_to_all(value, 'row', 0, 0, tiled=True)  11.4 us
    ppermute x2, starting transfers between devices, local(): other = lax.ppermute(mine, 'col', [(i, i ^ 1) for i in range(n_col)])  7.49 us
    pallas_call x2, Pallas kernels, local(): pl.pallas_call(functools.partial(late_kernel, n_row, step, n_steps), out_...  6.83 us
    squeeze x3, local copies, waits for them, and re-layouts, fetch(): later = (later[0][step], later[1][step], later[2], later[3])  4.31 us
    another operation x2, loops' own time, fetch(): middle, tiled = lax.switch(which, leads, block, own, first)  3.27 us
  transfers between devices with their start and end apart: 21, of which 5 were waited for; matrix products, arithmetic and copies ran while one was open for 8% of the time, Pallas kernels for 2%

profile of v8, /device:TPU:35, one launch (start us, length us, event | category | flops | bytes accessed | tf_op | source)
XLA Modules:
  0.0 133.2 jit_solution(1375806640094652654)
XLA Ops:
  0.7 20.2 %conditional.2 = (f32[512,256]{1,0:T(8,128)S(1)}, f32[512,256]{1,0:T(8,128)}) conditional(s32[]{:T(128)} %clamp.6, (s32[]{:T(128)}, s32[]{:T(128)}, f32[512,256]{1,0:T(8,128)}) %tuple.139, (s32[]{:T(128)}, s32[]{:T(128)}, f32[512,256]{1,0:T(8,128)}) %tuple.140, (s32[]{:T(128)}, s32[]{:T(128)}, ...), branch_computations={%region_0.1_spmd, %region_1.2_spmd, %region_2.3_spmd, %region_3.4_... | conditional | flops 524301 | bytes 13468004 | solution.py:129
  3.5 1.7 %constant_dynamic-slice_fusion.19 = f32[256,256]{1,0:T(8,128)} fusion(f32[512,256]{1,0:T(8,128)} %get-tuple-element.193, u32[]{:T(128)S(6)} %convert_element_type.78), kind=kLoop, calls=%fused_computation.29 | loop fusion | bytes 524292 | tf_op jit(solution)/shard_map/cond/branch_9_fun/dynamic_slice | solution.py:113
  5.2 6.9 %all-to-all-start.9 = ((f32[16,16,256]{2,1,0:T(8,128)}), f32[16,16,256]{2,1,0:T(8,128)S(1)}, u32[]{:S(2)}, u32[]{:S(2)}) async-start(f32[16,16,256]{2,1,0:T(8,128)} %bitcast.27), calls=%async_computation.9 | async-start | bytes 524288 | tf_op jit(solution)/shard_map/cond/branch_9_fun/all_to_all | solution.py:105
  13.4 5.4 %all-to-all-done.9 = f32[16,16,256]{2,1,0:T(8,128)S(1)} async-done(((f32[16,16,256]{2,1,0:T(8,128)}), f32[16,16,256]{2,1,0:T(8,128)S(1)}, u32[]{:S(2)}, u32[]{:S(2)}) %all-to-all-start.9) | async-done | bytes 262176 | tf_op jit(solution)/shard_map/cond/branch_9_fun/all_to_all | solution.py:105
  20.9 1.5 %collective-permute-start.73 = (f32[512,256]{1,0:T(8,128)S(1)}, f32[512,256]{1,0:T(8,128)}, u32[]{:S(2)}, u32[]{:S(2)}) collective-permute-start(f32[512,256]{1,0:T(8,128)S(1)} %get-tuple-element.283), channel_id=1, source_target_pairs={{6,4},{7,5},{14,12},{15,13},{22,20},{23,21},{30,28},{31,29},{38,36... | collective-permute-start | bytes 1572872 | tf_op jit(solution)/shard_map/ppermute | solution.py:99
  22.4 1.5 %collective-permute-start.72 = (f32[512,256]{1,0:T(8,128)S(1)}, f32[512,256]{1,0:T(8,128)}, u32[]{:S(2)}, u32[]{:S(2)}) collective-permute-start(f32[512,256]{1,0:T(8,128)S(1)} %get-tuple-element.283), channel_id=1, source_target_pairs={{6,8},{7,9},{14,16},{15,17},{22,24},{23,25},{30,0},{31,1},{38,40},... | collective-permute-start | bytes 1572872 | tf_op jit(solution)/shard_map/ppermute | solution.py:99
  24.7 4.2 %all-to-all-start.20 = ((f32[16,32,256]{2,1,0:T(8,128)}), f32[16,32,256]{2,1,0:T(8,128)S(1)}, u32[]{:S(2)}, u32[]{:S(2)}) async-start(f32[16,32,256]{2,1,0:T(8,128)} %bitcast.65), calls=%async_computation.20 | async-start | bytes 1048576 | tf_op jit(solution)/shard_map/all_to_all | solution.py:105
  30.9 1.3 collective-permute-start.75
  32.3 1.7 %slice_bitcast_fusion.2 = (f32[512,512]{1,0:T(8,128)S(1)}, f32[512,512]{1,0:T(8,128)S(1)}) fusion(f32[2,512,512]{2,1,0:T(8,128)} %param.31, f32[2,512,512]{2,1,0:T(8,128)} %param.30), kind=kLoop, calls=%fused_computation.52 | loop fusion | bytes 4194304 | tf_op jit(solution)/shard_map/squeeze | solution.py:131
  34.0 24.5 %collective-permute-done.74 = f32[256,256]{1,0:T(8,128)} collective-permute-done((f32[256,256]{1,0:T(8,128)}, f32[256,256]{1,0:T(8,128)}, u32[]{:S(2)}, u32[]{:S(2)}) %collective-permute-start.74) | collective-permute-done | bytes 262176 | tf_op jit(solution)/shard_map/ppermute | solution.py:99
  59.7 4.2 %collective-permute-start.76 = (f32[512,256]{1,0:T(8,128)S(1)}, f32[512,256]{1,0:T(8,128)}, u32[]{:S(2)}, u32[]{:S(2)}) collective-permute-start(f32[512,256]{1,0:T(8,128)S(1)} %fusion.1.mine_ref), channel_id=1, source_target_pairs={{0,1},{1,0},{2,3},{3,2},{4,5},{5,4},{6,7},{7,6},{8,9},{9,8},{10,11... | collective-permute-start | bytes 1572872 | tf_op jit(solution)/shard_map/ppermute | solution.py:165
  66.2 3.7 %late.2 = (f32[512,256]{1,0:T(8,128)}, f32[256,256]{1,0:T(8,128)}) custom-call(s32[8]{0:T(128)S(1)} %pad_add_fusion.flags, f32[512,256]{1,0:T(8,128)} %collective-permute-done.76.other_ref, f32[512,512]{1,0:T(8,128)S(1)} %get-tuple-element.295.part_ref, f32[512,256]{1,0:T(8,128)S(1)} %get-tuple-element.296.rows_ref, ...), custom_call_target="tpu_custom_call" | custom-call | flops 805306368 | bytes 3145728 | tf_op jit(solution)/shard_map/late/pallas_call | solution.py:181
  69.9 19.0 %conditional.3 = (f32[512,256]{1,0:T(8,128)S(1)}, f32[512,256]{1,0:T(8,128)}) conditional(s32[]{:T(128)} %clamp.7, (s32[]{:T(128)}, s32[]{:T(128)}, f32[512,256]{1,0:T(8,128)}, f32[256,256]{1,0:T(8,128)}) %tuple.113, (s32[]{:T(128)}, s32[]{:T(128)}, f32[512,256]{1,0:T(8,128)}, f32[256,256]{1,0:T(8,128)}) %tuple.113, ...), branch_computations={%region_10.11_spmd, %region_11.12_spmd, %region_12.13_spmd, %regio... | conditional | flops 524298 | bytes 12943680 | solution.py:129
  72.7 6.9 %all-to-all-start.15 = ((f32[16,16,256]{2,1,0:T(8,128)}), f32[16,16,256]{2,1,0:T(8,128)S(1)}, u32[]{:S(2)}, u32[]{:S(2)}) async-start(f32[16,16,256]{2,1,0:T(8,128)} %bitcast.45), calls=%async_computation.15 | async-start | bytes 524288 | tf_op jit(solution)/shard_map/cond/branch_5_fun/all_to_all | solution.py:105
  80.8 6.0 %all-to-all-done.15 = f32[16,16,256]{2,1,0:T(8,128)S(1)} async-done(((f32[16,16,256]{2,1,0:T(8,128)}), f32[16,16,256]{2,1,0:T(8,128)S(1)}, u32[]{:S(2)}, u32[]{:S(2)}) %all-to-all-start.15) | async-done | bytes 262176 | tf_op jit(solution)/shard_map/cond/branch_5_fun/all_to_all | solution.py:105
  89.7 1.5 %collective-permute-start.78 = (f32[512,256]{1,0:T(8,128)S(1)}, f32[512,256]{1,0:T(8,128)}, u32[]{:S(2)}, u32[]{:S(2)}) collective-permute-start(f32[512,256]{1,0:T(8,128)S(1)} %get-tuple-element.299), channel_id=1, source_target_pairs={{6,4},{7,5},{14,12},{15,13},{22,20},{23,21},{30,28},{31,29},{38,36... | collective-permute-start | bytes 1572872 | tf_op jit(solution)/shard_map/ppermute | solution.py:99
  91.2 1.4 %collective-permute-start.77 = (f32[512,256]{1,0:T(8,128)S(1)}, f32[512,256]{1,0:T(8,128)}, u32[]{:S(2)}, u32[]{:S(2)}) collective-permute-start(f32[512,256]{1,0:T(8,128)S(1)} %get-tuple-element.299), channel_id=1, source_target_pairs={{6,8},{7,9},{14,16},{15,17},{22,24},{23,25},{30,0},{31,1},{38,40},... | collective-permute-start | bytes 1572872 | tf_op jit(solution)/shard_map/ppermute | solution.py:99
  92.6 4.8 %all-to-all-start.21 = ((f32[16,32,256]{2,1,0:T(8,128)}), f32[16,32,256]{2,1,0:T(8,128)S(1)}, u32[]{:S(2)}, u32[]{:S(2)}) async-start(f32[16,32,256]{2,1,0:T(8,128)} %bitcast.69), calls=%async_computation.21 | async-start | bytes 1048576 | tf_op jit(solution)/shard_map/all_to_all | solution.py:105
  98.8 1.3 collective-permute-start.80
  100.1 1.3 slice_bitcast_fusion.1.lower_ref
  101.4 1.3 slice_bitcast_fusion.upper_ref
  102.7 22.3 %collective-permute-done.79 = f32[256,256]{1,0:T(8,128)S(1)} collective-permute-done((f32[256,256]{1,0:T(8,128)}, f32[256,256]{1,0:T(8,128)S(1)}, u32[]{:S(2)}, u32[]{:S(2)}) %collective-permute-start.79) | collective-permute-done | bytes 262176 | tf_op jit(solution)/shard_map/ppermute | solution.py:99
  125.1 3.3 %collective-permute-start.81 = (f32[512,256]{1,0:T(8,128)S(1)}, f32[512,256]{1,0:T(8,128)}, u32[]{:S(2)}, u32[]{:S(2)}) collective-permute-start(f32[512,256]{1,0:T(8,128)S(1)} %fusion.3.mine_ref), channel_id=1, source_target_pairs={{0,1},{1,0},{2,3},{3,2},{4,5},{5,4},{6,7},{7,6},{8,9},{9,8},{10,11... | collective-permute-start | bytes 1572872 | tf_op jit(solution)/shard_map/ppermute | solution.py:165
  130.1 3.1 %late.3 = f32[512,256]{1,0:T(8,128)} custom-call(s32[8]{0:T(128)S(1)} %pad_add_fusion.flags, f32[512,256]{1,0:T(8,128)} %collective-permute-done.81.other_ref, f32[512,512]{1,0:T(8,128)S(1)} %get-tuple-element.309.part_ref, f32[512,256]{1,0:T(8,128)S(1)} %get-tuple-element.310.rows_ref, f32[512,512]{1,0:T(8,128)S(1)} %slice_bitcast_fusion.upper_ref, ...), custom_call_target="tpu_custom_call" | custom-call | flops 805306368 | bytes 3145728 | tf_op jit(solution)/shard_map/late/pallas_call | solution.py:181
  (53 shorter events, 18.6 us)
Async XLA Ops:
  0.7 23.2 %copy-start.5 = (s32[2,2]{1,0:T(2,128)S(1)}, s32[2,2]{1,0:T(2,128)}, u32[]{:S(2)}) copy-start(s32[2,2]{1,0:T(2,128)} %param.27) | copy-start | bytes 52
  0.7 23.3 %copy-start.3 = (s32[2,1]{0,1:T(1,128)S(1)}, s32[2,1]{0,1:T(1,128)}, u32[]{:S(2)}) copy-start(s32[2,1]{0,1:T(1,128)} %param.28) | copy-start | bytes 28
  0.7 19.0 %collective-permute-start.35 = (f32[512,256]{1,0:T(8,128)}, f32[512,256]{1,0:T(8,128)S(1)}, u32[]{:S(2)}, u32[]{:S(2)}) collective-permute-start(f32[512,256]{1,0:T(8,128)} %get-tuple-element.193), channel_id=1, source_target_pairs={{30,14},{31,15},{62,46},{63,47},{94,78},{95,79},{126,110},{127,111... | collective-permute-start | bytes 1572872 | tf_op jit(solution)/shard_map/cond/branch_9_fun/ppermute | solution.py:99
  1.4 18.3 %collective-permute-start.34 = (f32[512,256]{1,0:T(8,128)}, f32[512,256]{1,0:T(8,128)S(1)}, u32[]{:S(2)}, u32[]{:S(2)}) collective-permute-start(f32[512,256]{1,0:T(8,128)} %get-tuple-element.193), channel_id=1, source_target_pairs={{30,6},{31,7},{62,38},{63,39},{94,70},{95,71},{126,102},{127,103},... | collective-permute-start | bytes 1572872 | tf_op jit(solution)/shard_map/cond/branch_9_fun/ppermute | solution.py:99
  2.1 17.6 %collective-permute-start.33 = (f32[512,256]{1,0:T(8,128)}, f32[512,256]{1,0:T(8,128)S(1)}, u32[]{:S(2)}, u32[]{:S(2)}) collective-permute-start(f32[512,256]{1,0:T(8,128)} %get-tuple-element.193), channel_id=1, source_target_pairs={{30,22},{31,23},{62,54},{63,55},{94,86},{95,87},{126,118},{127,119... | collective-permute-start | bytes 1572872 | tf_op jit(solution)/shard_map/cond/branch_9_fun/ppermute | solution.py:99
  5.2 13.7 %all-to-all-start.9 = ((f32[16,16,256]{2,1,0:T(8,128)}), f32[16,16,256]{2,1,0:T(8,128)S(1)}, u32[]{:S(2)}, u32[]{:S(2)}) async-start(f32[16,16,256]{2,1,0:T(8,128)} %bitcast.27), calls=%async_computation.9 | async-start | bytes 524288 | tf_op jit(solution)/shard_map/cond/branch_9_fun/all_to_all | solution.py:105
  20.9 37.6 %collective-permute-start.73 = (f32[512,256]{1,0:T(8,128)S(1)}, f32[512,256]{1,0:T(8,128)}, u32[]{:S(2)}, u32[]{:S(2)}) collective-permute-start(f32[512,256]{1,0:T(8,128)S(1)} %get-tuple-element.283), channel_id=1, source_target_pairs={{6,4},{7,5},{14,12},{15,13},{22,20},{23,21},{30,28},{31,29},{38,36... | collective-permute-start | bytes 1572872 | tf_op jit(solution)/shard_map/ppermute | solution.py:99
  22.4 11.6 %collective-permute-start.72 = (f32[512,256]{1,0:T(8,128)S(1)}, f32[512,256]{1,0:T(8,128)}, u32[]{:S(2)}, u32[]{:S(2)}) collective-permute-start(f32[512,256]{1,0:T(8,128)S(1)} %get-tuple-element.283), channel_id=1, source_target_pairs={{6,8},{7,9},{14,16},{15,17},{22,24},{23,25},{30,0},{31,1},{38,40},... | collective-permute-start | bytes 1572872 | tf_op jit(solution)/shard_map/ppermute | solution.py:99
  24.7 40.5 %all-to-all-start.20 = ((f32[16,32,256]{2,1,0:T(8,128)}), f32[16,32,256]{2,1,0:T(8,128)S(1)}, u32[]{:S(2)}, u32[]{:S(2)}) async-start(f32[16,32,256]{2,1,0:T(8,128)} %bitcast.65), calls=%async_computation.20 | async-start | bytes 1048576 | tf_op jit(solution)/shard_map/all_to_all | solution.py:105
  29.7 28.9 %collective-permute-start.74 = (f32[256,256]{1,0:T(8,128)}, f32[256,256]{1,0:T(8,128)}, u32[]{:S(2)}, u32[]{:S(2)}) collective-permute-start(f32[256,256]{1,0:T(8,128)} %get-tuple-element.313), channel_id=1, source_target_pairs={{6,10},{7,11},{14,18},{15,19},{22,26},{23,27},{30,2},{31,3},{38,42... | collective-permute-start | bytes 786440 | tf_op jit(solution)/shard_map/ppermute | solution.py:99
  30.9 27.6 %collective-permute-start.75 = (f32[256,256]{1,0:T(8,128)S(1)}, f32[256,256]{1,0:T(8,128)}, u32[]{:S(2)}, u32[]{:S(2)}) collective-permute-start(f32[256,256]{1,0:T(8,128)S(1)} %get-tuple-element.314), channel_id=1, source_target_pairs={{6,2},{7,3},{14,10},{15,11},{22,18},{23,19},{30,26},{31,27},{38,34... | collective-permute-start | bytes 786440 | tf_op jit(solution)/shard_map/ppermute | solution.py:99
  34.0 29.9 %copy-start.4 = (s32[2]{0:T(128)S(1)}, s32[2]{0:T(128)}, u32[]{:S(2)}) copy-start(s32[2]{0:T(128)} %param.29) | copy-start | bytes 28
  59.7 6.5 %collective-permute-start.76 = (f32[512,256]{1,0:T(8,128)S(1)}, f32[512,256]{1,0:T(8,128)}, u32[]{:S(2)}, u32[]{:S(2)}) collective-permute-start(f32[512,256]{1,0:T(8,128)S(1)} %fusion.1.mine_ref), channel_id=1, source_target_pairs={{0,1},{1,0},{2,3},{3,2},{4,5},{5,4},{6,7},{7,6},{8,9},{9,8},{10,11... | collective-permute-start | bytes 1572872 | tf_op jit(solution)/shard_map/ppermute | solution.py:165
  69.9 17.7 %collective-permute-start.59 = (f32[512,256]{1,0:T(8,128)}, f32[512,256]{1,0:T(8,128)S(1)}, u32[]{:S(2)}, u32[]{:S(2)}) collective-permute-start(f32[512,256]{1,0:T(8,128)} %get-tuple-element.229), channel_id=1, source_target_pairs={{12,30},{13,31},{28,14},{29,15},{44,62},{45,63},{60,46},{61,47},{7... | collective-permute-start | bytes 1572872 | tf_op jit(solution)/shard_map/cond/branch_5_fun/ppermute | solution.py:99
  70.6 17.0 %collective-permute-start.58 = (f32[512,256]{1,0:T(8,128)}, f32[512,256]{1,0:T(8,128)S(1)}, u32[]{:S(2)}, u32[]{:S(2)}) collective-permute-start(f32[512,256]{1,0:T(8,128)} %get-tuple-element.229), channel_id=1, source_target_pairs={{12,22},{13,23},{28,6},{29,7},{44,54},{45,55},{60,38},{61,39},{76,... | collective-permute-start | bytes 1572872 | tf_op jit(solution)/shard_map/cond/branch_5_fun/ppermute | solution.py:99
  71.3 16.4 %collective-permute-start.57 = (f32[512,256]{1,0:T(8,128)}, f32[512,256]{1,0:T(8,128)S(1)}, u32[]{:S(2)}, u32[]{:S(2)}) collective-permute-start(f32[512,256]{1,0:T(8,128)} %get-tuple-element.229), channel_id=1, source_target_pairs={{4,30},{5,31},{12,6},{13,7},{20,14},{21,15},{28,22},{29,23},{36,62... | collective-permute-start | bytes 1572872 | tf_op jit(solution)/shard_map/cond/branch_5_fun/ppermute | solution.py:99
  72.0 15.7 %collective-permute-start.56 = (f32[512,256]{1,0:T(8,128)}, f32[512,256]{1,0:T(8,128)S(1)}, u32[]{:S(2)}, u32[]{:S(2)}) collective-permute-start(f32[512,256]{1,0:T(8,128)} %get-tuple-element.229), channel_id=1, source_target_pairs={{4,6},{5,7},{12,14},{13,15},{20,22},{21,23},{28,30},{29,31},{36,38... | collective-permute-start | bytes 1572872 | tf_op jit(solution)/shard_map/cond/branch_5_fun/ppermute | solution.py:99
  72.7 14.1 %all-to-all-start.15 = ((f32[16,16,256]{2,1,0:T(8,128)}), f32[16,16,256]{2,1,0:T(8,128)S(1)}, u32[]{:S(2)}, u32[]{:S(2)}) async-start(f32[16,16,256]{2,1,0:T(8,128)} %bitcast.45), calls=%async_computation.15 | async-start | bytes 524288 | tf_op jit(solution)/shard_map/cond/branch_5_fun/all_to_all | solution.py:105
  89.7 35.2 %collective-permute-start.78 = (f32[512,256]{1,0:T(8,128)S(1)}, f32[512,256]{1,0:T(8,128)}, u32[]{:S(2)}, u32[]{:S(2)}) collective-permute-start(f32[512,256]{1,0:T(8,128)S(1)} %get-tuple-element.299), channel_id=1, source_target_pairs={{6,4},{7,5},{14,12},{15,13},{22,20},{23,21},{30,28},{31,29},{38,36... | collective-permute-start | bytes 1572872 | tf_op jit(solution)/shard_map/ppermute | solution.py:99
  91.2 11.5 %collective-permute-start.77 = (f32[512,256]{1,0:T(8,128)S(1)}, f32[512,256]{1,0:T(8,128)}, u32[]{:S(2)}, u32[]{:S(2)}) collective-permute-start(f32[512,256]{1,0:T(8,128)S(1)} %get-tuple-element.299), channel_id=1, source_target_pairs={{6,8},{7,9},{14,16},{15,17},{22,24},{23,25},{30,0},{31,1},{38,40},... | collective-permute-start | bytes 1572872 | tf_op jit(solution)/shard_map/ppermute | solution.py:99
  92.6 35.8 %all-to-all-start.21 = ((f32[16,32,256]{2,1,0:T(8,128)}), f32[16,32,256]{2,1,0:T(8,128)S(1)}, u32[]{:S(2)}, u32[]{:S(2)}) async-start(f32[16,32,256]{2,1,0:T(8,128)} %bitcast.69), calls=%async_computation.21 | async-start | bytes 1048576 | tf_op jit(solution)/shard_map/all_to_all | solution.py:105
  97.5 27.5 %collective-permute-start.79 = (f32[256,256]{1,0:T(8,128)}, f32[256,256]{1,0:T(8,128)S(1)}, u32[]{:S(2)}, u32[]{:S(2)}) collective-permute-start(f32[256,256]{1,0:T(8,128)} %get-tuple-element.311), channel_id=1, source_target_pairs={{6,10},{7,11},{14,18},{15,19},{22,26},{23,27},{30,2},{31,3},{38,42... | collective-permute-start | bytes 786440 | tf_op jit(solution)/shard_map/ppermute | solution.py:99
  98.8 26.2 %collective-permute-start.80 = (f32[256,256]{1,0:T(8,128)S(1)}, f32[256,256]{1,0:T(8,128)S(1)}, u32[]{:S(2)}, u32[]{:S(2)}) collective-permute-start(f32[256,256]{1,0:T(8,128)S(1)} %get-tuple-element.312), channel_id=1, source_target_pairs={{6,2},{7,3},{14,10},{15,11},{22,18},{23,19},{30,26},{31,27},{38,34... | collective-permute-start | bytes 786440 | tf_op jit(solution)/shard_map/ppermute | solution.py:99
  125.1 4.9 %collective-permute-start.81 = (f32[512,256]{1,0:T(8,128)S(1)}, f32[512,256]{1,0:T(8,128)}, u32[]{:S(2)}, u32[]{:S(2)}) collective-permute-start(f32[512,256]{1,0:T(8,128)S(1)} %fusion.3.mine_ref), channel_id=1, source_target_pairs={{0,1},{1,0},{2,3},{3,2},{4,5},{5,4},{6,7},{7,6},{8,9},{9,8},{10,11... | collective-permute-start | bytes 1572872 | tf_op jit(solution)/shard_map/ppermute | solution.py:165
  (3 other events, 26.6 us)

commit v9 on v8

--- a/solution.py
+++ b/solution.py
@@ -145,10 +145,10 @@
     leads = []
     for place in (0, 1, 2, 4, 5, 6):
         hops = [hop - place % 4 for hop in (7, -5, 3, -1)]
-        hops.sort(key=abs, reverse=True)
+        hops.sort(key=abs)
         leads.append(to_leaders([(place, 8 if abs(hop) > 3 else 4, hop) for hop in hops]))
     for place in range(3, n_z, 4):
-        leads.append(to_leaders([(place, n_z, hop) for hop in (8, 4, -4)]))
+        leads.append(to_leaders([(place, n_z, hop) for hop in (-4, 4, 8)]))
     whole = pl.BlockSpec(memory_space=pltpu.VMEM)
     scalars = pl.BlockSpec(memory_space=pltpu.SMEM)
     params = pltpu.CompilerParams(vmem_limit_bytes=VMEM_BYTES)

time: 134 us -> 140 us (1.045)
  waiting for transfers between devices: 58.9 us -> 63.8 us
    ppermute x15, waiting for transfers between devices: 46.8 us -> 51.8 us  [send_z(): return lax.ppermute(value, 'col', pairs)]
  transfers between devices with their start and end apart: 21 -> 21, of which waited for: 5 -> 5; matrix products, arithmetic and copies ran while one was open for 8% -> 8% of each run, Pallas kernels for 2% -> 1%
where the time goes in v9:
time: 140 us; the launch traced here: 138 us
  waiting for transfers between devices  63.8 us (46%)
  starting transfers between devices  46.3 us (33%)
  local copies, waits for them, and re-layouts  9.98 us (7%)
  Pallas kernels  8.89 us (6%)
  other arithmetic  4.47 us (3%)
  loops' own time  3.27 us (2%)
  between operations  1.48 us (1%)
    ppermute x15, waiting for transfers between devices, send_z(): return lax.ppermute(value, 'col', pairs)  51.8 us
    all_to_all x4, starting transfers between devices, exchange(): return lax.all_to_all(value, 'row', 0, 0, tiled=True)  22.9 us
    ppermute x15, starting transfers between devices, send_z(): return lax.ppermute(value, 'col', pairs)  15.8 us
    all_to_all x4, waiting for transfers between devices, exchange(): return lax.all_to_all(value, 'row', 0, 0, tiled=True)  11.4 us
    ppermute x2, starting transfers between devices, local(): other = lax.ppermute(mine, 'col', [(i, i ^ 1) for i in range(n_col)])  7.6 us
    pallas_call x2, Pallas kernels, local(): pl.pallas_call(functools.partial(late_kernel, n_row, step, n_steps), out_...  6.84 us
    squeeze x3, local copies, waits for them, and re-layouts, fetch(): later = (later[0][step], later[1][step], later[2], later[3])  4.31 us
    another operation x2, loops' own time, fetch(): middle, tiled = lax.switch(which, leads, block, own, first)  3.27 us
  transfers between devices with their start and end apart: 21, of which 5 were waited for; matrix products, arithmetic and copies ran while one was open for 8% of the time, Pallas kernels for 1%

profile of v9, /device:TPU:35, one launch (start us, length us, event | category | flops | bytes accessed | tf_op | source)
XLA Modules:
  0.0 138.3 jit_solution(15725695850788618810)
XLA Ops:
  0.7 20.2 %conditional.2 = (f32[512,256]{1,0:T(8,128)S(1)}, f32[512,256]{1,0:T(8,128)}) conditional(s32[]{:T(128)} %clamp.6, (s32[]{:T(128)}, s32[]{:T(128)}, f32[512,256]{1,0:T(8,128)}) %tuple.139, (s32[]{:T(128)}, s32[]{:T(128)}, f32[512,256]{1,0:T(8,128)}) %tuple.140, (s32[]{:T(128)}, s32[]{:T(128)}, ...), branch_computations={%region_0.1_spmd, %region_1.2_spmd, %region_2.3_spmd, %region_3.4_... | conditional | flops 524301 | bytes 13468004 | solution.py:129
  3.5 1.7 %constant_dynamic-slice_fusion.19 = f32[256,256]{1,0:T(8,128)} fusion(f32[512,256]{1,0:T(8,128)} %get-tuple-element.193, u32[]{:T(128)S(6)} %convert_element_type.78), kind=kLoop, calls=%fused_computation.29 | loop fusion | bytes 524292 | tf_op jit(solution)/shard_map/cond/branch_9_fun/dynamic_slice | solution.py:113
  5.2 6.9 %all-to-all-start.9 = ((f32[16,16,256]{2,1,0:T(8,128)}), f32[16,16,256]{2,1,0:T(8,128)S(1)}, u32[]{:S(2)}, u32[]{:S(2)}) async-start(f32[16,16,256]{2,1,0:T(8,128)} %bitcast.27), calls=%async_computation.9 | async-start | bytes 524288 | tf_op jit(solution)/shard_map/cond/branch_9_fun/all_to_all | solution.py:105
  13.4 5.4 %all-to-all-done.9 = f32[16,16,256]{2,1,0:T(8,128)S(1)} async-done(((f32[16,16,256]{2,1,0:T(8,128)}), f32[16,16,256]{2,1,0:T(8,128)S(1)}, u32[]{:S(2)}, u32[]{:S(2)}) %all-to-all-start.9) | async-done | bytes 262176 | tf_op jit(solution)/shard_map/cond/branch_9_fun/all_to_all | solution.py:105
  20.9 1.5 %collective-permute-start.73 = (f32[512,256]{1,0:T(8,128)S(1)}, f32[512,256]{1,0:T(8,128)}, u32[]{:S(2)}, u32[]{:S(2)}) collective-permute-start(f32[512,256]{1,0:T(8,128)S(1)} %get-tuple-element.283), channel_id=1, source_target_pairs={{6,4},{7,5},{14,12},{15,13},{22,20},{23,21},{30,28},{31,29},{38,36... | collective-permute-start | bytes 1572872 | tf_op jit(solution)/shard_map/ppermute | solution.py:99
  22.4 1.5 %collective-permute-start.72 = (f32[512,256]{1,0:T(8,128)S(1)}, f32[512,256]{1,0:T(8,128)}, u32[]{:S(2)}, u32[]{:S(2)}) collective-permute-start(f32[512,256]{1,0:T(8,128)S(1)} %get-tuple-element.283), channel_id=1, source_target_pairs={{6,8},{7,9},{14,16},{15,17},{22,24},{23,25},{30,0},{31,1},{38,40},... | collective-permute-start | bytes 1572872 | tf_op jit(solution)/shard_map/ppermute | solution.py:99
  24.7 4.2 %all-to-all-start.20 = ((f32[16,32,256]{2,1,0:T(8,128)}), f32[16,32,256]{2,1,0:T(8,128)S(1)}, u32[]{:S(2)}, u32[]{:S(2)}) async-start(f32[16,32,256]{2,1,0:T(8,128)} %bitcast.65), calls=%async_computation.20 | async-start | bytes 1048576 | tf_op jit(solution)/shard_map/all_to_all | solution.py:105
  30.9 1.3 collective-permute-start.75
  32.3 1.7 %slice_bitcast_fusion.2 = (f32[512,512]{1,0:T(8,128)S(1)}, f32[512,512]{1,0:T(8,128)S(1)}) fusion(f32[2,512,512]{2,1,0:T(8,128)} %param.31, f32[2,512,512]{2,1,0:T(8,128)} %param.30), kind=kLoop, calls=%fused_computation.52 | loop fusion | bytes 4194304 | tf_op jit(solution)/shard_map/squeeze | solution.py:131
  34.0 23.6 %collective-permute-done.74 = f32[256,256]{1,0:T(8,128)} collective-permute-done((f32[256,256]{1,0:T(8,128)}, f32[256,256]{1,0:T(8,128)}, u32[]{:S(2)}, u32[]{:S(2)}) %collective-permute-start.74) | collective-permute-done | bytes 262176 | tf_op jit(solution)/shard_map/ppermute | solution.py:99
  58.8 4.2 %collective-permute-start.76 = (f32[512,256]{1,0:T(8,128)S(1)}, f32[512,256]{1,0:T(8,128)}, u32[]{:S(2)}, u32[]{:S(2)}) collective-permute-start(f32[512,256]{1,0:T(8,128)S(1)} %fusion.1.mine_ref), channel_id=1, source_target_pairs={{0,1},{1,0},{2,3},{3,2},{4,5},{5,4},{6,7},{7,6},{8,9},{9,8},{10,11... | collective-permute-start | bytes 1572872 | tf_op jit(solution)/shard_map/ppermute | solution.py:165
  65.3 3.7 %late.2 = (f32[512,256]{1,0:T(8,128)}, f32[256,256]{1,0:T(8,128)}) custom-call(s32[8]{0:T(128)S(1)} %pad_add_fusion.flags, f32[512,256]{1,0:T(8,128)} %collective-permute-done.76.other_ref, f32[512,512]{1,0:T(8,128)S(1)} %get-tuple-element.295.part_ref, f32[512,256]{1,0:T(8,128)S(1)} %get-tuple-element.296.rows_ref, ...), custom_call_target="tpu_custom_call" | custom-call | flops 805306368 | bytes 3145728 | tf_op jit(solution)/shard_map/late/pallas_call | solution.py:181
  69.0 19.0 %conditional.3 = (f32[512,256]{1,0:T(8,128)S(1)}, f32[512,256]{1,0:T(8,128)}) conditional(s32[]{:T(128)} %clamp.7, (s32[]{:T(128)}, s32[]{:T(128)}, f32[512,256]{1,0:T(8,128)}, f32[256,256]{1,0:T(8,128)}) %tuple.113, (s32[]{:T(128)}, s32[]{:T(128)}, f32[512,256]{1,0:T(8,128)}, f32[256,256]{1,0:T(8,128)}) %tuple.113, ...), branch_computations={%region_10.11_spmd, %region_11.12_spmd, %region_12.13_spmd, %regio... | conditional | flops 524298 | bytes 12943680 | solution.py:129
  71.8 6.9 %all-to-all-start.15 = ((f32[16,16,256]{2,1,0:T(8,128)}), f32[16,16,256]{2,1,0:T(8,128)S(1)}, u32[]{:S(2)}, u32[]{:S(2)}) async-start(f32[16,16,256]{2,1,0:T(8,128)} %bitcast.45), calls=%async_computation.15 | async-start | bytes 524288 | tf_op jit(solution)/shard_map/cond/branch_5_fun/all_to_all | solution.py:105
  79.9 6.0 %all-to-all-done.15 = f32[16,16,256]{2,1,0:T(8,128)S(1)} async-done(((f32[16,16,256]{2,1,0:T(8,128)}), f32[16,16,256]{2,1,0:T(8,128)S(1)}, u32[]{:S(2)}, u32[]{:S(2)}) %all-to-all-start.15) | async-done | bytes 262176 | tf_op jit(solution)/shard_map/cond/branch_5_fun/all_to_all | solution.py:105
  88.8 1.5 %collective-permute-start.78 = (f32[512,256]{1,0:T(8,128)S(1)}, f32[512,256]{1,0:T(8,128)}, u32[]{:S(2)}, u32[]{:S(2)}) collective-permute-start(f32[512,256]{1,0:T(8,128)S(1)} %get-tuple-element.299), channel_id=1, source_target_pairs={{6,4},{7,5},{14,12},{15,13},{22,20},{23,21},{30,28},{31,29},{38,36... | collective-permute-start | bytes 1572872 | tf_op jit(solution)/shard_map/ppermute | solution.py:99
  90.3 1.4 %collective-permute-start.77 = (f32[512,256]{1,0:T(8,128)S(1)}, f32[512,256]{1,0:T(8,128)}, u32[]{:S(2)}, u32[]{:S(2)}) collective-permute-start(f32[512,256]{1,0:T(8,128)S(1)} %get-tuple-element.299), channel_id=1, source_target_pairs={{6,8},{7,9},{14,16},{15,17},{22,24},{23,25},{30,0},{31,1},{38,40},... | collective-permute-start | bytes 1572872 | tf_op jit(solution)/shard_map/ppermute | solution.py:99
  91.7 4.8 %all-to-all-start.21 = ((f32[16,32,256]{2,1,0:T(8,128)}), f32[16,32,256]{2,1,0:T(8,128)S(1)}, u32[]{:S(2)}, u32[]{:S(2)}) async-start(f32[16,32,256]{2,1,0:T(8,128)} %bitcast.69), calls=%async_computation.21 | async-start | bytes 1048576 | tf_op jit(solution)/shard_map/all_to_all | solution.py:105
  97.9 1.3 collective-permute-start.80
  99.2 1.3 slice_bitcast_fusion.1.lower_ref
  100.5 1.3 slice_bitcast_fusion.upper_ref
  101.8 28.1 %collective-permute-done.79 = f32[256,256]{1,0:T(8,128)S(1)} collective-permute-done((f32[256,256]{1,0:T(8,128)}, f32[256,256]{1,0:T(8,128)S(1)}, u32[]{:S(2)}, u32[]{:S(2)}) %collective-permute-start.79) | collective-permute-done | bytes 262176 | tf_op jit(solution)/shard_map/ppermute | solution.py:99
  130.1 3.4 %collective-permute-start.81 = (f32[512,256]{1,0:T(8,128)S(1)}, f32[512,256]{1,0:T(8,128)}, u32[]{:S(2)}, u32[]{:S(2)}) collective-permute-start(f32[512,256]{1,0:T(8,128)S(1)} %fusion.3.mine_ref), channel_id=1, source_target_pairs={{0,1},{1,0},{2,3},{3,2},{4,5},{5,4},{6,7},{7,6},{8,9},{9,8},{10,11... | collective-permute-start | bytes 1572872 | tf_op jit(solution)/shard_map/ppermute | solution.py:165
  135.1 3.1 %late.3 = f32[512,256]{1,0:T(8,128)} custom-call(s32[8]{0:T(128)S(1)} %pad_add_fusion.flags, f32[512,256]{1,0:T(8,128)} %collective-permute-done.81.other_ref, f32[512,512]{1,0:T(8,128)S(1)} %get-tuple-element.309.part_ref, f32[512,256]{1,0:T(8,128)S(1)} %get-tuple-element.310.rows_ref, f32[512,512]{1,0:T(8,128)S(1)} %slice_bitcast_fusion.upper_ref, ...), custom_call_target="tpu_custom_call" | custom-call | flops 805306368 | bytes 3145728 | tf_op jit(solution)/shard_map/late/pallas_call | solution.py:181
  (53 shorter events, 18.6 us)
Async XLA Ops:
  0.7 23.2 %copy-start.5 = (s32[2,2]{1,0:T(2,128)S(1)}, s32[2,2]{1,0:T(2,128)}, u32[]{:S(2)}) copy-start(s32[2,2]{1,0:T(2,128)} %param.27) | copy-start | bytes 52
  0.7 23.3 %copy-start.3 = (s32[2,1]{0,1:T(1,128)S(1)}, s32[2,1]{0,1:T(1,128)}, u32[]{:S(2)}) copy-start(s32[2,1]{0,1:T(1,128)} %param.28) | copy-start | bytes 28
  0.7 19.0 %collective-permute-start.35 = (f32[512,256]{1,0:T(8,128)}, f32[512,256]{1,0:T(8,128)S(1)}, u32[]{:S(2)}, u32[]{:S(2)}) collective-permute-start(f32[512,256]{1,0:T(8,128)} %get-tuple-element.193), channel_id=1, source_target_pairs={{30,22},{31,23},{62,54},{63,55},{94,86},{95,87},{126,118},{127,119... | collective-permute-start | bytes 1572872 | tf_op jit(solution)/shard_map/cond/branch_9_fun/ppermute | solution.py:99
  1.4 18.3 %collective-permute-start.34 = (f32[512,256]{1,0:T(8,128)}, f32[512,256]{1,0:T(8,128)S(1)}, u32[]{:S(2)}, u32[]{:S(2)}) collective-permute-start(f32[512,256]{1,0:T(8,128)} %get-tuple-element.193), channel_id=1, source_target_pairs={{30,6},{31,7},{62,38},{63,39},{94,70},{95,71},{126,102},{127,103},... | collective-permute-start | bytes 1572872 | tf_op jit(solution)/shard_map/cond/branch_9_fun/ppermute | solution.py:99
  2.1 17.6 %collective-permute-start.33 = (f32[512,256]{1,0:T(8,128)}, f32[512,256]{1,0:T(8,128)S(1)}, u32[]{:S(2)}, u32[]{:S(2)}) collective-permute-start(f32[512,256]{1,0:T(8,128)} %get-tuple-element.193), channel_id=1, source_target_pairs={{30,14},{31,15},{62,46},{63,47},{94,78},{95,79},{126,110},{127,111... | collective-permute-start | bytes 1572872 | tf_op jit(solution)/shard_map/cond/branch_9_fun/ppermute | solution.py:99
  5.2 13.7 %all-to-all-start.9 = ((f32[16,16,256]{2,1,0:T(8,128)}), f32[16,16,256]{2,1,0:T(8,128)S(1)}, u32[]{:S(2)}, u32[]{:S(2)}) async-start(f32[16,16,256]{2,1,0:T(8,128)} %bitcast.27), calls=%async_computation.9 | async-start | bytes 524288 | tf_op jit(solution)/shard_map/cond/branch_9_fun/all_to_all | solution.py:105
  20.9 36.7 %collective-permute-start.73 = (f32[512,256]{1,0:T(8,128)S(1)}, f32[512,256]{1,0:T(8,128)}, u32[]{:S(2)}, u32[]{:S(2)}) collective-permute-start(f32[512,256]{1,0:T(8,128)S(1)} %get-tuple-element.283), channel_id=1, source_target_pairs={{6,4},{7,5},{14,12},{15,13},{22,20},{23,21},{30,28},{31,29},{38,36... | collective-permute-start | bytes 1572872 | tf_op jit(solution)/shard_map/ppermute | solution.py:99
  22.4 11.6 %collective-permute-start.72 = (f32[512,256]{1,0:T(8,128)S(1)}, f32[512,256]{1,0:T(8,128)}, u32[]{:S(2)}, u32[]{:S(2)}) collective-permute-start(f32[512,256]{1,0:T(8,128)S(1)} %get-tuple-element.283), channel_id=1, source_target_pairs={{6,8},{7,9},{14,16},{15,17},{22,24},{23,25},{30,0},{31,1},{38,40},... | collective-permute-start | bytes 1572872 | tf_op jit(solution)/shard_map/ppermute | solution.py:99
  24.7 39.6 %all-to-all-start.20 = ((f32[16,32,256]{2,1,0:T(8,128)}), f32[16,32,256]{2,1,0:T(8,128)S(1)}, u32[]{:S(2)}, u32[]{:S(2)}) async-start(f32[16,32,256]{2,1,0:T(8,128)} %bitcast.65), calls=%async_computation.20 | async-start | bytes 1048576 | tf_op jit(solution)/shard_map/all_to_all | solution.py:105
  29.7 28.0 %collective-permute-start.74 = (f32[256,256]{1,0:T(8,128)}, f32[256,256]{1,0:T(8,128)}, u32[]{:S(2)}, u32[]{:S(2)}) collective-permute-start(f32[256,256]{1,0:T(8,128)} %get-tuple-element.313), channel_id=1, source_target_pairs={{6,10},{7,11},{14,18},{15,19},{22,26},{23,27},{30,2},{31,3},{38,42... | collective-permute-start | bytes 786440 | tf_op jit(solution)/shard_map/ppermute | solution.py:99
  30.9 26.7 %collective-permute-start.75 = (f32[256,256]{1,0:T(8,128)S(1)}, f32[256,256]{1,0:T(8,128)}, u32[]{:S(2)}, u32[]{:S(2)}) collective-permute-start(f32[256,256]{1,0:T(8,128)S(1)} %get-tuple-element.314), channel_id=1, source_target_pairs={{6,2},{7,3},{14,10},{15,11},{22,18},{23,19},{30,26},{31,27},{38,34... | collective-permute-start | bytes 786440 | tf_op jit(solution)/shard_map/ppermute | solution.py:99
  34.0 29.1 %copy-start.4 = (s32[2]{0:T(128)S(1)}, s32[2]{0:T(128)}, u32[]{:S(2)}) copy-start(s32[2]{0:T(128)} %param.29) | copy-start | bytes 28
  58.8 6.5 %collective-permute-start.76 = (f32[512,256]{1,0:T(8,128)S(1)}, f32[512,256]{1,0:T(8,128)}, u32[]{:S(2)}, u32[]{:S(2)}) collective-permute-start(f32[512,256]{1,0:T(8,128)S(1)} %fusion.1.mine_ref), channel_id=1, source_target_pairs={{0,1},{1,0},{2,3},{3,2},{4,5},{5,4},{6,7},{7,6},{8,9},{9,8},{10,11... | collective-permute-start | bytes 1572872 | tf_op jit(solution)/shard_map/ppermute | solution.py:165
  69.0 17.7 %collective-permute-start.59 = (f32[512,256]{1,0:T(8,128)}, f32[512,256]{1,0:T(8,128)S(1)}, u32[]{:S(2)}, u32[]{:S(2)}) collective-permute-start(f32[512,256]{1,0:T(8,128)} %get-tuple-element.229), channel_id=1, source_target_pairs={{4,6},{5,7},{12,14},{13,15},{20,22},{21,23},{28,30},{29,31},{36,38... | collective-permute-start | bytes 1572872 | tf_op jit(solution)/shard_map/cond/branch_5_fun/ppermute | solution.py:99
  69.7 17.0 %collective-permute-start.58 = (f32[512,256]{1,0:T(8,128)}, f32[512,256]{1,0:T(8,128)S(1)}, u32[]{:S(2)}, u32[]{:S(2)}) collective-permute-start(f32[512,256]{1,0:T(8,128)} %get-tuple-element.229), channel_id=1, source_target_pairs={{4,30},{5,31},{12,6},{13,7},{20,14},{21,15},{28,22},{29,23},{36,62... | collective-permute-start | bytes 1572872 | tf_op jit(solution)/shard_map/cond/branch_5_fun/ppermute | solution.py:99
  70.4 16.3 %collective-permute-start.57 = (f32[512,256]{1,0:T(8,128)}, f32[512,256]{1,0:T(8,128)S(1)}, u32[]{:S(2)}, u32[]{:S(2)}) collective-permute-start(f32[512,256]{1,0:T(8,128)} %get-tuple-element.229), channel_id=1, source_target_pairs={{12,22},{13,23},{28,6},{29,7},{44,54},{45,55},{60,38},{61,39},{76,... | collective-permute-start | bytes 1572872 | tf_op jit(solution)/shard_map/cond/branch_5_fun/ppermute | solution.py:99
  71.1 15.6 %collective-permute-start.56 = (f32[512,256]{1,0:T(8,128)}, f32[512,256]{1,0:T(8,128)S(1)}, u32[]{:S(2)}, u32[]{:S(2)}) collective-permute-start(f32[512,256]{1,0:T(8,128)} %get-tuple-element.229), channel_id=1, source_target_pairs={{12,30},{13,31},{28,14},{29,15},{44,62},{45,63},{60,46},{61,47},{7... | collective-permute-start | bytes 1572872 | tf_op jit(solution)/shard_map/cond/branch_5_fun/ppermute | solution.py:99
  71.8 14.1 %all-to-all-start.15 = ((f32[16,16,256]{2,1,0:T(8,128)}), f32[16,16,256]{2,1,0:T(8,128)S(1)}, u32[]{:S(2)}, u32[]{:S(2)}) async-start(f32[16,16,256]{2,1,0:T(8,128)} %bitcast.45), calls=%async_computation.15 | async-start | bytes 524288 | tf_op jit(solution)/shard_map/cond/branch_5_fun/all_to_all | solution.py:105
  88.8 41.1 %collective-permute-start.78 = (f32[512,256]{1,0:T(8,128)S(1)}, f32[512,256]{1,0:T(8,128)}, u32[]{:S(2)}, u32[]{:S(2)}) collective-permute-start(f32[512,256]{1,0:T(8,128)S(1)} %get-tuple-element.299), channel_id=1, source_target_pairs={{6,4},{7,5},{14,12},{15,13},{22,20},{23,21},{30,28},{31,29},{38,36... | collective-permute-start | bytes 1572872 | tf_op jit(solution)/shard_map/ppermute | solution.py:99
  90.3 11.5 %collective-permute-start.77 = (f32[512,256]{1,0:T(8,128)S(1)}, f32[512,256]{1,0:T(8,128)}, u32[]{:S(2)}, u32[]{:S(2)}) collective-permute-start(f32[512,256]{1,0:T(8,128)S(1)} %get-tuple-element.299), channel_id=1, source_target_pairs={{6,8},{7,9},{14,16},{15,17},{22,24},{23,25},{30,0},{31,1},{38,40},... | collective-permute-start | bytes 1572872 | tf_op jit(solution)/shard_map/ppermute | solution.py:99
  91.7 41.7 %all-to-all-start.21 = ((f32[16,32,256]{2,1,0:T(8,128)}), f32[16,32,256]{2,1,0:T(8,128)S(1)}, u32[]{:S(2)}, u32[]{:S(2)}) async-start(f32[16,32,256]{2,1,0:T(8,128)} %bitcast.69), calls=%async_computation.21 | async-start | bytes 1048576 | tf_op jit(solution)/shard_map/all_to_all | solution.py:105
  96.6 33.3 %collective-permute-start.79 = (f32[256,256]{1,0:T(8,128)}, f32[256,256]{1,0:T(8,128)S(1)}, u32[]{:S(2)}, u32[]{:S(2)}) collective-permute-start(f32[256,256]{1,0:T(8,128)} %get-tuple-element.311), channel_id=1, source_target_pairs={{6,10},{7,11},{14,18},{15,19},{22,26},{23,27},{30,2},{31,3},{38,42... | collective-permute-start | bytes 786440 | tf_op jit(solution)/shard_map/ppermute | solution.py:99
  97.9 32.1 %collective-permute-start.80 = (f32[256,256]{1,0:T(8,128)S(1)}, f32[256,256]{1,0:T(8,128)S(1)}, u32[]{:S(2)}, u32[]{:S(2)}) collective-permute-start(f32[256,256]{1,0:T(8,128)S(1)} %get-tuple-element.312), channel_id=1, source_target_pairs={{6,2},{7,3},{14,10},{15,11},{22,18},{23,19},{30,26},{31,27},{38,34... | collective-permute-start | bytes 786440 | tf_op jit(solution)/shard_map/ppermute | solution.py:99
  130.1 5.0 %collective-permute-start.81 = (f32[512,256]{1,0:T(8,128)S(1)}, f32[512,256]{1,0:T(8,128)}, u32[]{:S(2)}, u32[]{:S(2)}) collective-permute-start(f32[512,256]{1,0:T(8,128)S(1)} %fusion.3.mine_ref), channel_id=1, source_target_pairs={{0,1},{1,0},{2,3},{3,2},{4,5},{5,4},{6,7},{7,6},{8,9},{9,8},{10,11... | collective-permute-start | bytes 1572872 | tf_op jit(solution)/shard_map/ppermute | solution.py:165
  (3 other events, 26.6 us)

commit v10 on v9

--- a/solution.py
+++ b/solution.py
@@ -129,11 +129,12 @@
         middle, tiled = lax.switch(which, leads, block, own, first)
         tiled, later = lax.optimization_barrier((tiled, later))
         later = later[0][step], later[1][step], later[2], later[3]
+        halves = lax.optimization_barrier((middle[:size], middle[size:], tiled))
         up = from_class(middle, 3, 4, 1)
         down = from_class(middle, 3, 4, -1)
-        top = from_class(middle[:size], 3, 4, 2)
-        bottom = from_class(middle[size:], 3, 4, -2)
-        gathered = exchange(tiled)
+        top = from_class(halves[0], 3, 4, 2)
+        bottom = from_class(halves[1], 3, 4, -2)
+        gathered = exchange(halves[2])
         near = my_z & 3
         up, later = lax.optimization_barrier((up, later))
         both = jnp.concatenate([top, bottom], axis=0)

time: 140 us -> 137 us (0.979)
  waiting for transfers between devices: 63.8 us -> 58.9 us
  local copies, waits for them, and re-layouts: 9.98 us -> 11.9 us
  other arithmetic: 4.47 us -> 6.06 us
    ppermute x15, waiting for transfers between devices: 51.8 us -> 46.8 us  [send_z(): return lax.ppermute(value, 'col', pairs)]
    slice x2, local copies, waits for them, and re-layouts: 1.59 us -> 3.53 us  [fetch(): halves = lax.optimization_barrier((middle[:size], middle[size:], tiled))]
    select_n x2, other arithmetic: 2.41 us -> 3.99 us  [run(): middle = jnp.where(dist == hop % n_z, value, middle)]
    ppermute x15, starting transfers between devices: 15.8 us -> 14.3 us  [send_z(): return lax.ppermute(value, 'col', pairs)]
  transfers between devices with their start and end apart: 21 -> 21, of which waited for: 5 -> 6; matrix products, arithmetic and copies ran while one was open for 8% -> 8% of each run, Pallas kernels for 1% -> 2%
where the time goes in v10:
time: 137 us; the launch traced here: 135 us
  waiting for transfers between devices  58.9 us (43%)
  starting transfers between devices  45.1 us (33%)
  local copies, waits for them, and re-layouts  11.9 us (9%)
  Pallas kernels  8.72 us (6%)
  other arithmetic  6.06 us (4%)
  loops' own time  3.18 us (2%)
  between operations  1.44 us (1%)
    ppermute x15, waiting for transfers between devices, send_z(): return lax.ppermute(value, 'col', pairs)  46.8 us
    all_to_all x4, starting transfers between devices, exchange(): return lax.all_to_all(value, 'row', 0, 0, tiled=True)  22.7 us
    ppermute x15, starting transfers between devices, send_z(): return lax.ppermute(value, 'col', pairs)  14.3 us
    all_to_all x4, waiting for transfers between devices, exchange(): return lax.all_to_all(value, 'row', 0, 0, tiled=True)  11.5 us
    ppermute x2, starting transfers between devices, local(): other = lax.ppermute(mine, 'col', [(i, i ^ 1) for i in range(n_col)])  8.11 us
    pallas_call x2, Pallas kernels, local(): pl.pallas_call(functools.partial(late_kernel, n_row, step, n_steps), out_...  6.68 us
    squeeze x3, local copies, waits for them, and re-layouts, fetch(): later = (later[0][step], later[1][step], later[2], later[3])  4.31 us
    select_n x2, other arithmetic, run(): middle = jnp.where(dist == hop % n_z, value, middle)  3.99 us
  transfers between devices with their start and end apart: 21, of which 6 were waited for; matrix products, arithmetic and copies ran while one was open for 8% of the time, Pallas kernels for 2%

profile of v10, /device:TPU:35, one launch (start us, length us, event | category | flops | bytes accessed | tf_op | source)
XLA Modules:
  0.0 135.3 jit_solution(3670705623989296396)
XLA Ops:
  0.7 23.5 %conditional.2 = (f32[512,256]{1,0:T(8,128)}, f32[512,256]{1,0:T(8,128)}, f32[256,256]{1,0:T(8,128)}, f32[256,256]{1,0:T(8,128)S(1)}) conditional(s32[]{:T(128)} %clamp.6, (s32[]{:T(128)}, s32[]{:T(128)}, f32[512,256]{1,0:T(8,128)}) %tuple.181, (s32[]{:T(128)}, s32[]{:T(128)}, f32[512,256]{1,0:T(8,128)}) %tuple.182, ...), branch_computations={%region_0.1_spmd, %region_1.2_spmd, %region_2.3_spmd, %region_3.4_... | conditional | flops 524301 | bytes 14516596 | solution.py:129
  4.2 1.7 %constant_dynamic-slice_fusion.5 = f32[256,256]{1,0:T(8,128)} fusion(f32[512,256]{1,0:T(8,128)} %get-tuple-element.162, u32[]{:T(128)S(6)} %convert_element_type.64), kind=kLoop, calls=%fused_computation.8 | loop fusion | bytes 524292 | tf_op jit(solution)/shard_map/cond/branch_2_fun/dynamic_slice | solution.py:113
  5.8 6.9 %all-to-all-start.2 = ((f32[16,16,256]{2,1,0:T(8,128)}), f32[16,16,256]{2,1,0:T(8,128)S(1)}, u32[]{:S(2)}, u32[]{:S(2)}) async-start(f32[16,16,256]{2,1,0:T(8,128)} %bitcast.6), calls=%async_computation.2 | async-start | bytes 524288 | tf_op jit(solution)/shard_map/cond/branch_2_fun/all_to_all | solution.py:105
  14.1 5.4 %all-to-all-done.2 = f32[16,16,256]{2,1,0:T(8,128)S(1)} async-done(((f32[16,16,256]{2,1,0:T(8,128)}), f32[16,16,256]{2,1,0:T(8,128)S(1)}, u32[]{:S(2)}, u32[]{:S(2)}) %all-to-all-start.2) | async-done | bytes 262176 | tf_op jit(solution)/shard_map/cond/branch_2_fun/all_to_all | solution.py:105
  20.4 2.0 %select_select_fusion.2 = f32[512,256]{1,0:T(8,128)} fusion(f32[512,256]{1,0:T(8,128)S(1)} %collective-permute-done.8, f32[512,256]{1,0:T(8,128)S(1)} %collective-permute-done.9, f32[512,256]{1,0:T(8,128)S(1)} %collective-permute-done.10, f32[512,256]{1,0:T(8,128)S(1)} %collective-permute-done.11, f32[512,256]{1,0:T(8,128)} %get-tuple-element.162, ...), kind=kLoop, calls=%fused_computation.6 | loop fusion | flops 524288 | bytes 3145732 | tf_op jit(solution)/shard_map/cond/branch_2_fun/jit(_where)/select_n | solution.py:118
  22.4 1.8 %fusion.6 = (f32[256,256]{1,0:T(8,128)S(1)}, f32[256,256]{1,0:T(8,128)}) fusion(f32[512,256]{1,0:T(8,128)} %select_select_fusion.2), kind=kLoop, calls=%fused_computation.63 | loop fusion | bytes 1048576 | tf_op jit(solution)/shard_map/slice | solution.py:132
  24.9 1.5 %collective-permute-start.73 = (f32[512,256]{1,0:T(8,128)}, f32[512,256]{1,0:T(8,128)}, u32[]{:S(2)}, u32[]{:S(2)}) collective-permute-start(f32[512,256]{1,0:T(8,128)} %get-tuple-element.297), channel_id=1, source_target_pairs={{6,4},{7,5},{14,12},{15,13},{22,20},{23,21},{30,28},{31,29},{38,36... | collective-permute-start | bytes 1572872 | tf_op jit(solution)/shard_map/ppermute | solution.py:99
  27.1 4.2 %all-to-all-start.20 = ((f32[16,32,256]{2,1,0:T(8,128)}), f32[16,32,256]{2,1,0:T(8,128)S(1)}, u32[]{:S(2)}, u32[]{:S(2)}) async-start(f32[16,32,256]{2,1,0:T(8,128)} %bitcast.65), calls=%async_computation.20 | async-start | bytes 1048576 | tf_op jit(solution)/shard_map/all_to_all | solution.py:105
  34.0 1.7 %slice_bitcast_fusion.2 = (f32[512,512]{1,0:T(8,128)S(1)}, f32[512,512]{1,0:T(8,128)S(1)}) fusion(f32[2,512,512]{2,1,0:T(8,128)} %param.31, f32[2,512,512]{2,1,0:T(8,128)} %param.30), kind=kLoop, calls=%fused_computation.52 | loop fusion | bytes 4194304 | tf_op jit(solution)/shard_map/squeeze | solution.py:131
  35.7 24.0 %collective-permute-done.74 = f32[256,256]{1,0:T(8,128)} collective-permute-done((f32[256,256]{1,0:T(8,128)}, f32[256,256]{1,0:T(8,128)}, u32[]{:S(2)}, u32[]{:S(2)}) %collective-permute-start.74) | collective-permute-done | bytes 262176 | tf_op jit(solution)/shard_map/ppermute | solution.py:99
  59.8 3.8 %collective-permute-done.75 = f32[256,256]{1,0:T(8,128)} collective-permute-done((f32[256,256]{1,0:T(8,128)S(1)}, f32[256,256]{1,0:T(8,128)}, u32[]{:S(2)}, u32[]{:S(2)}) %collective-permute-start.75) | collective-permute-done | bytes 262176 | tf_op jit(solution)/shard_map/ppermute | solution.py:99
  64.8 4.8 %collective-permute-start.76 = (f32[512,256]{1,0:T(8,128)S(1)}, f32[512,256]{1,0:T(8,128)}, u32[]{:S(2)}, u32[]{:S(2)}) collective-permute-start(f32[512,256]{1,0:T(8,128)S(1)} %fusion.1.mine_ref), channel_id=1, source_target_pairs={{0,1},{1,0},{2,3},{3,2},{4,5},{5,4},{6,7},{7,6},{8,9},{9,8},{10,11... | collective-permute-start | bytes 1572872 | tf_op jit(solution)/shard_map/ppermute | solution.py:166
  71.8 3.5 %late.2 = (f32[512,256]{1,0:T(8,128)}, f32[256,256]{1,0:T(8,128)}) custom-call(s32[8]{0:T(128)S(1)} %pad_add_fusion.flags, f32[512,256]{1,0:T(8,128)} %collective-permute-done.76.other_ref, f32[512,512]{1,0:T(8,128)S(1)} %get-tuple-element.314.part_ref, f32[512,256]{1,0:T(8,128)S(1)} %get-tuple-element.315.rows_ref, ...), custom_call_target="tpu_custom_call" | custom-call | flops 805306368 | bytes 3145728 | tf_op jit(solution)/shard_map/late/pallas_call | solution.py:182
  75.4 20.5 %conditional.3 = (f32[512,256]{1,0:T(8,128)}, f32[512,256]{1,0:T(8,128)}, f32[256,256]{1,0:T(8,128)}, f32[256,256]{1,0:T(8,128)S(1)}) conditional(s32[]{:T(128)} %clamp.7, (s32[]{:T(128)}, s32[]{:T(128)}, f32[512,256]{1,0:T(8,128)}, f32[256,256]{1,0:T(8,128)}) %tuple.136, (s32[]{:T(128)}, s32[]{:T(128)}, ...), branch_computations={%region_10.11_spmd, %region_11.12_spmd, %region_12.13_spmd, %regio... | conditional | flops 524298 | bytes 13992272 | solution.py:129
  77.5 6.7 %all-to-all-start.19 = ((f32[16,16,256]{2,1,0:T(8,128)}), f32[16,16,256]{2,1,0:T(8,128)S(1)}, u32[]{:S(2)}, u32[]{:S(2)}) async-start(f32[16,16,256]{2,1,0:T(8,128)} %bitcast.57), calls=%async_computation.19 | async-start | bytes 524288 | tf_op jit(solution)/shard_map/cond/branch_9_fun/all_to_all | solution.py:105
  85.3 6.0 %all-to-all-done.19 = f32[16,16,256]{2,1,0:T(8,128)S(1)} async-done(((f32[16,16,256]{2,1,0:T(8,128)}), f32[16,16,256]{2,1,0:T(8,128)S(1)}, u32[]{:S(2)}, u32[]{:S(2)}) %all-to-all-start.19) | async-done | bytes 262176 | tf_op jit(solution)/shard_map/cond/branch_9_fun/all_to_all | solution.py:105
  92.2 2.0 %select_select_fusion.19 = f32[512,256]{1,0:T(8,128)} fusion(f32[512,256]{1,0:T(8,128)S(1)} %collective-permute-done.69, f32[512,256]{1,0:T(8,128)S(1)} %collective-permute-done.70, f32[512,256]{1,0:T(8,128)S(1)} %collective-permute-done.71, f32[512,256]{1,0:T(8,128)} %get-tuple-element.257, pred[]{:T(512)S(6)} %eq.228, pred[]{:T(512)S(6)} %eq.227, pred[]{:T(512)S(6)} %eq.226), kind=kLoop, calls=%fused_computation.48 | loop fusion | flops 393216 | bytes 2621443 | tf_op jit(solution)/shard_map/cond/branch_9_fun/jit(_where)/select_n | solution.py:118
  94.1 1.8 %fusion.23 = (f32[256,256]{1,0:T(8,128)S(1)}, f32[256,256]{1,0:T(8,128)}) fusion(f32[512,256]{1,0:T(8,128)} %select_select_fusion.19), kind=kLoop, calls=%fused_computation.80 | loop fusion | bytes 1048576 | tf_op jit(solution)/shard_map/slice | solution.py:132
  95.9 1.5 %collective-permute-start.78 = (f32[512,256]{1,0:T(8,128)}, f32[512,256]{1,0:T(8,128)}, u32[]{:S(2)}, u32[]{:S(2)}) collective-permute-start(f32[512,256]{1,0:T(8,128)} %get-tuple-element.318), channel_id=1, source_target_pairs={{6,4},{7,5},{14,12},{15,13},{22,20},{23,21},{30,28},{31,29},{38,36... | collective-permute-start | bytes 1572872 | tf_op jit(solution)/shard_map/ppermute | solution.py:99
  98.1 4.8 %all-to-all-start.21 = ((f32[16,32,256]{2,1,0:T(8,128)}), f32[16,32,256]{2,1,0:T(8,128)S(1)}, u32[]{:S(2)}, u32[]{:S(2)}) async-start(f32[16,32,256]{2,1,0:T(8,128)} %bitcast.69), calls=%async_computation.21 | async-start | bytes 1048576 | tf_op jit(solution)/shard_map/all_to_all | solution.py:105
  105.5 1.3 slice_bitcast_fusion.1.lower_ref
  108.1 18.9 %collective-permute-done.79 = f32[256,256]{1,0:T(8,128)S(1)} collective-permute-done((f32[256,256]{1,0:T(8,128)}, f32[256,256]{1,0:T(8,128)S(1)}, u32[]{:S(2)}, u32[]{:S(2)}) %collective-permute-start.79) | collective-permute-done | bytes 262176 | tf_op jit(solution)/shard_map/ppermute | solution.py:99
  127.2 3.3 %collective-permute-start.81 = (f32[512,256]{1,0:T(8,128)S(1)}, f32[512,256]{1,0:T(8,128)}, u32[]{:S(2)}, u32[]{:S(2)}) collective-permute-start(f32[512,256]{1,0:T(8,128)S(1)} %fusion.3.mine_ref), channel_id=1, source_target_pairs={{0,1},{1,0},{2,3},{3,2},{4,5},{5,4},{6,7},{7,6},{8,9},{9,8},{10,11... | collective-permute-start | bytes 1572872 | tf_op jit(solution)/shard_map/ppermute | solution.py:166
  132.1 3.1 %late.3 = f32[512,256]{1,0:T(8,128)} custom-call(s32[8]{0:T(128)S(1)} %pad_add_fusion.flags, f32[512,256]{1,0:T(8,128)} %collective-permute-done.81.other_ref, f32[512,512]{1,0:T(8,128)S(1)} %get-tuple-element.333.part_ref, f32[512,256]{1,0:T(8,128)S(1)} %get-tuple-element.334.rows_ref, f32[512,512]{1,0:T(8,128)S(1)} %slice_bitcast_fusion.upper_ref, ...), custom_call_target="tpu_custom_call" | custom-call | flops 805306368 | bytes 3145728 | tf_op jit(solution)/shard_map/late/pallas_call | solution.py:182
  (53 shorter events, 19.8 us)
Async XLA Ops:
  0.7 25.7 %copy-start.3 = (s32[2,1]{0,1:T(1,128)S(1)}, s32[2,1]{0,1:T(1,128)}, u32[]{:S(2)}) copy-start(s32[2,1]{0,1:T(1,128)} %param.28) | copy-start | bytes 28
  0.7 19.7 %collective-permute-start.11 = (f32[512,256]{1,0:T(8,128)}, f32[512,256]{1,0:T(8,128)S(1)}, u32[]{:S(2)}, u32[]{:S(2)}) collective-permute-start(f32[512,256]{1,0:T(8,128)} %get-tuple-element.162), channel_id=1, source_target_pairs={{4,6},{5,7},{12,14},{13,15},{20,22},{21,23},{28,30},{29,31},{36,38... | collective-permute-start | bytes 1572872 | tf_op jit(solution)/shard_map/cond/branch_2_fun/ppermute | solution.py:99
  1.4 19.0 %collective-permute-start.10 = (f32[512,256]{1,0:T(8,128)}, f32[512,256]{1,0:T(8,128)S(1)}, u32[]{:S(2)}, u32[]{:S(2)}) collective-permute-start(f32[512,256]{1,0:T(8,128)} %get-tuple-element.162), channel_id=1, source_target_pairs={{4,30},{5,31},{12,6},{13,7},{20,14},{21,15},{28,22},{29,23},{36,62... | collective-permute-start | bytes 1572872 | tf_op jit(solution)/shard_map/cond/branch_2_fun/ppermute | solution.py:99
  2.1 18.3 %collective-permute-start.9 = (f32[512,256]{1,0:T(8,128)}, f32[512,256]{1,0:T(8,128)S(1)}, u32[]{:S(2)}, u32[]{:S(2)}) collective-permute-start(f32[512,256]{1,0:T(8,128)} %get-tuple-element.162), channel_id=1, source_target_pairs={{4,14},{5,15},{20,30},{21,31},{36,46},{37,47},{52,62},{53,63},{68,... | collective-permute-start | bytes 1572872 | tf_op jit(solution)/shard_map/cond/branch_2_fun/ppermute | solution.py:99
  2.8 17.6 %collective-permute-start.8 = (f32[512,256]{1,0:T(8,128)}, f32[512,256]{1,0:T(8,128)S(1)}, u32[]{:S(2)}, u32[]{:S(2)}) collective-permute-start(f32[512,256]{1,0:T(8,128)} %get-tuple-element.162), channel_id=1, source_target_pairs={{4,22},{5,23},{20,6},{21,7},{36,54},{37,55},{52,38},{53,39},{68,86... | collective-permute-start | bytes 1572872 | tf_op jit(solution)/shard_map/cond/branch_2_fun/ppermute | solution.py:99
  5.8 13.7 %all-to-all-start.2 = ((f32[16,16,256]{2,1,0:T(8,128)}), f32[16,16,256]{2,1,0:T(8,128)S(1)}, u32[]{:S(2)}, u32[]{:S(2)}) async-start(f32[16,16,256]{2,1,0:T(8,128)} %bitcast.6), calls=%async_computation.2 | async-start | bytes 524288 | tf_op jit(solution)/shard_map/cond/branch_2_fun/all_to_all | solution.py:105
  24.2 11.5 %collective-permute-start.72 = (f32[512,256]{1,0:T(8,128)}, f32[512,256]{1,0:T(8,128)S(1)}, u32[]{:S(2)}, u32[]{:S(2)}) collective-permute-start(f32[512,256]{1,0:T(8,128)} %get-tuple-element.297), channel_id=1, source_target_pairs={{6,8},{7,9},{14,16},{15,17},{22,24},{23,25},{30,0},{31,1},{38,40},... | collective-permute-start | bytes 1572872 | tf_op jit(solution)/shard_map/ppermute | solution.py:99
  24.9 38.7 %collective-permute-start.73 = (f32[512,256]{1,0:T(8,128)}, f32[512,256]{1,0:T(8,128)}, u32[]{:S(2)}, u32[]{:S(2)}) collective-permute-start(f32[512,256]{1,0:T(8,128)} %get-tuple-element.297), channel_id=1, source_target_pairs={{6,4},{7,5},{14,12},{15,13},{22,20},{23,21},{30,28},{31,29},{38,36... | collective-permute-start | bytes 1572872 | tf_op jit(solution)/shard_map/ppermute | solution.py:99
  27.1 43.6 %all-to-all-start.20 = ((f32[16,32,256]{2,1,0:T(8,128)}), f32[16,32,256]{2,1,0:T(8,128)S(1)}, u32[]{:S(2)}, u32[]{:S(2)}) async-start(f32[16,32,256]{2,1,0:T(8,128)} %bitcast.65), calls=%async_computation.20 | async-start | bytes 1048576 | tf_op jit(solution)/shard_map/all_to_all | solution.py:105
  31.4 28.4 %collective-permute-start.74 = (f32[256,256]{1,0:T(8,128)}, f32[256,256]{1,0:T(8,128)}, u32[]{:S(2)}, u32[]{:S(2)}) collective-permute-start(f32[256,256]{1,0:T(8,128)} %get-tuple-element.309), channel_id=1, source_target_pairs={{6,10},{7,11},{14,18},{15,19},{22,26},{23,27},{30,2},{31,3},{38,42... | collective-permute-start | bytes 786440 | tf_op jit(solution)/shard_map/ppermute | solution.py:99
  32.7 30.9 %collective-permute-start.75 = (f32[256,256]{1,0:T(8,128)S(1)}, f32[256,256]{1,0:T(8,128)}, u32[]{:S(2)}, u32[]{:S(2)}) collective-permute-start(f32[256,256]{1,0:T(8,128)S(1)} %get-tuple-element.310), channel_id=1, source_target_pairs={{6,2},{7,3},{14,10},{15,11},{22,18},{23,19},{30,26},{31,27},{38,34... | collective-permute-start | bytes 786440 | tf_op jit(solution)/shard_map/ppermute | solution.py:99
  35.7 33.9 %copy-start.4 = (s32[2]{0:T(128)S(1)}, s32[2]{0:T(128)}, u32[]{:S(2)}) copy-start(s32[2]{0:T(128)} %param.29) | copy-start | bytes 28
  35.7 27.9 %copy-start.1 = (f32[512,256]{1,0:T(8,128)}, f32[512,256]{1,0:T(8,128)S(1)}, u32[]{:S(2)}) copy-start(f32[512,256]{1,0:T(8,128)S(1)} %collective-permute-done.72) | copy-start | bytes 1572868
  64.8 7.0 %collective-permute-start.76 = (f32[512,256]{1,0:T(8,128)S(1)}, f32[512,256]{1,0:T(8,128)}, u32[]{:S(2)}, u32[]{:S(2)}) collective-permute-start(f32[512,256]{1,0:T(8,128)S(1)} %fusion.1.mine_ref), channel_id=1, source_target_pairs={{0,1},{1,0},{2,3},{3,2},{4,5},{5,4},{6,7},{7,6},{8,9},{9,8},{10,11... | collective-permute-start | bytes 1572872 | tf_op jit(solution)/shard_map/ppermute | solution.py:166
  75.4 16.8 %collective-permute-start.71 = (f32[512,256]{1,0:T(8,128)}, f32[512,256]{1,0:T(8,128)S(1)}, u32[]{:S(2)}, u32[]{:S(2)}) collective-permute-start(f32[512,256]{1,0:T(8,128)} %get-tuple-element.257), channel_id=1, source_target_pairs={{30,22},{31,23},{62,54},{63,55},{94,86},{95,87},{126,118},{127,119... | collective-permute-start | bytes 1572872 | tf_op jit(solution)/shard_map/cond/branch_9_fun/ppermute | solution.py:99
  76.1 16.1 %collective-permute-start.70 = (f32[512,256]{1,0:T(8,128)}, f32[512,256]{1,0:T(8,128)S(1)}, u32[]{:S(2)}, u32[]{:S(2)}) collective-permute-start(f32[512,256]{1,0:T(8,128)} %get-tuple-element.257), channel_id=1, source_target_pairs={{30,6},{31,7},{62,38},{63,39},{94,70},{95,71},{126,102},{127,103},... | collective-permute-start | bytes 1572872 | tf_op jit(solution)/shard_map/cond/branch_9_fun/ppermute | solution.py:99
  76.8 15.4 %collective-permute-start.69 = (f32[512,256]{1,0:T(8,128)}, f32[512,256]{1,0:T(8,128)S(1)}, u32[]{:S(2)}, u32[]{:S(2)}) collective-permute-start(f32[512,256]{1,0:T(8,128)} %get-tuple-element.257), channel_id=1, source_target_pairs={{30,14},{31,15},{62,46},{63,47},{94,78},{95,79},{126,110},{127,111... | collective-permute-start | bytes 1572872 | tf_op jit(solution)/shard_map/cond/branch_9_fun/ppermute | solution.py:99
  77.5 13.8 %all-to-all-start.19 = ((f32[16,16,256]{2,1,0:T(8,128)}), f32[16,16,256]{2,1,0:T(8,128)S(1)}, u32[]{:S(2)}, u32[]{:S(2)}) async-start(f32[16,16,256]{2,1,0:T(8,128)} %bitcast.57), calls=%async_computation.19 | async-start | bytes 524288 | tf_op jit(solution)/shard_map/cond/branch_9_fun/all_to_all | solution.py:105
  95.9 31.1 %collective-permute-start.78 = (f32[512,256]{1,0:T(8,128)}, f32[512,256]{1,0:T(8,128)}, u32[]{:S(2)}, u32[]{:S(2)}) collective-permute-start(f32[512,256]{1,0:T(8,128)} %get-tuple-element.318), channel_id=1, source_target_pairs={{6,4},{7,5},{14,12},{15,13},{22,20},{23,21},{30,28},{31,29},{38,36... | collective-permute-start | bytes 1572872 | tf_op jit(solution)/shard_map/ppermute | solution.py:99
  97.4 10.7 %collective-permute-start.77 = (f32[512,256]{1,0:T(8,128)}, f32[512,256]{1,0:T(8,128)S(1)}, u32[]{:S(2)}, u32[]{:S(2)}) collective-permute-start(f32[512,256]{1,0:T(8,128)} %get-tuple-element.318), channel_id=1, source_target_pairs={{6,8},{7,9},{14,16},{15,17},{22,24},{23,25},{30,0},{31,1},{38,40},... | collective-permute-start | bytes 1572872 | tf_op jit(solution)/shard_map/ppermute | solution.py:99
  98.1 32.4 %all-to-all-start.21 = ((f32[16,32,256]{2,1,0:T(8,128)}), f32[16,32,256]{2,1,0:T(8,128)S(1)}, u32[]{:S(2)}, u32[]{:S(2)}) async-start(f32[16,32,256]{2,1,0:T(8,128)} %bitcast.69), calls=%async_computation.21 | async-start | bytes 1048576 | tf_op jit(solution)/shard_map/all_to_all | solution.py:105
  102.9 24.1 %collective-permute-start.79 = (f32[256,256]{1,0:T(8,128)}, f32[256,256]{1,0:T(8,128)S(1)}, u32[]{:S(2)}, u32[]{:S(2)}) collective-permute-start(f32[256,256]{1,0:T(8,128)} %get-tuple-element.328), channel_id=1, source_target_pairs={{6,10},{7,11},{14,18},{15,19},{22,26},{23,27},{30,2},{31,3},{38,42... | collective-permute-start | bytes 786440 | tf_op jit(solution)/shard_map/ppermute | solution.py:99
  104.2 22.8 %collective-permute-start.80 = (f32[256,256]{1,0:T(8,128)S(1)}, f32[256,256]{1,0:T(8,128)S(1)}, u32[]{:S(2)}, u32[]{:S(2)}) collective-permute-start(f32[256,256]{1,0:T(8,128)S(1)} %get-tuple-element.329), channel_id=1, source_target_pairs={{6,2},{7,3},{14,10},{15,11},{22,18},{23,19},{30,26},{31,27},{38,34... | collective-permute-start | bytes 786440 | tf_op jit(solution)/shard_map/ppermute | solution.py:99
  127.2 4.9 %collective-permute-start.81 = (f32[512,256]{1,0:T(8,128)S(1)}, f32[512,256]{1,0:T(8,128)}, u32[]{:S(2)}, u32[]{:S(2)}) collective-permute-start(f32[512,256]{1,0:T(8,128)S(1)} %fusion.3.mine_ref), channel_id=1, source_target_pairs={{0,1},{1,0},{2,3},{3,2},{4,5},{5,4},{6,7},{7,6},{8,9},{9,8},{10,11... | collective-permute-start | bytes 1572872 | tf_op jit(solution)/shard_map/ppermute | solution.py:166
  (3 other events, 45.7 us)

commit v11 on v9

--- a/solution.py
+++ b/solution.py
@@ -113,10 +113,10 @@
                 own = lax.dynamic_slice_in_dim(block, own_at.astype(jnp.uint32), size, 0)
             chunk_at = ((first & (n_row - 1)) * piece).astype(jnp.uint32)
             chunk = lax.dynamic_slice_in_dim(exchange(own), chunk_at, 2 * piece, 0)
-            tiled, middle = lax.optimization_barrier((jnp.tile(chunk, (n_row, 1)), block))
+            chunk, middle = lax.optimization_barrier((chunk, block))
             for (_, _, hop), value in zip(sends, got):
                 middle = jnp.where(dist == hop % n_z, value, middle)
-            return middle, tiled
+            return middle, chunk
 
         return run
 
@@ -126,14 +126,14 @@
         which = jnp.where(
             plane & 3 == 3, 6 + (plane >> 2), (plane & 3) + 3 * ((plane >> 2) & 1)
         )
-        middle, tiled = lax.switch(which, leads, block, own, first)
-        tiled, later = lax.optimization_barrier((tiled, later))
+        middle, chunk = lax.switch(which, leads, block, own, first)
+        chunk, later = lax.optimization_barrier((chunk, later))
         later = later[0][step], later[1][step], later[2], later[3]
         up = from_class(middle, 3, 4, 1)
         down = from_class(middle, 3, 4, -1)
         top = from_class(middle[:size], 3, 4, 2)
         bottom = from_class(middle[size:], 3, 4, -2)
-        gathered = exchange(tiled)
+        gathered = exchange(jnp.tile(chunk, (n_row, 1)))
         near = my_z & 3
         up, later = lax.optimization_barrier((up, later))
         both = jnp.concatenate([top, bottom], axis=0)

time: 140 us -> 133 us (0.950)
  the two profiles are of different devices: /device:TPU:35 before, /device:TPU:61 now
where the time goes in v11:
time: 133 us; the launch traced here: 135 us
  waiting for transfers between devices  54.6 us (41%)
  starting transfers between devices  51.1 us (38%)
  local copies, waits for them, and re-layouts  9.9 us (7%)
  Pallas kernels  8.7 us (7%)
  other arithmetic  5.48 us (4%)
  loops' own time  3.62 us (3%)
  between operations  1.52 us (1%)
    ppermute x15, waiting for transfers between devices, send_z(): return lax.ppermute(value, 'col', pairs)  48 us
    all_to_all x4, starting transfers between devices, exchange(): return lax.all_to_all(value, 'row', 0, 0, tiled=True)  27.8 us
    ppermute x15, starting transfers between devices, send_z(): return lax.ppermute(value, 'col', pairs)  15.8 us
    ppermute x2, starting transfers between devices, local(): other = lax.ppermute(mine, 'col', [(i, i ^ 1) for i in range(n_col)])  7.46 us
    pallas_call x2, Pallas kernels, local(): pl.pallas_call(functools.partial(late_kernel, n_row, step, n_steps), out_...  6.66 us
    all_to_all x4, waiting for transfers between devices, exchange(): return lax.all_to_all(value, 'row', 0, 0, tiled=True)  5.94 us
    squeeze x3, local copies, waits for them, and re-layouts, fetch(): later = (later[0][step], later[1][step], later[2], later[3])  4.3 us
    another operation x2, loops' own time, fetch(): middle, chunk = lax.switch(which, leads, block, own, first)  3.62 us
  transfers between devices with their start and end apart: 21, of which 6 were waited for; matrix products, arithmetic and copies ran while one was open for 10% of the time, Pallas kernels for 2%

profile of v11, /device:TPU:61, one launch (start us, length us, event | category | flops | bytes accessed | tf_op | source)
XLA Modules:
  0.0 134.9 jit_solution(4181768652920686962)
XLA Ops:
  0.7 16.4 %conditional.2 = (f32[512,256]{1,0:T(8,128)S(1)}, f32[32,256]{1,0:T(8,128)S(1)}) conditional(s32[]{:T(128)} %clamp.6, (s32[]{:T(128)}, s32[]{:T(128)}, f32[512,256]{1,0:T(8,128)}) %tuple.139, (s32[]{:T(128)}, s32[]{:T(128)}, f32[512,256]{1,0:T(8,128)}) %tuple.140, (s32[]{:T(128)}, s32[]{:T(128)}, ...), branch_computations={%region_0.1_spmd, %region_1.2_spmd, %region_2.3_spmd, %region_3.4_... | conditional | flops 524301 | bytes 12910948 | solution.py:129
  3.5 1.7 %constant_dynamic-slice_fusion.19 = f32[256,256]{1,0:T(8,128)} fusion(f32[512,256]{1,0:T(8,128)} %get-tuple-element.193, u32[]{:T(128)S(6)} %convert_element_type.78), kind=kLoop, calls=%fused_computation.29 | loop fusion | bytes 524292 | tf_op jit(solution)/shard_map/cond/branch_9_fun/dynamic_slice | solution.py:113
  5.2 6.6 %all-to-all-start.9 = ((f32[16,16,256]{2,1,0:T(8,128)}), f32[16,16,256]{2,1,0:T(8,128)S(1)}, u32[]{:S(2)}, u32[]{:S(2)}) async-start(f32[16,16,256]{2,1,0:T(8,128)} %bitcast.18), calls=%async_computation.9 | async-start | bytes 524288 | tf_op jit(solution)/shard_map/cond/branch_9_fun/all_to_all | solution.py:105
  13.0 2.8 %all-to-all-done.9 = f32[16,16,256]{2,1,0:T(8,128)S(1)} async-done(((f32[16,16,256]{2,1,0:T(8,128)}), f32[16,16,256]{2,1,0:T(8,128)S(1)}, u32[]{:S(2)}, u32[]{:S(2)}) %all-to-all-start.9) | async-done | bytes 262176 | tf_op jit(solution)/shard_map/cond/branch_9_fun/all_to_all | solution.py:105
  17.1 1.5 %collective-permute-start.72 = (f32[512,256]{1,0:T(8,128)S(1)}, f32[512,256]{1,0:T(8,128)}, u32[]{:S(2)}, u32[]{:S(2)}) collective-permute-start(f32[512,256]{1,0:T(8,128)S(1)} %get-tuple-element.283), channel_id=1, source_target_pairs={{6,8},{7,9},{14,16},{15,17},{22,24},{23,25},{30,0},{31,1},{38,40},... | collective-permute-start | bytes 1572872 | tf_op jit(solution)/shard_map/ppermute | solution.py:99
  18.6 1.4 %collective-permute-start.73 = (f32[512,256]{1,0:T(8,128)S(1)}, f32[512,256]{1,0:T(8,128)}, u32[]{:S(2)}, u32[]{:S(2)}) collective-permute-start(f32[512,256]{1,0:T(8,128)S(1)} %get-tuple-element.283), channel_id=1, source_target_pairs={{6,4},{7,5},{14,12},{15,13},{22,20},{23,21},{30,28},{31,29},{38,36... | collective-permute-start | bytes 1572872 | tf_op jit(solution)/shard_map/ppermute | solution.py:99
  22.0 1.3 collective-permute-start.75
  25.0 7.0 %all-to-all-start.20 = ((f32[16,32,256]{2,1,0:T(8,128)}), f32[16,32,256]{2,1,0:T(8,128)S(1)}, u32[]{:S(2)}, u32[]{:S(2)}) async-start(f32[16,32,256]{2,1,0:T(8,128)} %tile.4), calls=%async_computation.20 | async-start | bytes 1048576 | tf_op jit(solution)/shard_map/all_to_all | solution.py:105
  32.0 1.7 %slice_bitcast_fusion.2 = (f32[512,512]{1,0:T(8,128)S(1)}, f32[512,512]{1,0:T(8,128)S(1)}) fusion(f32[2,512,512]{2,1,0:T(8,128)} %param.31, f32[2,512,512]{2,1,0:T(8,128)} %param.30), kind=kLoop, calls=%fused_computation.52 | loop fusion | bytes 4194304 | tf_op jit(solution)/shard_map/squeeze | solution.py:131
  33.7 22.8 %collective-permute-done.74 = f32[256,256]{1,0:T(8,128)} collective-permute-done((f32[256,256]{1,0:T(8,128)}, f32[256,256]{1,0:T(8,128)}, u32[]{:S(2)}, u32[]{:S(2)}) %collective-permute-start.74) | collective-permute-done | bytes 262176 | tf_op jit(solution)/shard_map/ppermute | solution.py:99
  57.8 4.1 %collective-permute-start.76 = (f32[512,256]{1,0:T(8,128)S(1)}, f32[512,256]{1,0:T(8,128)}, u32[]{:S(2)}, u32[]{:S(2)}) collective-permute-start(f32[512,256]{1,0:T(8,128)S(1)} %fusion.1.mine_ref), channel_id=1, source_target_pairs={{0,1},{1,0},{2,3},{3,2},{4,5},{5,4},{6,7},{7,6},{8,9},{9,8},{10,11... | collective-permute-start | bytes 1572872 | tf_op jit(solution)/shard_map/ppermute | solution.py:165
  64.2 3.5 %late.2 = (f32[512,256]{1,0:T(8,128)}, f32[256,256]{1,0:T(8,128)}) custom-call(s32[8]{0:T(128)S(1)} %pad_add_fusion.flags, f32[512,256]{1,0:T(8,128)} %collective-permute-done.76.other_ref, f32[512,512]{1,0:T(8,128)S(1)} %get-tuple-element.295.part_ref, f32[512,256]{1,0:T(8,128)S(1)} %get-tuple-element.296.rows_ref, ...), custom_call_target="tpu_custom_call" | custom-call | flops 805306368 | bytes 3145728 | tf_op jit(solution)/shard_map/late/pallas_call | solution.py:181
  67.7 15.3 %conditional.3 = (f32[512,256]{1,0:T(8,128)S(1)}, f32[32,256]{1,0:T(8,128)S(1)}) conditional(s32[]{:T(128)} %clamp.7, (s32[]{:T(128)}, s32[]{:T(128)}, f32[512,256]{1,0:T(8,128)}, f32[256,256]{1,0:T(8,128)}) %tuple.113, (s32[]{:T(128)}, s32[]{:T(128)}, f32[512,256]{1,0:T(8,128)}, f32[256,256]{1,0:T(8,128)}) %tuple.113, ...), branch_computations={%region_10.11_spmd, %region_11.12_spmd, %region_12.13_spmd, %regio... | conditional | flops 524298 | bytes 12386624 | solution.py:129
  70.5 6.6 %all-to-all-start.12 = ((f32[16,16,256]{2,1,0:T(8,128)}), f32[16,16,256]{2,1,0:T(8,128)S(1)}, u32[]{:S(2)}, u32[]{:S(2)}) async-start(f32[16,16,256]{2,1,0:T(8,128)} %bitcast.24), calls=%async_computation.12 | async-start | bytes 524288 | tf_op jit(solution)/shard_map/cond/branch_2_fun/all_to_all | solution.py:105
  78.3 3.1 %all-to-all-done.12 = f32[16,16,256]{2,1,0:T(8,128)S(1)} async-done(((f32[16,16,256]{2,1,0:T(8,128)}), f32[16,16,256]{2,1,0:T(8,128)S(1)}, u32[]{:S(2)}, u32[]{:S(2)}) %all-to-all-start.12) | async-done | bytes 262176 | tf_op jit(solution)/shard_map/cond/branch_2_fun/all_to_all | solution.py:105
  83.0 1.5 %collective-permute-start.77 = (f32[512,256]{1,0:T(8,128)S(1)}, f32[512,256]{1,0:T(8,128)}, u32[]{:S(2)}, u32[]{:S(2)}) collective-permute-start(f32[512,256]{1,0:T(8,128)S(1)} %get-tuple-element.299), channel_id=1, source_target_pairs={{6,8},{7,9},{14,16},{15,17},{22,24},{23,25},{30,0},{31,1},{38,40},... | collective-permute-start | bytes 1572872 | tf_op jit(solution)/shard_map/ppermute | solution.py:99
  85.2 1.5 %collective-permute-start.78 = (f32[512,256]{1,0:T(8,128)S(1)}, f32[512,256]{1,0:T(8,128)}, u32[]{:S(2)}, u32[]{:S(2)}) collective-permute-start(f32[512,256]{1,0:T(8,128)S(1)} %get-tuple-element.299), channel_id=1, source_target_pairs={{6,4},{7,5},{14,12},{15,13},{22,20},{23,21},{30,28},{31,29},{38,36... | collective-permute-start | bytes 1572872 | tf_op jit(solution)/shard_map/ppermute | solution.py:99
  90.1 7.7 %all-to-all-start.21 = ((f32[16,32,256]{2,1,0:T(8,128)}), f32[16,32,256]{2,1,0:T(8,128)S(1)}, u32[]{:S(2)}, u32[]{:S(2)}) async-start(f32[16,32,256]{2,1,0:T(8,128)} %tile.5), calls=%async_computation.21 | async-start | bytes 1048576 | tf_op jit(solution)/shard_map/all_to_all | solution.py:105
  97.8 1.3 slice_bitcast_fusion.upper_ref
  99.1 1.3 slice_bitcast_fusion.1.lower_ref
  100.4 23.1 %collective-permute-done.79 = f32[256,256]{1,0:T(8,128)} collective-permute-done((f32[256,256]{1,0:T(8,128)}, f32[256,256]{1,0:T(8,128)}, u32[]{:S(2)}, u32[]{:S(2)}) %collective-permute-start.79) | collective-permute-done | bytes 262176 | tf_op jit(solution)/shard_map/ppermute | solution.py:99
  123.5 2.1 %collective-permute-done.80 = f32[256,256]{1,0:T(8,128)} collective-permute-done((f32[256,256]{1,0:T(8,128)S(1)}, f32[256,256]{1,0:T(8,128)}, u32[]{:S(2)}, u32[]{:S(2)}) %collective-permute-start.80) | collective-permute-done | bytes 262176 | tf_op jit(solution)/shard_map/ppermute | solution.py:99
  126.7 3.4 %collective-permute-start.81 = (f32[512,256]{1,0:T(8,128)S(1)}, f32[512,256]{1,0:T(8,128)}, u32[]{:S(2)}, u32[]{:S(2)}) collective-permute-start(f32[512,256]{1,0:T(8,128)S(1)} %fusion.3.mine_ref), channel_id=1, source_target_pairs={{0,1},{1,0},{2,3},{3,2},{4,5},{5,4},{6,7},{7,6},{8,9},{9,8},{10,11... | collective-permute-start | bytes 1572872 | tf_op jit(solution)/shard_map/ppermute | solution.py:165
  131.7 3.1 %late.3 = f32[512,256]{1,0:T(8,128)} custom-call(s32[8]{0:T(128)S(1)} %pad_add_fusion.flags, f32[512,256]{1,0:T(8,128)} %collective-permute-done.81.other_ref, f32[512,512]{1,0:T(8,128)S(1)} %get-tuple-element.309.part_ref, f32[512,256]{1,0:T(8,128)S(1)} %get-tuple-element.310.rows_ref, f32[512,512]{1,0:T(8,128)S(1)} %slice_bitcast_fusion.upper_ref, ...), custom_call_target="tpu_custom_call" | custom-call | flops 805306368 | bytes 3145728 | tf_op jit(solution)/shard_map/late/pallas_call | solution.py:181
  (53 shorter events, 20.8 us)
Async XLA Ops:
  0.7 22.7 %copy-start.5 = (s32[2,2]{1,0:T(2,128)S(1)}, s32[2,2]{1,0:T(2,128)}, u32[]{:S(2)}) copy-start(s32[2,2]{1,0:T(2,128)} %param.27) | copy-start | bytes 52
  0.7 22.8 %copy-start.3 = (s32[2,1]{0,1:T(1,128)S(1)}, s32[2,1]{0,1:T(1,128)}, u32[]{:S(2)}) copy-start(s32[2,1]{0,1:T(1,128)} %param.28) | copy-start | bytes 28
  0.7 15.1 %collective-permute-start.33 = (f32[512,256]{1,0:T(8,128)}, f32[512,256]{1,0:T(8,128)S(1)}, u32[]{:S(2)}, u32[]{:S(2)}) collective-permute-start(f32[512,256]{1,0:T(8,128)} %get-tuple-element.193), channel_id=1, source_target_pairs={{30,14},{31,15},{62,46},{63,47},{94,78},{95,79},{126,110},{127,111... | collective-permute-start | bytes 1572872 | tf_op jit(solution)/shard_map/cond/branch_9_fun/ppermute | solution.py:99
  1.4 14.4 %collective-permute-start.34 = (f32[512,256]{1,0:T(8,128)}, f32[512,256]{1,0:T(8,128)S(1)}, u32[]{:S(2)}, u32[]{:S(2)}) collective-permute-start(f32[512,256]{1,0:T(8,128)} %get-tuple-element.193), channel_id=1, source_target_pairs={{30,6},{31,7},{62,38},{63,39},{94,70},{95,71},{126,102},{127,103},... | collective-permute-start | bytes 1572872 | tf_op jit(solution)/shard_map/cond/branch_9_fun/ppermute | solution.py:99
  2.1 13.7 %collective-permute-start.35 = (f32[512,256]{1,0:T(8,128)}, f32[512,256]{1,0:T(8,128)S(1)}, u32[]{:S(2)}, u32[]{:S(2)}) collective-permute-start(f32[512,256]{1,0:T(8,128)} %get-tuple-element.193), channel_id=1, source_target_pairs={{30,22},{31,23},{62,54},{63,55},{94,86},{95,87},{126,118},{127,119... | collective-permute-start | bytes 1572872 | tf_op jit(solution)/shard_map/cond/branch_9_fun/ppermute | solution.py:99
  5.2 10.7 %all-to-all-start.9 = ((f32[16,16,256]{2,1,0:T(8,128)}), f32[16,16,256]{2,1,0:T(8,128)S(1)}, u32[]{:S(2)}, u32[]{:S(2)}) async-start(f32[16,16,256]{2,1,0:T(8,128)} %bitcast.18), calls=%async_computation.9 | async-start | bytes 524288 | tf_op jit(solution)/shard_map/cond/branch_9_fun/all_to_all | solution.py:105
  17.1 16.6 %collective-permute-start.72 = (f32[512,256]{1,0:T(8,128)S(1)}, f32[512,256]{1,0:T(8,128)}, u32[]{:S(2)}, u32[]{:S(2)}) collective-permute-start(f32[512,256]{1,0:T(8,128)S(1)} %get-tuple-element.283), channel_id=1, source_target_pairs={{6,8},{7,9},{14,16},{15,17},{22,24},{23,25},{30,0},{31,1},{38,40},... | collective-permute-start | bytes 1572872 | tf_op jit(solution)/shard_map/ppermute | solution.py:99
  18.6 38.0 %collective-permute-start.73 = (f32[512,256]{1,0:T(8,128)S(1)}, f32[512,256]{1,0:T(8,128)}, u32[]{:S(2)}, u32[]{:S(2)}) collective-permute-start(f32[512,256]{1,0:T(8,128)S(1)} %get-tuple-element.283), channel_id=1, source_target_pairs={{6,4},{7,5},{14,12},{15,13},{22,20},{23,21},{30,28},{31,29},{38,36... | collective-permute-start | bytes 1572872 | tf_op jit(solution)/shard_map/ppermute | solution.py:99
  20.8 35.8 %collective-permute-start.74 = (f32[256,256]{1,0:T(8,128)}, f32[256,256]{1,0:T(8,128)}, u32[]{:S(2)}, u32[]{:S(2)}) collective-permute-start(f32[256,256]{1,0:T(8,128)} %get-tuple-element.313), channel_id=1, source_target_pairs={{6,10},{7,11},{14,18},{15,19},{22,26},{23,27},{30,2},{31,3},{38,42... | collective-permute-start | bytes 786440 | tf_op jit(solution)/shard_map/ppermute | solution.py:99
  22.0 34.5 %collective-permute-start.75 = (f32[256,256]{1,0:T(8,128)S(1)}, f32[256,256]{1,0:T(8,128)}, u32[]{:S(2)}, u32[]{:S(2)}) collective-permute-start(f32[256,256]{1,0:T(8,128)S(1)} %get-tuple-element.314), channel_id=1, source_target_pairs={{6,2},{7,3},{14,10},{15,11},{22,18},{23,19},{30,26},{31,27},{38,34... | collective-permute-start | bytes 786440 | tf_op jit(solution)/shard_map/ppermute | solution.py:99
  25.0 38.1 %all-to-all-start.20 = ((f32[16,32,256]{2,1,0:T(8,128)}), f32[16,32,256]{2,1,0:T(8,128)S(1)}, u32[]{:S(2)}, u32[]{:S(2)}) async-start(f32[16,32,256]{2,1,0:T(8,128)} %tile.4), calls=%async_computation.20 | async-start | bytes 1048576 | tf_op jit(solution)/shard_map/all_to_all | solution.py:105
  33.7 28.1 %copy-start.4 = (s32[2]{0:T(128)S(1)}, s32[2]{0:T(128)}, u32[]{:S(2)}) copy-start(s32[2]{0:T(128)} %param.29) | copy-start | bytes 28
  57.8 6.4 %collective-permute-start.76 = (f32[512,256]{1,0:T(8,128)S(1)}, f32[512,256]{1,0:T(8,128)}, u32[]{:S(2)}, u32[]{:S(2)}) collective-permute-start(f32[512,256]{1,0:T(8,128)S(1)} %fusion.1.mine_ref), channel_id=1, source_target_pairs={{0,1},{1,0},{2,3},{3,2},{4,5},{5,4},{6,7},{7,6},{8,9},{9,8},{10,11... | collective-permute-start | bytes 1572872 | tf_op jit(solution)/shard_map/ppermute | solution.py:165
  67.7 13.8 %collective-permute-start.44 = (f32[512,256]{1,0:T(8,128)}, f32[512,256]{1,0:T(8,128)S(1)}, u32[]{:S(2)}, u32[]{:S(2)}) collective-permute-start(f32[512,256]{1,0:T(8,128)} %get-tuple-element.211), channel_id=1, source_target_pairs={{4,22},{5,23},{20,6},{21,7},{36,54},{37,55},{52,38},{53,39},{68,86... | collective-permute-start | bytes 1572872 | tf_op jit(solution)/shard_map/cond/branch_2_fun/ppermute | solution.py:99
  68.4 13.1 %collective-permute-start.45 = (f32[512,256]{1,0:T(8,128)}, f32[512,256]{1,0:T(8,128)S(1)}, u32[]{:S(2)}, u32[]{:S(2)}) collective-permute-start(f32[512,256]{1,0:T(8,128)} %get-tuple-element.211), channel_id=1, source_target_pairs={{4,14},{5,15},{20,30},{21,31},{36,46},{37,47},{52,62},{53,63},{68,... | collective-permute-start | bytes 1572872 | tf_op jit(solution)/shard_map/cond/branch_2_fun/ppermute | solution.py:99
  69.1 12.4 %collective-permute-start.46 = (f32[512,256]{1,0:T(8,128)}, f32[512,256]{1,0:T(8,128)S(1)}, u32[]{:S(2)}, u32[]{:S(2)}) collective-permute-start(f32[512,256]{1,0:T(8,128)} %get-tuple-element.211), channel_id=1, source_target_pairs={{4,30},{5,31},{12,6},{13,7},{20,14},{21,15},{28,22},{29,23},{36,62... | collective-permute-start | bytes 1572872 | tf_op jit(solution)/shard_map/cond/branch_2_fun/ppermute | solution.py:99
  69.8 11.7 %collective-permute-start.47 = (f32[512,256]{1,0:T(8,128)}, f32[512,256]{1,0:T(8,128)S(1)}, u32[]{:S(2)}, u32[]{:S(2)}) collective-permute-start(f32[512,256]{1,0:T(8,128)} %get-tuple-element.211), channel_id=1, source_target_pairs={{4,6},{5,7},{12,14},{13,15},{20,22},{21,23},{28,30},{29,31},{36,38... | collective-permute-start | bytes 1572872 | tf_op jit(solution)/shard_map/cond/branch_2_fun/ppermute | solution.py:99
  70.5 11.0 %all-to-all-start.12 = ((f32[16,16,256]{2,1,0:T(8,128)}), f32[16,16,256]{2,1,0:T(8,128)S(1)}, u32[]{:S(2)}, u32[]{:S(2)}) async-start(f32[16,16,256]{2,1,0:T(8,128)} %bitcast.24), calls=%async_computation.12 | async-start | bytes 524288 | tf_op jit(solution)/shard_map/cond/branch_2_fun/all_to_all | solution.py:105
  83.0 17.4 %collective-permute-start.77 = (f32[512,256]{1,0:T(8,128)S(1)}, f32[512,256]{1,0:T(8,128)}, u32[]{:S(2)}, u32[]{:S(2)}) collective-permute-start(f32[512,256]{1,0:T(8,128)S(1)} %get-tuple-element.299), channel_id=1, source_target_pairs={{6,8},{7,9},{14,16},{15,17},{22,24},{23,25},{30,0},{31,1},{38,40},... | collective-permute-start | bytes 1572872 | tf_op jit(solution)/shard_map/ppermute | solution.py:99
  85.2 40.4 %collective-permute-start.78 = (f32[512,256]{1,0:T(8,128)S(1)}, f32[512,256]{1,0:T(8,128)}, u32[]{:S(2)}, u32[]{:S(2)}) collective-permute-start(f32[512,256]{1,0:T(8,128)S(1)} %get-tuple-element.299), channel_id=1, source_target_pairs={{6,4},{7,5},{14,12},{15,13},{22,20},{23,21},{30,28},{31,29},{38,36... | collective-permute-start | bytes 1572872 | tf_op jit(solution)/shard_map/ppermute | solution.py:99
  86.6 36.8 %collective-permute-start.79 = (f32[256,256]{1,0:T(8,128)}, f32[256,256]{1,0:T(8,128)}, u32[]{:S(2)}, u32[]{:S(2)}) collective-permute-start(f32[256,256]{1,0:T(8,128)} %get-tuple-element.311), channel_id=1, source_target_pairs={{6,10},{7,11},{14,18},{15,19},{22,26},{23,27},{30,2},{31,3},{38,42... | collective-permute-start | bytes 786440 | tf_op jit(solution)/shard_map/ppermute | solution.py:99
  87.9 37.6 %collective-permute-start.80 = (f32[256,256]{1,0:T(8,128)S(1)}, f32[256,256]{1,0:T(8,128)}, u32[]{:S(2)}, u32[]{:S(2)}) collective-permute-start(f32[256,256]{1,0:T(8,128)S(1)} %get-tuple-element.312), channel_id=1, source_target_pairs={{6,2},{7,3},{14,10},{15,11},{22,18},{23,19},{30,26},{31,27},{38,34... | collective-permute-start | bytes 786440 | tf_op jit(solution)/shard_map/ppermute | solution.py:99
  90.1 40.0 %all-to-all-start.21 = ((f32[16,32,256]{2,1,0:T(8,128)}), f32[16,32,256]{2,1,0:T(8,128)S(1)}, u32[]{:S(2)}, u32[]{:S(2)}) async-start(f32[16,32,256]{2,1,0:T(8,128)} %tile.5), calls=%async_computation.21 | async-start | bytes 1048576 | tf_op jit(solution)/shard_map/all_to_all | solution.py:105
  126.7 5.0 %collective-permute-start.81 = (f32[512,256]{1,0:T(8,128)S(1)}, f32[512,256]{1,0:T(8,128)}, u32[]{:S(2)}, u32[]{:S(2)}) collective-permute-start(f32[512,256]{1,0:T(8,128)S(1)} %fusion.3.mine_ref), channel_id=1, source_target_pairs={{0,1},{1,0},{2,3},{3,2},{4,5},{5,4},{6,7},{7,6},{8,9},{9,8},{10,11... | collective-permute-start | bytes 1572872 | tf_op jit(solution)/shard_map/ppermute | solution.py:165
  (3 other events, 33.8 us)
